TPU v7x, 128 devices: a whole 4x4x4 slice. The times are simulated.
128 devices in a mesh: dp: 16 (over y, z_lo, core), tensor: 8 (over z_hi, x).
Axes of the slice: x: 4, y: 4, z: 4 (z_hi: 2, z_lo: 2; z = z_hi * 2 + z_lo), core: 2. Of those that a mesh axis runs over, the one named last changes fastest.
Arguments:
- layer_input: bfloat16 [16384, 1024], P(('dp', 'tensor')), may hold values from -6 to 6
- cotangent: bfloat16 [16384, 1024], P(('dp', 'tensor')), may hold values from -6 to 6
- segment: int32 [16384], P('dp'), may hold values from 0 to 2, as said below
- live_mask: int32 [16384], P('dp'), may hold values from 0 to 1, as said below
- query_weight: bfloat16 [2, 1024, 1024], P(None, 'dp', 'tensor'), may hold values from -0.1875 to 0.1875
- key_weight: bfloat16 [2, 1024, 1024], P(None, 'dp', 'tensor'), may hold values from -0.1875 to 0.1875
- value_weight: bfloat16 [2, 1024, 1024], P(None, 'dp', 'tensor'), may hold values from -0.1875 to 0.1875
- out_weight: bfloat16 [2, 1024, 1024], P(None, 'tensor', 'dp'), may hold values from -3 to 3
- up_weight: bfloat16 [2, 1024, 4096], P(None, 'dp', 'tensor'), may hold values from -0.1875 to 0.1875
- down_weight: bfloat16 [2, 4096, 1024], P(None, 'tensor', 'dp'), may hold values from -0.09375 to 0.09375
- query_bias: float32 [2, 1024], P(None, 'tensor'), may hold values from -3 to 3
- value_bias: float32 [2, 1024], P(None, 'tensor'), may hold values from -3 to 3
- up_bias: float32 [2, 4096], P(None, 'tensor'), may hold values from -3 to 3
- out_bias: float32 [2, 1024], replicated, may hold values from -3 to 3
- down_bias: float32 [2, 1024], replicated, may hold values from -3 to 3
- attention_gain: float32 [2, 1024], replicated, may hold values from 0.5 to 1.5
- attention_shift: float32 [2, 1024], replicated, may hold values from -3 to 3
- output_gain: float32 [2, 1024], replicated, may hold values from 0.5 to 1.5
- output_shift: float32 [2, 1024], replicated, may hold values from -3 to 3
Outputs:
- layer_output: float32 [16384, 1024], P(('dp', 'tensor'))
- input_grad: float32 [16384, 1024], P(('dp', 'tensor'))
- query_weight_grad: float32 [2, 1024, 1024], P(None, 'dp', 'tensor')
- key_weight_grad: float32 [2, 1024, 1024], P(None, 'dp', 'tensor')
- value_weight_grad: float32 [2, 1024, 1024], P(None, 'dp', 'tensor')
- out_weight_grad: float32 [2, 1024, 1024], P(None, 'tensor', 'dp')
- up_weight_grad: float32 [2, 1024, 4096], P(None, 'dp', 'tensor')
- down_weight_grad: float32 [2, 4096, 1024], P(None, 'tensor', 'dp')
- query_bias_grad: float32 [2, 1024], P(None, 'tensor')
- value_bias_grad: float32 [2, 1024], P(None, 'tensor')
- up_bias_grad: float32 [2, 4096], P(None, 'tensor')
- out_bias_grad: float32 [2, 1024], replicated
- down_bias_grad: float32 [2, 1024], replicated
- attention_gain_grad: float32 [2, 1024], replicated
- attention_shift_grad: float32 [2, 1024], replicated
- output_gain_grad: float32 [2, 1024], replicated
- output_shift_grad: float32 [2, 1024], replicated
Inputs may be any that keep to these rules, and one draw needn't show every extreme that they name: Within each aligned block of 1024 positions the segment numbers are 0, 1, 2 in that order, never falling, each present. `live_mask`: within each segment the ones form a prefix of one or more positions.
All inputs are finite; a program needn't handle non-finite values.
Results may differ from a plain program's by a relative error of at most 0.039.
Values may be sent and summed in bfloat16 or wider, within the bound.
No kernel may reach another device: no remote copies, remote signals or barrier semaphores. Data moves between devices by JAX's collectives and lax.ppermute only.
A program may use at most 128 MiB of HBM per device.

v0:
```python
import jax
import jax.numpy as jnp
from jax import lax
from jax.experimental import pallas as pl
from jax.experimental.pallas import tpu as pltpu
from jax.sharding import Mesh, PartitionSpec as P

HEAD_DIM = 64
NORM_EPS = 1e-12
MASKED = -1000000000.0
F32 = jnp.float32
BF16 = jnp.bfloat16

AXES = ("y", "zl", "c", "zh", "x")
DP = ("y", "zl", "c")
TENSOR = ("zh", "x")
OWNERS = ("y", "zl", "zh")
HOPS = (0, 1, 3, 2)
ORDER = (2, 1, 3, 0)
ARRIVAL = (0, 1, 3, 2)


def dot(left, right, left_dim, right_dim):
    return lax.dot_general(
        left, right, (((left_dim,), (right_dim,)), ((), ())), preferred_element_type=F32
    )


def along_x(value, hop):
    ring = lax.axis_size("x")
    return lax.ppermute(value, "x", [(i, (i + hop) % ring) for i in range(ring)])


def other_core(value):
    return lax.ppermute(value, "c", [(0, 1), (1, 0)])


def swap_core_z(value):
    ring = lax.axis_size("x")
    pairs = []
    for core in range(2):
        for high in range(2):
            for x in range(ring):
                pairs.append(((core * 2 + high) * ring + x, (high * 2 + core) * ring + x))
    return lax.ppermute(value, ("c", "zh", "x"), pairs)


def gather_pairs(rows):
    mine = {hop: along_x(rows, hop) if hop else rows for hop in (1, 3, 2, 0)}
    return {hop: (mine[hop], other_core(mine[hop])) for hop in ARRIVAL}


def scatter_pairs(parts):
    total = None
    for hop in ORDER:
        keep, send = parts[hop]
        both = keep + other_core(send).astype(F32)
        if hop:
            both = along_x(both.astype(BF16), -hop).astype(F32)
        total = both if total is None else total + both
    return total


def normalized(rows):
    center = rows - jnp.mean(rows, axis=-1, keepdims=True)
    spread = jnp.mean(center * center, axis=-1, keepdims=True)
    scale = lax.rsqrt(spread + NORM_EPS)
    return center * scale, scale


def norm_back(grad, unit, scale, gain):
    gain_grad = jnp.sum(grad * unit, axis=0)
    shift_grad = jnp.sum(grad, axis=0)
    scaled = grad * gain
    mean_all = jnp.mean(scaled, axis=-1, keepdims=True)
    mean_unit = jnp.mean(scaled * unit, axis=-1, keepdims=True)
    return scale * (scaled - mean_all - unit * mean_unit), gain_grad, shift_grad


def whole(array):
    rank = len(array.shape)
    return pl.BlockSpec(array.shape, lambda *_: (0,) * rank)


def call(body, args, outs, flops, grid=(), in_specs=None, out_specs=None, room=40):
    size = sum(a.size * a.dtype.itemsize for a in (*args, *outs))
    return pl.pallas_call(
        body,
        grid=grid,
        in_specs=in_specs or [whole(a) for a in args],
        out_specs=out_specs or [whole(o) for o in outs],
        out_shape=list(outs),
        compiler_params=pltpu.CompilerParams(vmem_limit_bytes=room * 1024 * 1024),
        cost_estimate=pl.CostEstimate(flops=flops, bytes_accessed=size, transcendentals=0),
    )(*args)


def shaped(shape, dtype):
    return jax.ShapeDtypeStruct(shape, dtype)


def both_rows(mine, other):
    return jnp.concatenate([mine[...], other[...]], axis=0)


def store_part(part, keep, send):
    half = keep.shape[0]
    keep[...] = part[:half]
    send[...] = part[half:].astype(BF16)


def part_shapes(rows, width):
    return [shaped((rows, width), F32), shaped((rows, width), BF16)]


def qkv_body(mine, other, mat, bias, query, key, value):
    out = (dot(both_rows(mine, other), mat[...], 1, 0) + bias[...]).astype(BF16)
    step = query.shape[1]
    query[...] = out[:, :step]
    key[...] = out[:, step : 2 * step]
    value[...] = out[:, 2 * step :]


def make_qkv(pair, mat, bias):
    rows, width = pair[0].shape
    out = shaped((2 * rows, mat.shape[1] // 3), BF16)
    return call(qkv_body, (*pair, mat, bias), [out] * 3, 4 * rows * mat.size)


def lanes_of(shape, head):
    return lax.broadcasted_iota(jnp.int32, shape, 1) // HEAD_DIM == head


def attend_body(query, key, value, row_mark, key_mark, out_mat, mixed, soft, keep, send):
    allowed = row_mark[...] == key_mark[...]
    total = jnp.zeros(query.shape, F32)
    for head in range(soft.shape[0]):
        lanes = lanes_of(query.shape, head)
        chosen = jnp.where(lanes, query[...], jnp.zeros(query.shape, BF16))
        scores = dot(chosen, key[...], 1, 1) * HEAD_DIM**-0.5
        scores = jnp.where(allowed, scores, MASKED)
        exps = jnp.exp(scores - jnp.max(scores, axis=-1, keepdims=True))
        probs = (exps * (1.0 / jnp.sum(exps, axis=-1, keepdims=True))).astype(BF16)
        soft[head] = probs
        total = jnp.where(lanes, dot(probs, value[...], 1, 0), total)
    low = total.astype(BF16)
    mixed[...] = low
    store_part(dot(low, out_mat[...], 1, 1), keep, send)


def attend(query, key, value, row_mark, key_mark, out_mat):
    rows, width = query.shape
    heads = width // HEAD_DIM
    outs = [shaped((rows, width), BF16), shaped((heads, rows, key.shape[0]), BF16)]
    outs += part_shapes(rows // 2, out_mat.shape[0])
    flops = 4 * heads * rows * key.size + 2 * rows * out_mat.size
    return call(attend_body, (query, key, value, row_mark, key_mark, out_mat), outs, 3 * flops)


def attend_back_body(mine, other, out_mat, query, key, value, soft, key_in, value_in, grad_query, key_out, value_out):
    grads = dot(both_rows(mine, other), out_mat[...], 1, 0).astype(BF16)
    for_query = jnp.zeros(query.shape, F32)
    for_key = jnp.zeros(key.shape, F32)
    for_value = jnp.zeros(key.shape, F32)
    for head in range(soft.shape[0]):
        lanes = lanes_of(query.shape, head)
        tall = lanes_of(key.shape, head)
        probs = soft[head]
        wide = probs.astype(F32)
        chosen = jnp.where(lanes, grads, jnp.zeros(query.shape, BF16))
        grad_soft = dot(chosen, value[...], 1, 1)
        row = jnp.sum(grad_soft * wide, axis=-1, keepdims=True)
        scores = (wide * (grad_soft - row)).astype(BF16)
        for_query = jnp.where(lanes, dot(scores, key[...], 1, 0), for_query)
        for_key = jnp.where(tall, dot(scores, query[...], 0, 0), for_key)
        for_value = jnp.where(tall, dot(probs, grads, 0, 0), for_value)
    grad_query[...] = (for_query * HEAD_DIM**-0.5).astype(BF16)
    key_out[...] = key_in[...] + for_key * HEAD_DIM**-0.5
    value_out[...] = value_in[...] + for_value


def attend_back(pair, out_mat, query, key, value, soft, key_sum, value_sum):
    outs = [shaped(query.shape, BF16), shaped(key.shape, F32), shaped(key.shape, F32)]
    args = (*pair, out_mat, query, key, value, soft, key_sum, value_sum)
    flops = 8 * soft.shape[0] * query.shape[0] * key.size
    return call(attend_back_body, args, outs, 2 * flops)


def inputs_back_body(grad_query, grad_key, grad_value, mat, joined, sums, keep, send):
    rows = jnp.concatenate(
        [grad_query[...], grad_key[...].astype(BF16), grad_value[...].astype(BF16)], axis=1
    )
    joined[...] = rows
    sums[...] = jnp.sum(rows.astype(F32), axis=0, keepdims=True)
    store_part(dot(rows, mat[...], 1, 1), keep, send)


def inputs_back(grad_query, grad_key, grad_value, index, mat):
    rows, width = grad_query.shape
    outs = [shaped((rows, 3 * width), BF16), shaped((1, 3 * width), F32)]
    outs += part_shapes(rows // 2, mat.shape[0])
    block = pl.BlockSpec((rows, width), lambda *_: (index, 0))
    args = (grad_query, grad_key, grad_value, mat)
    specs = [whole(grad_query), block, block, whole(mat)]
    return call(inputs_back_body, args, outs, 2 * rows * mat.size, (1,), specs)


def ffn_body(mine, other, up, bias, down, act, slope, keep, send):
    pre = dot(both_rows(mine, other), up[...], 1, 0) + bias[...]
    area = 0.5 + 0.5 * lax.erf(pre * 0.7071067811865476)
    low = (pre * area).astype(BF16)
    act[...] = low
    slope[...] = (area + pre * (jnp.exp(pre * pre * -0.5) * 0.3989422804014327)).astype(BF16)
    store_part(dot(low, down[...], 1, 1), keep, send)


def ffn(pair, up, bias, down):
    rows, width = pair[0].shape
    outs = [shaped((2 * rows, up.shape[1]), BF16)] * 2 + part_shapes(rows, width)
    return call(ffn_body, (*pair, up, bias, down), outs, 4 * rows * (up.size + down.size))


def ffn_back_body(mine, other, up, down, slope, grad, sums, keep, send):
    low = (dot(both_rows(mine, other), down[...], 1, 0) * slope[...].astype(F32)).astype(BF16)
    grad[...] = low
    sums[...] = jnp.sum(low.astype(F32), axis=0, keepdims=True)
    store_part(dot(low, up[...], 1, 1), keep, send)


def ffn_back(pair, up, down, slope):
    rows, width = pair[0].shape
    outs = [shaped(slope.shape, BF16), shaped((1, slope.shape[1]), F32)] + part_shapes(rows, width)
    return call(ffn_back_body, (*pair, up, down, slope), outs, 4 * rows * (up.size + down.size))


def weight_grads(pairs, owners, extra=None):
    count = len(HOPS)
    tile = 256
    args, specs, cols = [], [], 0
    for left, right in pairs:
        flat = [half for hop in HOPS for half in left[hop]]
        rows, width = flat[0].shape
        args += flat + [right[hop] for hop in HOPS]
        specs += [pl.BlockSpec((rows, tile), lambda i: (0, i))] * len(flat)
        specs += [whole(right[hop]) for hop in HOPS]
        cols += right[0].shape[1]
    slab = width // owners
    depth = slab
    if extra is not None:
        args.append(extra)
        specs.append(whole(extra))
        depth += extra.shape[0]

    def body(*refs):
        out = refs[-1]
        start = 0
        for index in range(len(pairs)):
            here = refs[index * 3 * count : (index + 1) * 3 * count]
            left = jnp.concatenate([ref[...] for ref in here[: 2 * count]], axis=0)
            right = jnp.concatenate([ref[...] for ref in here[2 * count :]], axis=0)
            end = start + right.shape[1]
            found = dot(left, right, 0, 0).astype(BF16)
            for part in range(tile // slab):
                out[part, :slab, start:end] = found[part * slab : (part + 1) * slab]
            start = end
        if extra is not None:
            for part in range(tile // slab):
                out[part, slab:, :] = refs[-2][...]

    out = shaped((owners, depth, cols), BF16)
    out_spec = pl.BlockSpec((tile // slab, depth, cols), lambda i: (i, 0, 0))
    flops = 2 * rows * 2 * count * width * cols
    return call(body, args, [out], 2 * flops, (width // tile,), specs, [out_spec], 58)[0]


def stack_chunks(chunks):
    return jnp.concatenate([chunks[hop] for hop in HOPS], axis=0)


def sum_group(vectors, core, x):
    ring = lax.axis_size("x")
    slices = vectors.reshape(vectors.shape[0], 2, ring, -1)
    slices = jnp.transpose(slices, (1, 2, 0, 3))
    mine = lax.dynamic_index_in_dim(slices, core, 0, False)
    send = lax.dynamic_index_in_dim(slices, 1 - core, 0, False)
    both = mine + other_core(send)
    kept = None
    for hop in HOPS:
        part = lax.dynamic_index_in_dim(both, lax.rem(x + ring - hop, ring), 0, False)
        part = along_x(part, -hop) if hop else part
        kept = part if kept is None else kept + part
    return kept


def on_device(
    layer_input,
    cotangent,
    segment,
    live_mask,
    query_weight,
    key_weight,
    value_weight,
    out_weight,
    up_weight,
    down_weight,
    query_bias,
    value_bias,
    up_bias,
    out_bias,
    down_bias,
    attention_gain,
    attention_shift,
    output_gain,
    output_shift,
):
    layers = query_weight.shape[0]
    core, high, x = lax.axis_index("c"), lax.axis_index("zh"), lax.axis_index("x")
    ring = lax.axis_size("x")
    owners = 16
    rows_in = swap_core_z(layer_input)

    head_cols = query_weight.shape[2]
    qkv_cols = 3 * head_cols
    shard_rows = query_weight.shape[1]
    ffn_half = up_weight.shape[2]
    qkv_shards = jnp.concatenate([query_weight, key_weight, value_weight], axis=2)

    turned_out = jnp.swapaxes(out_weight, 1, 2)
    first = swap_core_z(jnp.concatenate([qkv_shards[0], turned_out[0]], axis=1))
    spread = jnp.broadcast_to(first, (owners,) + first.shape)
    first = lax.all_to_all(spread, OWNERS, 0, 0, tiled=True).reshape(-1, first.shape[1])

    def gather_mat(*shards):
        mat = lax.all_gather(jnp.concatenate(shards, axis=1), DP, axis=0, tiled=True)
        return swap_core_z(mat)

    attn_mats, ffn_mats = [], []
    for layer in range(layers):
        if layer:
            attn_mats.append(gather_mat(qkv_shards[layer], turned_out[layer]))
        else:
            attn_mats.append(first)
        ffn_mats.append(gather_mat(up_weight[layer], jnp.swapaxes(down_weight[layer], 0, 1)))
    qkv_mats = [mat[:, :qkv_cols] for mat in attn_mats]
    out_mats = [mat[:, qkv_cols:] for mat in attn_mats]
    up_mats = [mat[:, :ffn_half] for mat in ffn_mats]
    down_mats = [mat[:, ffn_half:] for mat in ffn_mats]

    biases = jnp.concatenate([query_bias, value_bias, up_bias], axis=1)
    biases = swap_core_z(biases)
    query_bias = biases[:, :head_cols]
    value_bias = biases[:, head_cols : 2 * head_cols]
    up_bias = biases[:, 2 * head_cols :]

    packed = (segment * 2 + live_mask).astype(F32)
    packed = jnp.where(core == high, packed, other_core(packed)).reshape(2, ring, -1)
    packed = jnp.where(core == 0, packed, packed[::-1])
    ordered = []
    for hop in HOPS:
        ordered.append(lax.dynamic_index_in_dim(packed, lax.rem(x + ring - hop, ring), 1, False))
    marks = jnp.stack(ordered).reshape(len(HOPS), -1)
    seg_chunks = jnp.floor(marks * 0.5)
    live = (marks - 2 * seg_chunks).reshape(-1)
    key_mark = jnp.where(live > 0.5, seg_chunks.reshape(-1), -1.0)
    row_marks = {hop: seg_chunks[index][:, None] for index, hop in enumerate(HOPS)}
    key_mark = key_mark[None, :]

    current = rows_in.astype(F32)
    saved = []
    for layer in range(layers):
        qkv_mat, out_mat = qkv_mats[layer], out_mats[layer]
        up_mat, down_mat = up_mats[layer], down_mats[layer]
        qkv_bias = jnp.concatenate(
            [query_bias[layer], jnp.zeros_like(query_bias[layer]), value_bias[layer]]
        )
        inputs = gather_pairs(current.astype(BF16))
        qkv = {hop: make_qkv(inputs[hop], qkv_mat, qkv_bias[None, :]) for hop in ARRIVAL}
        keys = stack_chunks({hop: qkv[hop][1] for hop in HOPS})
        values = stack_chunks({hop: qkv[hop][2] for hop in HOPS})
        attended, soft, parts = {}, {}, {}
        for hop in ORDER:
            attended[hop], soft[hop], *parts[hop] = attend(
                qkv[hop][0], keys, values, row_marks[hop], key_mark, out_mat
            )
        first_sum = current + scatter_pairs(parts) + out_bias[layer]
        mid_unit, mid_scale = normalized(first_sum)
        normed_mid = mid_unit * attention_gain[layer] + attention_shift[layer]
        mids = gather_pairs(normed_mid.astype(BF16))
        activated, slopes, parts = {}, {}, {}
        for hop in ARRIVAL:
            activated[hop], slopes[hop], *parts[hop] = ffn(
                mids[hop], up_mat, up_bias[layer][None, :], down_mat
            )
        second_sum = normed_mid + scatter_pairs(parts) + down_bias[layer]
        out_unit, out_scale = normalized(second_sum)
        current = out_unit * output_gain[layer] + output_shift[layer]
        saved.append(
            (inputs, qkv, keys, values, attended, soft, mid_unit, mid_scale, mids, slopes,
             activated, out_unit, out_scale)
        )
    layer_output = swap_core_z(current.astype(BF16)).astype(F32)

    grad_rows = swap_core_z(cotangent).astype(F32)
    def sum_owners(terms):
        return jnp.sum(lax.all_to_all(terms, OWNERS, 0, 0, tiled=True).astype(F32), axis=0)

    def extra_rows(values, cols):
        count = -(-values.shape[0] // (16 * cols)) * 16
        padded = jnp.pad(values, (0, count * cols - values.shape[0]))
        return padded.reshape(count, cols).astype(BF16)

    late_grads, qkv_grads = [None] * layers, [None] * layers
    row_sums, head_sums, waiting = [], [], []
    for layer in reversed(range(layers)):
        (inputs, qkv, keys, values, attended, soft, mid_unit, mid_scale, mids, slopes,
         activated, out_unit, out_scale) = saved[layer]
        qkv_mat, out_mat = qkv_mats[layer], out_mats[layer]
        up_mat, down_mat = up_mats[layer], down_mats[layer]
        grad_second, out_gain_term, out_shift_term = norm_back(
            grad_rows, out_unit, out_scale, output_gain[layer]
        )
        branch_low = grad_second.astype(BF16)
        down_bias_term = jnp.sum(branch_low.astype(F32), axis=0)
        branch = gather_pairs(branch_low)
        grad_pre, parts, up_sums = {}, {}, []
        for hop in ARRIVAL:
            grad_pre[hop], up_sum, *parts[hop] = ffn_back(
                branch[hop], up_mat, down_mat, slopes[hop]
            )
            up_sums.append(up_sum[0])
        grad_mid = grad_second + scatter_pairs(parts)
        up_bias_term = sum(up_sums)
        grad_first, att_gain_term, att_shift_term = norm_back(
            grad_mid, mid_unit, mid_scale, attention_gain[layer]
        )
        attn_low = grad_first.astype(BF16)
        out_bias_term = jnp.sum(attn_low.astype(F32), axis=0)
        attn_chunks = gather_pairs(attn_low)
        row_sums.append(
            jnp.stack([out_bias_term, down_bias_term, att_gain_term, att_shift_term, out_gain_term,
                       out_shift_term])
        )
        head_sums.append(up_bias_term)
        late = [(mids, grad_pre), (branch, activated), (attn_chunks, attended)]
        if layer:
            terms = weight_grads(late, owners)
            found = lax.psum_scatter(terms, OWNERS, scatter_dimension=0, tiled=False)
            late_grads[layer] = swap_core_z(found)
        else:
            kept = sum_group(jnp.concatenate(row_sums), core, x)
            small = jnp.concatenate(head_sums + [kept.reshape(-1)])
            cols = sum(right[0].shape[1] for _, right in late + waiting)
            terms = weight_grads(late + waiting, owners, extra_rows(small, cols))
            joint = sum_owners(terms)
            early_sums = joint[shard_rows:].reshape(-1)[: small.shape[0]]
            joint = swap_core_z(joint[:shard_rows].astype(BF16))
            late_cols = cols - (layers - 1) * qkv_cols
            late_grads[0] = joint[:, :late_cols]
            for index in range(1, layers):
                start = late_cols + (layers - 1 - index) * qkv_cols
                qkv_grads[index] = joint[:, start : start + qkv_cols]
        grad_q = {}
        grad_k, grad_v = jnp.zeros(keys.shape, F32), jnp.zeros(keys.shape, F32)
        for hop in ARRIVAL:
            grad_q[hop], grad_k, grad_v = attend_back(
                attn_chunks[hop], out_mat, qkv[hop][0], keys, values, soft[hop], grad_k, grad_v
            )
        parts, grad_qkv, sums = {}, {}, []
        for hop in ORDER:
            grad_qkv[hop], qkv_sum, *parts[hop] = inputs_back(
                grad_q[hop], grad_k, grad_v, HOPS.index(hop), qkv_mat
            )
            sums.append(qkv_sum[0])
        grad_rows = grad_first + scatter_pairs(parts)
        bias_terms = sum(sums)
        pair_sums = jnp.concatenate([bias_terms[:head_cols], bias_terms[2 * head_cols :]])
        if layer:
            waiting.append((inputs, grad_qkv))
            head_sums.append(pair_sums)
        else:
            terms = weight_grads([(inputs, grad_qkv)], owners, extra_rows(pair_sums, qkv_cols))
            got = sum_owners(terms)
            qkv_grads[0] = swap_core_z(got[:shard_rows].astype(BF16))
            last_sums = got[shard_rows:].reshape(-1)[: 2 * head_cols]

    head_len = sum(item.shape[0] for item in head_sums)
    ups, pairs, place = [None] * layers, [last_sums] + [None] * (layers - 1), 0
    for layer in reversed(range(layers)):
        ups[layer] = early_sums[place : place + ffn_half]
        place += ffn_half
        if layer:
            pairs[layer] = early_sums[place : place + 2 * head_cols]
            place += 2 * head_cols
    up_all = swap_core_z(jnp.stack(ups))
    pair_all = swap_core_z(jnp.stack(pairs))
    input_grad = swap_core_z(grad_rows.astype(BF16)).astype(F32)

    piece = early_sums[head_len:].reshape(layers * 6, -1)
    table = jnp.zeros((2, ring) + piece.shape, F32)
    for hop in HOPS:
        one = along_x(piece, hop) if hop else piece
        where = lax.rem(x + ring - hop, ring)
        table = lax.dynamic_update_slice(table, one[None, None], (core, where, 0, 0))
    pair = lax.dynamic_slice_in_dim(table, core, 1, 0)
    table = lax.dynamic_update_slice(table, other_core(pair), (1 - core, 0, 0, 0))
    rows_out = jnp.transpose(table, (2, 0, 1, 3)).reshape(layers, 6, -1)[::-1]

    def cols(pieces, start, count, turn=False):
        chosen = [piece[:, start : start + count].astype(F32) for piece in pieces]
        return jnp.stack([jnp.swapaxes(one, 0, 1) if turn else one for one in chosen])

    return (
        layer_output,
        input_grad,
        cols(qkv_grads, 0, head_cols),
        cols(qkv_grads, head_cols, head_cols),
        cols(qkv_grads, 2 * head_cols, head_cols),
        cols(late_grads, 2 * ffn_half, head_cols, True),
        cols(late_grads, 0, ffn_half),
        cols(late_grads, ffn_half, ffn_half, True),
        pair_all[:, :head_cols],
        pair_all[:, head_cols:],
        up_all,
        rows_out[:, 0],
        rows_out[:, 1],
        rows_out[:, 2],
        rows_out[:, 3],
        rows_out[:, 4],
        rows_out[:, 5],
    )


def solution(mesh):
    split = Mesh(mesh.devices.reshape(4, 2, 2, 2, 4), AXES)
    rows = P(DP + TENSOR, None)
    tall = P(None, DP, TENSOR)
    wide = P(None, TENSOR, DP)
    held = P(None, TENSOR)
    return jax.shard_map(
        on_device,
        mesh=split,
        in_specs=(rows, rows, P(DP), P(DP), tall, tall, tall, wide, tall, wide, held, held, held)
        + (P(),) * 6,
        out_specs=(rows, rows, tall, tall, tall, wide, tall, wide, held, held, held) + (P(),) * 6,
        check_vma=False,
    )
```

profile of v0, /device:TPU:25, one launch (start us, length us, event | category | flops | bytes accessed | tf_op | source)
XLA Modules:
  0.0 546.5 jit_solution(15298784474366025133)
XLA Ops:
  15.6 5.4 collective-permute-start.4
  23.0 5.1 collective-permute-start
  30.5 4.6 all-to-all-start
  45.8 4.4 collective-permute-start.9
  73.2 3.0 collective-permute-start.12
  76.2 4.5 collective-permute-start.20
  88.8 2.8 collective-permute-done.16
  96.7 6.5 %collective-permute-done.18.mine.refs_6_ = bf16[128,1024]{1,0:T(8,128)(2,1)S(1)} collective-permute-done((bf16[128,1024]{1,0:T(8,128)(2,1)S(1)}, bf16[128,1024]{1,0:T(8,128)(2,1)S(1)}, u32[]{:S(2)}, u32[]{:S(2)}) %collective-permute-start.18) | collective-permute-done | bytes 262176 | tf_op jit(solution)/shard_map/ppermute | solution.py:31
  103.6 4.7 collective-permute-done.23.mine.refs_2_
  122.3 5.5 %collective-permute-start.35 = (bf16[1024,512]{1,0:T(8,128)(2,1)}, bf16[1024,512]{1,0:T(8,128)(2,1)S(1)}, u32[]{:S(2)}, u32[]{:S(2)}) collective-permute-start(bf16[1024,512]{1,0:T(8,128)(2,1)} %all-gather.6.cloned.1.call-done), channel_id=1, source_target_pairs={{0,0},{1,1},{2,2},{3,3},{4,8},{5,9},{6,10},{7,11},{8,4},{9,5},{10,... | collective-permute-start | bytes 3145736 | tf_op jit(solution)/shard_map/ppermute | solution.py:45
  127.8 2.8 collective-permute-done.26
  138.7 5.3 collective-permute-done.37.mine.refs_38_
  144.0 6.6 %collective-permute-start.38 = (bf16[128,1024]{1,0:T(8,128)(2,1)}, bf16[128,1024]{1,0:T(8,128)(2,1)}, u32[]{:S(2)}, u32[]{:S(2)}) collective-permute-start(bf16[128,1024]{1,0:T(8,128)(2,1)} %collective-permute-done.37.mine.refs_38_), channel_id=1, source_target_pairs={{0,8},{8,0},{1,9},{9,1},{2,10},{10,2},{3,11},{11,3},{4,12},{12,4},... | collective-permute-start | bytes 786440 | tf_op jit(solution)/shard_map/ppermute | solution.py:35
  152.3 3.5 collective-permute-start.50
  174.0 7.4 %collective-permute-done.42 = bf16[128,1024]{1,0:T(8,128)(2,1)S(1)} collective-permute-done((bf16[128,1024]{1,0:T(8,128)(2,1)S(1)}, bf16[128,1024]{1,0:T(8,128)(2,1)S(1)}, u32[]{:S(2)}, u32[]{:S(2)}) %collective-permute-start.42) | collective-permute-done | bytes 262176 | tf_op jit(solution)/shard_map/ppermute | solution.py:31
  184.0 3.5 collective-permute-done.46
  192.4 4.9 collective-permute-done.48.mine.refs_6_
  199.6 3.7 collective-permute-done.53.mine.refs_2_
  212.5 4.5 collective-permute-start.64
  219.5 3.8 collective-permute-done.56
  230.0 6.0 %collective-permute-done.65.mine.refs_18_ = bf16[128,1024]{1,0:T(8,128)(2,1)S(1)} collective-permute-done((bf16[128,1024]{1,0:T(8,128)(2,1)S(1)}, bf16[128,1024]{1,0:T(8,128)(2,1)S(1)}, u32[]{:S(2)}, u32[]{:S(2)}) %collective-permute-start.65) | collective-permute-done | bytes 262176 | tf_op jit(solution)/shard_map/ppermute | solution.py:31
  238.3 4.0 collective-permute-done.69.mine.refs_14_
  250.2 7.0 %collective-permute-done.68 = bf16[128,1024]{1,0:T(8,128)(2,1)S(1)} collective-permute-done((bf16[128,1024]{1,0:T(8,128)(2,1)S(1)}, bf16[128,1024]{1,0:T(8,128)(2,1)S(1)}, u32[]{:S(2)}, u32[]{:S(2)}) %collective-permute-start.68) | collective-permute-done | bytes 262176 | tf_op jit(solution)/shard_map/ppermute | solution.py:31
  257.2 3.8 collective-permute-done.72
  269.7 5.8 %collective-permute-done.83.mine.refs_26_ = bf16[128,1024]{1,0:T(8,128)(2,1)S(1)} collective-permute-done((bf16[128,1024]{1,0:T(8,128)(2,1)S(1)}, bf16[128,1024]{1,0:T(8,128)(2,1)S(1)}, u32[]{:S(2)}, u32[]{:S(2)}) %collective-permute-start.83) | collective-permute-done | bytes 262176 | tf_op jit(solution)/shard_map/ppermute | solution.py:31
  275.5 6.0 %collective-permute-start.84 = (bf16[128,1024]{1,0:T(8,128)(2,1)S(1)}, bf16[128,1024]{1,0:T(8,128)(2,1)S(1)}, u32[]{:S(2)}, u32[]{:S(2)}) collective-permute-start(bf16[128,1024]{1,0:T(8,128)(2,1)S(1)} %collective-permute-done.83.mine.refs_26_), channel_id=1, source_target_pairs={{0,8},{8,0},{1,9},{9,1},{2,10},{10,2},{3,11},{11,3},{4,12},{12,4},... | collective-permute-start | bytes 786440 | tf_op jit(solution)/shard_map/ppermute | solution.py:35
  300.5 5.2 collective-permute-done.87
  305.7 5.3 collective-permute-done.89
  315.4 2.7 collective-permute-start.97
  318.3 5.5 %collective-permute-done.93.mine.refs_18_ = bf16[128,1024]{1,0:T(8,128)(2,1)} collective-permute-done((bf16[128,1024]{1,0:T(8,128)(2,1)S(1)}, bf16[128,1024]{1,0:T(8,128)(2,1)}, u32[]{:S(2)}, u32[]{:S(2)}) %collective-permute-start.93) | collective-permute-done | bytes 262176 | tf_op jit(solution)/shard_map/ppermute | solution.py:31
  326.2 3.9 collective-permute-done.97.mine.refs_14_
  341.8 7.6 %shard_map.364 = bf16[16,64,1152]{2,1,0:T(8,128)(2,1)} custom-call(bf16[128,1024]{1,0:T(8,128)(2,1)} %copy-done.3, bf16[128,1024]{1,0:T(8,128)(2,1)} %copy-done.23, bf16[128,1024]{1,0:T(8,128)(2,1)} %copy-done.21, bf16[128,1024]{1,0:T(8,128)(2,1)} %copy-done.25, bf16[128,1024]{1,0:T(8,128)(2,1)} %copy-done.22, bf16[128,1024]{1,0:T(8,128)(2,1)} %copy-done.26, ...), custom_call_target="tpu_custom_call" | custom-call | flops 4831838208 | bytes 11010048 | tf_op jit(solution)/shard_map/pallas_call | solution.py:87
  349.4 4.2 collective-permute-done.100
  362.0 10.9 %collective-permute-done.111.mine.refs_26_ = bf16[128,1024]{1,0:T(8,128)(2,1)S(1)} collective-permute-done((bf16[128,1024]{1,0:T(8,128)(2,1)S(1)}, bf16[128,1024]{1,0:T(8,128)(2,1)S(1)}, u32[]{:S(2)}, u32[]{:S(2)}) %collective-permute-start.111) | collective-permute-done | bytes 262176 | tf_op jit(solution)/shard_map/ppermute | solution.py:31
  392.8 4.9 shard_map.362
  397.7 9.0 %all-to-all-start.1 = ((bf16[16,80,384]{2,1,0:T(8,128)(2,1)}), bf16[16,80,384]{2,1,0:T(8,128)(2,1)}, u32[]{:S(2)}, u32[]{:S(2)}) async-start(bf16[16,80,384]{2,1,0:T(8,128)(2,1)} %shard_map.362), calls=%async_computation.1 | async-start | bytes 1966080 | tf_op jit(solution)/shard_map/all_to_all | solution.py:405
  408.0 9.3 %shard_map.363 = bf16[16,80,1536]{2,1,0:T(8,128)(2,1)} custom-call(bf16[128,1024]{1,0:T(8,128)(2,1)} %copy-done.2, bf16[128,1024]{1,0:T(8,128)(2,1)} %copy-done.16, bf16[128,1024]{1,0:T(8,128)(2,1)} %copy-done.14, bf16[128,1024]{1,0:T(8,128)(2,1)} %copy-done.18, bf16[128,1024]{1,0:T(8,128)(2,1)} %copy-done.15, bf16[128,1024]{1,0:T(8,128)(2,1)} %copy-done.19, ...), custom_call_target="tpu_custom_call" | custom-call | flops 6442450944 | bytes 15515648 | tf_op jit(solution)/shard_map/pallas_call | solution.py:87
  417.3 5.6 %all-to-all-done.1 = bf16[16,80,384]{2,1,0:T(8,128)(2,1)} async-done(((bf16[16,80,384]{2,1,0:T(8,128)(2,1)}), bf16[16,80,384]{2,1,0:T(8,128)(2,1)}, u32[]{:S(2)}, u32[]{:S(2)}) %all-to-all-start.1) | async-done | bytes 983072 | tf_op jit(solution)/shard_map/all_to_all | solution.py:405
  422.9 10.2 %all-to-all-start.2 = ((bf16[16,80,1536]{2,1,0:T(8,128)(2,1)}), bf16[16,80,1536]{2,1,0:T(8,128)(2,1)}, u32[]{:S(2)}, u32[]{:S(2)}) async-start(bf16[16,80,1536]{2,1,0:T(8,128)(2,1)} %shard_map.363), calls=%async_computation.2 | async-start | bytes 7864320 | tf_op jit(solution)/shard_map/all_to_all | solution.py:405
  436.0 2.9 collective-permute-start.115
  440.6 5.7 %collective-permute-start.63 = (bf16[128,1024]{1,0:T(8,128)(2,1)S(1)}, bf16[128,1024]{1,0:T(8,128)(2,1)S(1)}, u32[]{:S(2)}, u32[]{:S(2)}) collective-permute-start(bf16[128,1024]{1,0:T(8,128)(2,1)S(1)} %copy-done.148), channel_id=1, source_target_pairs={{0,0},{1,1},{2,2},{3,3},{4,8},{5,9},{6,10},{7,11},{8,4},{9,5},{10,... | collective-permute-start | bytes 786440 | tf_op jit(solution)/shard_map/ppermute | solution.py:45
  446.3 3.9 collective-permute-done.117
  451.6 5.1 collective-permute-start.121
  460.0 38.9 %collective-permute-done.63 = bf16[128,1024]{1,0:T(8,128)(2,1)S(1)} collective-permute-done((bf16[128,1024]{1,0:T(8,128)(2,1)S(1)}, bf16[128,1024]{1,0:T(8,128)(2,1)S(1)}, u32[]{:S(2)}, u32[]{:S(2)}) %collective-permute-start.63) | collective-permute-done | bytes 262176 | tf_op jit(solution)/shard_map/ppermute | solution.py:45
  502.6 4.7 collective-permute-start.128
  507.3 3.5 collective-permute-done.128
  518.0 4.4 collective-permute-start.130
  525.2 4.4 collective-permute-start.127
  (851 shorter events, 246.2 us)
Async XLA Ops:
  7.2 69.0 %all-gather.4.cloned.1.call-start = ((), (), s32[]{:S(2)}) async-start(), calls=%async_computation.4 | async-start | bytes 2228224 | tf_op jit(solution)/shard_map/all_gather | solution.py:334
  9.7 112.6 %all-gather.6.cloned.1.call-start = ((), (), s32[]{:S(2)}) async-start(), calls=%async_computation.5 | async-start | bytes 1114112 | tf_op jit(solution)/shard_map/all_gather | solution.py:334
  13.5 138.8 %all-gather.8.cloned.1.call-start = ((), (), s32[]{:S(2)}) async-start(), calls=%async_computation.6 | async-start | bytes 2228224 | tf_op jit(solution)/shard_map/all_gather | solution.py:334
  14.2 15.2 %collective-permute-start.10 = (f32[1024]{0:T(1024)S(1)}, f32[1024]{0:T(1024)S(1)}, u32[]{:S(2)}, u32[]{:S(2)}) collective-permute-start(f32[1024]{0:T(1024)S(1)} %add_convert_fusion.26), channel_id=1, source_target_pairs={{0,8},{8,0},{1,9},{9,1},{2,10},{10,2},{3,11},{11,3},{4,12},{12,4},... | collective-permute-start | bytes 12296 | tf_op jit(solution)/shard_map/ppermute | solution.py:35
  15.6 29.6 %collective-permute-start.4 = (f32[2,768]{1,0:T(2,128)S(1)}, f32[2,768]{1,0:T(2,128)S(1)}, u32[]{:S(2)}, u32[]{:S(2)}) collective-permute-start(f32[2,768]{1,0:T(2,128)S(1)} %pad_maximum_fusion.4), channel_id=1, source_target_pairs={{0,0},{1,1},{2,2},{3,3},{4,8},{5,9},{6,10},{7,11},{8,4},{9,5},{10,... | collective-permute-start | bytes 18440 | tf_op jit(solution)/shard_map/ppermute | solution.py:45
  30.5 21.6 %all-to-all-start = ((bf16[16,64,512]{2,1,0:T(8,128)(2,1)}), bf16[16,64,512]{2,1,0:T(8,128)(2,1)}, u32[]{:S(2)}, u32[]{:S(2)}) async-start(bf16[16,64,512]{2,1,0:T(8,128)(2,1)} %broadcast_in_dim.18), calls=%async_computation | async-start | bytes 2097152 | tf_op jit(solution)/shard_map/all_to_all | solution.py:331
  35.1 467.5 %reduce-scatter.2.cloned.1.call-start = ((), (), s32[]{:S(2)}) async-start(), calls=%async_computation.7 | async-start | bytes 2506752 | tf_op jit(solution)/shard_map/reduce_scatter | solution.py:447
  39.3 15.0 %collective-permute-start.5 = (bf16[128,1024]{1,0:T(8,128)(2,1)S(1)}, bf16[128,1024]{1,0:T(8,128)(2,1)S(1)}, u32[]{:S(2)}, u32[]{:S(2)}) collective-permute-start(bf16[128,1024]{1,0:T(8,128)(2,1)S(1)} %collective-permute-done.mine.refs_0_), channel_id=1, source_target_pairs={{0,8},{8,0},{1,9},{9,1},{2,10},{10,2},{3,11},{11,3},{4,12},{12,4},... | collective-permute-start | bytes 786440 | tf_op jit(solution)/shard_map/ppermute | solution.py:35
  64.5 16.2 %collective-permute-start.13 = (bf16[128,1024]{1,0:T(8,128)(2,1)}, bf16[128,1024]{1,0:T(8,128)(2,1)}, u32[]{:S(2)}, u32[]{:S(2)}) collective-permute-start(bf16[128,1024]{1,0:T(8,128)(2,1)} %get-tuple-element.206), channel_id=1, source_target_pairs={{0,8},{8,0},{1,9},{9,1},{2,10},{10,2},{3,11},{11,3},{4,12},{12,4},... | collective-permute-start | bytes 786440 | tf_op jit(solution)/shard_map/ppermute | solution.py:35
  68.5 14.0 %collective-permute-start.15 = (bf16[128,1024]{1,0:T(8,128)(2,1)}, bf16[128,1024]{1,0:T(8,128)(2,1)}, u32[]{:S(2)}, u32[]{:S(2)}) collective-permute-start(bf16[128,1024]{1,0:T(8,128)(2,1)} %get-tuple-element.209), channel_id=1, source_target_pairs={{0,8},{8,0},{1,9},{9,1},{2,10},{10,2},{3,11},{11,3},{4,12},{12,4},... | collective-permute-start | bytes 786440 | tf_op jit(solution)/shard_map/ppermute | solution.py:35
  72.2 14.9 %collective-permute-start.17 = (bf16[128,1024]{1,0:T(8,128)(2,1)}, bf16[128,1024]{1,0:T(8,128)(2,1)}, u32[]{:S(2)}, u32[]{:S(2)}) collective-permute-start(bf16[128,1024]{1,0:T(8,128)(2,1)} %get-tuple-element.212), channel_id=1, source_target_pairs={{0,8},{8,0},{1,9},{9,1},{2,10},{10,2},{3,11},{11,3},{4,12},{12,4},... | collective-permute-start | bytes 786440 | tf_op jit(solution)/shard_map/ppermute | solution.py:35
  73.2 13.9 %collective-permute-start.12 = (bf16[128,1024]{1,0:T(8,128)(2,1)S(1)}, bf16[128,1024]{1,0:T(8,128)(2,1)}, u32[]{:S(2)}, u32[]{:S(2)}) collective-permute-start(bf16[128,1024]{1,0:T(8,128)(2,1)S(1)} %add_convert_fusion.25), channel_id=1, source_target_pairs={{0,2},{1,3},{2,0},{3,1},{4,6},{5,7},{6,4},{7,5},{8,10},{9,11},{10,... | collective-permute-start | bytes 786440 | tf_op jit(solution)/shard_map/ppermute | solution.py:31
  76.2 32.6 %collective-permute-start.20 = (bf16[1024,1024]{1,0:T(8,128)(2,1)}, bf16[1024,1024]{1,0:T(8,128)(2,1)S(1)}, u32[]{:S(2)}, u32[]{:S(2)}) collective-permute-start(bf16[1024,1024]{1,0:T(8,128)(2,1)} %all-gather.4.cloned.1.call-done), channel_id=1, source_target_pairs={{0,0},{1,1},{2,2},{3,3},{4,8},{5,9},{6,10},{7,11},{8,4},{9,5},{10,... | collective-permute-start | bytes 6291464 | tf_op jit(solution)/shard_map/ppermute | solution.py:45
  93.9 14.4 %collective-permute-start.23 = (bf16[128,1024]{1,0:T(8,128)(2,1)S(1)}, bf16[128,1024]{1,0:T(8,128)(2,1)S(1)}, u32[]{:S(2)}, u32[]{:S(2)}) collective-permute-start(bf16[128,1024]{1,0:T(8,128)(2,1)S(1)} %fusion.7.mine.refs_0_), channel_id=1, source_target_pairs={{0,1},{1,2},{2,3},{3,0},{4,5},{5,6},{6,7},{7,4},{8,9},{9,10},{10,1... | collective-permute-start | bytes 786440 | tf_op jit(solution)/shard_map/ppermute | solution.py:31
  93.9 14.8 %collective-permute-start.27 = (bf16[128,1024]{1,0:T(8,128)(2,1)S(1)}, bf16[128,1024]{1,0:T(8,128)(2,1)S(1)}, u32[]{:S(2)}, u32[]{:S(2)}) collective-permute-start(bf16[128,1024]{1,0:T(8,128)(2,1)S(1)} %fusion.7.mine.refs_0_), channel_id=1, source_target_pairs={{0,3},{1,0},{2,1},{3,2},{4,7},{5,4},{6,5},{7,6},{8,11},{9,8},{10,9... | collective-permute-start | bytes 786440 | tf_op jit(solution)/shard_map/ppermute | solution.py:31
  96.6 19.1 %collective-permute-start.31 = (bf16[128,1024]{1,0:T(8,128)(2,1)S(1)}, bf16[128,1024]{1,0:T(8,128)(2,1)S(1)}, u32[]{:S(2)}, u32[]{:S(2)}) collective-permute-start(bf16[128,1024]{1,0:T(8,128)(2,1)S(1)} %fusion.7.mine.refs_0_), channel_id=1, source_target_pairs={{0,8},{8,0},{1,9},{9,1},{2,10},{10,2},{3,11},{11,3},{4,12},{12,4},... | collective-permute-start | bytes 786440 | tf_op jit(solution)/shard_map/ppermute | solution.py:35
  122.3 29.0 %collective-permute-start.35 = (bf16[1024,512]{1,0:T(8,128)(2,1)}, bf16[1024,512]{1,0:T(8,128)(2,1)S(1)}, u32[]{:S(2)}, u32[]{:S(2)}) collective-permute-start(bf16[1024,512]{1,0:T(8,128)(2,1)} %all-gather.6.cloned.1.call-done), channel_id=1, source_target_pairs={{0,0},{1,1},{2,2},{3,3},{4,8},{5,9},{6,10},{7,11},{8,4},{9,5},{10,... | collective-permute-start | bytes 3145736 | tf_op jit(solution)/shard_map/ppermute | solution.py:45
  135.0 20.8 %collective-permute-start.39 = (bf16[128,1024]{1,0:T(8,128)(2,1)S(1)}, bf16[128,1024]{1,0:T(8,128)(2,1)}, u32[]{:S(2)}, u32[]{:S(2)}) collective-permute-start(bf16[128,1024]{1,0:T(8,128)(2,1)S(1)} %fusion.8.mine.refs_36_), channel_id=1, source_target_pairs={{0,3},{1,0},{2,1},{3,2},{4,7},{5,4},{6,5},{7,6},{8,11},{9,8},{10,9... | collective-permute-start | bytes 786440 | tf_op jit(solution)/shard_map/ppermute | solution.py:31
  137.6 18.3 %collective-permute-start.33 = (bf16[128,1024]{1,0:T(8,128)(2,1)S(1)}, bf16[128,1024]{1,0:T(8,128)(2,1)}, u32[]{:S(2)}, u32[]{:S(2)}) collective-permute-start(bf16[128,1024]{1,0:T(8,128)(2,1)S(1)} %fusion.8.mine.refs_36_), channel_id=1, source_target_pairs={{0,2},{1,3},{2,0},{3,1},{4,6},{5,7},{6,4},{7,5},{8,10},{9,11},{10,... | collective-permute-start | bytes 786440 | tf_op jit(solution)/shard_map/ppermute | solution.py:31
  137.6 18.8 %collective-permute-start.36 = (bf16[128,1024]{1,0:T(8,128)(2,1)S(1)}, bf16[128,1024]{1,0:T(8,128)(2,1)}, u32[]{:S(2)}, u32[]{:S(2)}) collective-permute-start(bf16[128,1024]{1,0:T(8,128)(2,1)S(1)} %fusion.8.mine.refs_36_), channel_id=1, source_target_pairs={{0,8},{8,0},{1,9},{9,1},{2,10},{10,2},{3,11},{11,3},{4,12},{12,4},... | collective-permute-start | bytes 786440 | tf_op jit(solution)/shard_map/ppermute | solution.py:35
  144.0 15.0 %collective-permute-start.38 = (bf16[128,1024]{1,0:T(8,128)(2,1)}, bf16[128,1024]{1,0:T(8,128)(2,1)}, u32[]{:S(2)}, u32[]{:S(2)}) collective-permute-start(bf16[128,1024]{1,0:T(8,128)(2,1)} %collective-permute-done.37.mine.refs_38_), channel_id=1, source_target_pairs={{0,8},{8,0},{1,9},{9,1},{2,10},{10,2},{3,11},{11,3},{4,12},{12,4},... | collective-permute-start | bytes 786440 | tf_op jit(solution)/shard_map/ppermute | solution.py:35
  152.3 51.7 %collective-permute-start.50 = (bf16[1024,1024]{1,0:T(8,128)(2,1)}, bf16[1024,1024]{1,0:T(8,128)(2,1)S(1)}, u32[]{:S(2)}, u32[]{:S(2)}) collective-permute-start(bf16[1024,1024]{1,0:T(8,128)(2,1)} %all-gather.8.cloned.1.call-done), channel_id=1, source_target_pairs={{0,0},{1,1},{2,2},{3,3},{4,8},{5,9},{6,10},{7,11},{8,4},{9,5},{10,... | collective-permute-start | bytes 6291464 | tf_op jit(solution)/shard_map/ppermute | solution.py:45
  172.5 14.9 %collective-permute-start.46 = (bf16[128,1024]{1,0:T(8,128)(2,1)S(1)}, bf16[128,1024]{1,0:T(8,128)(2,1)S(1)}, u32[]{:S(2)}, u32[]{:S(2)}) collective-permute-start(bf16[128,1024]{1,0:T(8,128)(2,1)S(1)} %add_convert_fusion.17), channel_id=1, source_target_pairs={{0,1},{1,2},{2,3},{3,0},{4,5},{5,6},{6,7},{7,4},{8,9},{9,10},{10,1... | collective-permute-start | bytes 786440 | tf_op jit(solution)/shard_map/ppermute | solution.py:31
  188.4 14.9 %collective-permute-start.53 = (bf16[128,1024]{1,0:T(8,128)(2,1)S(1)}, bf16[128,1024]{1,0:T(8,128)(2,1)S(1)}, u32[]{:S(2)}, u32[]{:S(2)}) collective-permute-start(bf16[128,1024]{1,0:T(8,128)(2,1)S(1)} %fusion.9.mine.refs_0_), channel_id=1, source_target_pairs={{0,1},{1,2},{2,3},{3,0},{4,5},{5,6},{6,7},{7,4},{8,9},{9,10},{10,1... | collective-permute-start | bytes 786440 | tf_op jit(solution)/shard_map/ppermute | solution.py:31
  188.8 15.4 %collective-permute-start.57 = (bf16[128,1024]{1,0:T(8,128)(2,1)S(1)}, bf16[128,1024]{1,0:T(8,128)(2,1)S(1)}, u32[]{:S(2)}, u32[]{:S(2)}) collective-permute-start(bf16[128,1024]{1,0:T(8,128)(2,1)S(1)} %fusion.9.mine.refs_0_), channel_id=1, source_target_pairs={{0,3},{1,0},{2,1},{3,2},{4,7},{5,4},{6,5},{7,6},{8,11},{9,8},{10,9... | collective-permute-start | bytes 786440 | tf_op jit(solution)/shard_map/ppermute | solution.py:31
  191.1 14.7 %collective-permute-start.61 = (bf16[128,1024]{1,0:T(8,128)(2,1)S(1)}, bf16[128,1024]{1,0:T(8,128)(2,1)S(1)}, u32[]{:S(2)}, u32[]{:S(2)}) collective-permute-start(bf16[128,1024]{1,0:T(8,128)(2,1)S(1)} %fusion.9.mine.refs_0_), channel_id=1, source_target_pairs={{0,8},{8,0},{1,9},{9,1},{2,10},{10,2},{3,11},{11,3},{4,12},{12,4},... | collective-permute-start | bytes 786440 | tf_op jit(solution)/shard_map/ppermute | solution.py:35
  211.9 13.9 %collective-permute-start.60 = (bf16[128,1024]{1,0:T(8,128)(2,1)S(1)}, bf16[128,1024]{1,0:T(8,128)(2,1)S(1)}, u32[]{:S(2)}, u32[]{:S(2)}) collective-permute-start(bf16[128,1024]{1,0:T(8,128)(2,1)S(1)} %add_convert_fusion.14), channel_id=1, source_target_pairs={{0,1},{1,2},{2,3},{3,0},{4,5},{5,6},{6,7},{7,4},{8,9},{9,10},{10,1... | collective-permute-start | bytes 786440 | tf_op jit(solution)/shard_map/ppermute | solution.py:31
  212.5 14.0 %collective-permute-start.64 = (bf16[128,1024]{1,0:T(8,128)(2,1)S(1)}, bf16[128,1024]{1,0:T(8,128)(2,1)S(1)}, u32[]{:S(2)}, u32[]{:S(2)}) collective-permute-start(bf16[128,1024]{1,0:T(8,128)(2,1)S(1)} %copy-done.174), channel_id=1, source_target_pairs={{0,0},{1,1},{2,2},{3,3},{4,8},{5,9},{6,10},{7,11},{8,4},{9,5},{10,... | collective-permute-start | bytes 786440 | tf_op jit(solution)/shard_map/ppermute | solution.py:45
  227.3 15.0 %collective-permute-start.69 = (bf16[128,1024]{1,0:T(8,128)(2,1)S(1)}, bf16[128,1024]{1,0:T(8,128)(2,1)S(1)}, u32[]{:S(2)}, u32[]{:S(2)}) collective-permute-start(bf16[128,1024]{1,0:T(8,128)(2,1)S(1)} %get-tuple-element.392.mine.refs_12_), channel_id=1, source_target_pairs={{0,1},{1,2},{2,3},{3,0},{4,5},{5,6},{6,7},{7,4},{8,9},{9,10},{10,1... | collective-permute-start | bytes 786440 | tf_op jit(solution)/shard_map/ppermute | solution.py:31
  228.2 14.6 %collective-permute-start.73 = (bf16[128,1024]{1,0:T(8,128)(2,1)S(1)}, bf16[128,1024]{1,0:T(8,128)(2,1)S(1)}, u32[]{:S(2)}, u32[]{:S(2)}) collective-permute-start(bf16[128,1024]{1,0:T(8,128)(2,1)S(1)} %get-tuple-element.392.mine.refs_12_), channel_id=1, source_target_pairs={{0,3},{1,0},{2,1},{3,2},{4,7},{5,4},{6,5},{7,6},{8,11},{9,8},{10,9... | collective-permute-start | bytes 786440 | tf_op jit(solution)/shard_map/ppermute | solution.py:31
  249.6 13.9 %collective-permute-start.76 = (bf16[128,1024]{1,0:T(8,128)(2,1)S(1)}, bf16[128,1024]{1,0:T(8,128)(2,1)S(1)}, u32[]{:S(2)}, u32[]{:S(2)}) collective-permute-start(bf16[128,1024]{1,0:T(8,128)(2,1)S(1)} %add_convert_fusion.10), channel_id=1, source_target_pairs={{0,1},{1,2},{2,3},{3,0},{4,5},{5,6},{6,7},{7,4},{8,9},{9,10},{10,1... | collective-permute-start | bytes 786440 | tf_op jit(solution)/shard_map/ppermute | solution.py:31
  265.9 15.6 %collective-permute-start.81 = (bf16[128,1024]{1,0:T(8,128)(2,1)S(1)}, bf16[128,1024]{1,0:T(8,128)(2,1)S(1)}, u32[]{:S(2)}, u32[]{:S(2)}) collective-permute-start(bf16[128,1024]{1,0:T(8,128)(2,1)S(1)} %get-tuple-element.394.mine.refs_24_), channel_id=1, source_target_pairs={{0,3},{1,0},{2,1},{3,2},{4,7},{5,4},{6,5},{7,6},{8,11},{9,8},{10,9... | collective-permute-start | bytes 786440 | tf_op jit(solution)/shard_map/ppermute | solution.py:31
  296.9 14.1 %collective-permute-start.89 = (bf16[128,1024]{1,0:T(8,128)(2,1)}, bf16[128,1024]{1,0:T(8,128)(2,1)}, u32[]{:S(2)}, u32[]{:S(2)}) collective-permute-start(bf16[128,1024]{1,0:T(8,128)(2,1)} %add_convert_fusion.8), channel_id=1, source_target_pairs={{0,3},{1,0},{2,1},{3,2},{4,7},{5,4},{6,5},{7,6},{8,11},{9,8},{10,9... | collective-permute-start | bytes 786440 | tf_op jit(solution)/shard_map/ppermute | solution.py:31
  315.4 14.7 %collective-permute-start.97 = (bf16[128,1024]{1,0:T(8,128)(2,1)S(1)}, bf16[128,1024]{1,0:T(8,128)(2,1)S(1)}, u32[]{:S(2)}, u32[]{:S(2)}) collective-permute-start(bf16[128,1024]{1,0:T(8,128)(2,1)S(1)} %get-tuple-element.386.mine.refs_12_), channel_id=1, source_target_pairs={{0,1},{1,2},{2,3},{3,0},{4,5},{5,6},{6,7},{7,4},{8,9},{9,10},{10,1... | collective-permute-start | bytes 786440 | tf_op jit(solution)/shard_map/ppermute | solution.py:31
  339.3 14.3 %collective-permute-start.100 = (bf16[128,1024]{1,0:T(8,128)(2,1)S(1)}, bf16[128,1024]{1,0:T(8,128)(2,1)}, u32[]{:S(2)}, u32[]{:S(2)}) collective-permute-start(bf16[128,1024]{1,0:T(8,128)(2,1)S(1)} %add_convert_fusion.5), channel_id=1, source_target_pairs={{0,3},{1,0},{2,1},{3,2},{4,7},{5,4},{6,5},{7,6},{8,11},{9,8},{10,9... | collective-permute-start | bytes 786440 | tf_op jit(solution)/shard_map/ppermute | solution.py:31
  356.8 17.8 %collective-permute-start.109 = (bf16[128,1024]{1,0:T(8,128)(2,1)S(1)}, bf16[128,1024]{1,0:T(8,128)(2,1)S(1)}, u32[]{:S(2)}, u32[]{:S(2)}) collective-permute-start(bf16[128,1024]{1,0:T(8,128)(2,1)S(1)} %get-tuple-element.389.mine.refs_24_), channel_id=1, source_target_pairs={{0,3},{1,0},{2,1},{3,2},{4,7},{5,4},{6,5},{7,6},{8,11},{9,8},{10,9... | collective-permute-start | bytes 786440 | tf_op jit(solution)/shard_map/ppermute | solution.py:31
  359.1 15.5 %collective-permute-start.123 = (f32[4,12,128]{2,0,1:T(4,128)S(1)}, f32[4,12,128]{2,0,1:T(4,128)S(1)}, u32[]{:S(2)}, u32[]{:S(2)}) collective-permute-start(f32[4,12,128]{2,0,1:T(4,128)S(1)} %dynamic-slice_bitcast_fusion), channel_id=1, source_target_pairs={{0,8},{8,0},{1,9},{9,1},{2,10},{10,2},{3,11},{11,3},{4,12},{12,4},... | collective-permute-start | bytes 73736 | tf_op jit(solution)/shard_map/ppermute | solution.py:35
  360.5 14.4 %collective-permute-start.107 = (bf16[128,1024]{1,0:T(8,128)(2,1)S(1)}, bf16[128,1024]{1,0:T(8,128)(2,1)S(1)}, u32[]{:S(2)}, u32[]{:S(2)}) collective-permute-start(bf16[128,1024]{1,0:T(8,128)(2,1)S(1)} %get-tuple-element.389.mine.refs_24_), channel_id=1, source_target_pairs={{0,2},{1,3},{2,0},{3,1},{4,6},{5,7},{6,4},{7,5},{8,10},{9,11},{10,... | collective-permute-start | bytes 786440 | tf_op jit(solution)/shard_map/ppermute | solution.py:31
  361.7 14.7 %collective-permute-start.113 = (bf16[128,1024]{1,0:T(8,128)(2,1)S(1)}, bf16[128,1024]{1,0:T(8,128)(2,1)S(1)}, u32[]{:S(2)}, u32[]{:S(2)}) collective-permute-start(bf16[128,1024]{1,0:T(8,128)(2,1)S(1)} %get-tuple-element.389.mine.refs_24_), channel_id=1, source_target_pairs={{0,8},{8,0},{1,9},{9,1},{2,10},{10,2},{3,11},{11,3},{4,12},{12,4},... | collective-permute-start | bytes 786440 | tf_op jit(solution)/shard_map/ppermute | solution.py:35
  374.8 32.2 %collective-permute-start.124 = (f32[12,128]{1,0:T(8,128)S(1)}, f32[12,128]{1,0:T(8,128)S(1)}, u32[]{:S(2)}, u32[]{:S(2)}) collective-permute-start(f32[12,128]{1,0:T(8,128)S(1)} %bitcast.214), channel_id=1, source_target_pairs={{0,3},{1,0},{2,1},{3,2},{4,7},{5,4},{6,5},{7,6},{8,11},{9,8},{10,9... | collective-permute-start | bytes 18440 | tf_op jit(solution)/shard_map/ppermute | solution.py:31
  374.9 32.1 %collective-permute-start.125 = (f32[12,128]{1,0:T(8,128)S(1)}, f32[12,128]{1,0:T(8,128)S(1)}, u32[]{:S(2)}, u32[]{:S(2)}) collective-permute-start(f32[12,128]{1,0:T(8,128)S(1)} %bitcast.216), channel_id=1, source_target_pairs={{0,1},{1,2},{2,3},{3,0},{4,5},{5,6},{6,7},{7,4},{8,9},{9,10},{10,1... | collective-permute-start | bytes 18440 | tf_op jit(solution)/shard_map/ppermute | solution.py:31
  380.8 26.2 %collective-permute-start.126 = (f32[12,128]{1,0:T(8,128)S(1)}, f32[12,128]{1,0:T(8,128)S(1)}, u32[]{:S(2)}, u32[]{:S(2)}) collective-permute-start(f32[12,128]{1,0:T(8,128)S(1)} %bitcast.215), channel_id=1, source_target_pairs={{0,2},{1,3},{2,0},{3,1},{4,6},{5,7},{6,4},{7,5},{8,10},{9,11},{10,... | collective-permute-start | bytes 18440 | tf_op jit(solution)/shard_map/ppermute | solution.py:31
  397.7 25.3 %all-to-all-start.1 = ((bf16[16,80,384]{2,1,0:T(8,128)(2,1)}), bf16[16,80,384]{2,1,0:T(8,128)(2,1)}, u32[]{:S(2)}, u32[]{:S(2)}) async-start(bf16[16,80,384]{2,1,0:T(8,128)(2,1)} %shard_map.362), calls=%async_computation.1 | async-start | bytes 1966080 | tf_op jit(solution)/shard_map/all_to_all | solution.py:405
  422.9 87.9 %all-to-all-start.2 = ((bf16[16,80,1536]{2,1,0:T(8,128)(2,1)}), bf16[16,80,1536]{2,1,0:T(8,128)(2,1)}, u32[]{:S(2)}, u32[]{:S(2)}) async-start(bf16[16,80,1536]{2,1,0:T(8,128)(2,1)} %shard_map.363), calls=%async_computation.2 | async-start | bytes 7864320 | tf_op jit(solution)/shard_map/all_to_all | solution.py:405
  440.6 58.3 %collective-permute-start.63 = (bf16[128,1024]{1,0:T(8,128)(2,1)S(1)}, bf16[128,1024]{1,0:T(8,128)(2,1)S(1)}, u32[]{:S(2)}, u32[]{:S(2)}) collective-permute-start(bf16[128,1024]{1,0:T(8,128)(2,1)S(1)} %copy-done.148), channel_id=1, source_target_pairs={{0,0},{1,1},{2,2},{3,3},{4,8},{5,9},{6,10},{7,11},{8,4},{9,5},{10,... | collective-permute-start | bytes 786440 | tf_op jit(solution)/shard_map/ppermute | solution.py:45
  451.6 50.1 %collective-permute-start.121 = (bf16[128,1024]{1,0:T(8,128)(2,1)S(1)}, bf16[128,1024]{1,0:T(8,128)(2,1)S(1)}, u32[]{:S(2)}, u32[]{:S(2)}) collective-permute-start(bf16[128,1024]{1,0:T(8,128)(2,1)S(1)} %add_convert_fusion), channel_id=1, source_target_pairs={{0,0},{1,1},{2,2},{3,3},{4,8},{5,9},{6,10},{7,11},{8,4},{9,5},{10,... | collective-permute-start | bytes 786440 | tf_op jit(solution)/shard_map/ppermute | solution.py:45
  458.0 49.2 %collective-permute-start.122 = (bf16[64,384]{1,0:T(8,128)(2,1)S(1)}, bf16[64,384]{1,0:T(8,128)(2,1)S(1)}, u32[]{:S(2)}, u32[]{:S(2)}) collective-permute-start(bf16[64,384]{1,0:T(8,128)(2,1)S(1)} %slice.460), channel_id=1, source_target_pairs={{0,0},{1,1},{2,2},{3,3},{4,8},{5,9},{6,10},{7,11},{8,4},{9,5},{10,... | collective-permute-start | bytes 147464 | tf_op jit(solution)/shard_map/ppermute | solution.py:45
  515.3 14.4 %collective-permute-start.132 = (f32[12,128]{1,0:T(8,128)S(1)}, f32[12,128]{1,0:T(8,128)S(1)}, u32[]{:S(2)}, u32[]{:S(2)}) collective-permute-start(f32[12,128]{1,0:T(8,128)S(1)} %slice.418), channel_id=1, source_target_pairs={{0,3},{1,0},{2,1},{3,2},{4,7},{5,4},{6,5},{7,6},{8,11},{9,8},{10,9... | collective-permute-start | bytes 18440 | tf_op jit(solution)/shard_map/ppermute | solution.py:31
  (269 other events, 2170.0 us)
Sparse Core Ops, SparseCore 0:
  10.3 46.7 all-gather.3
  59.4 32.2 all-gather.5
  93.4 34.0 all-gather.7
  360.1 81.7 reduce-scatter.1
where the time goes:
time: 556 us; the launch traced here: 547 us
  starting transfers between devices  191 us (34%)
  waiting for transfers between devices  180 us (32%)
  Pallas kernels  80.1 us (14%)
  local copies, waits for them, and re-layouts  43.3 us (8%)
  other arithmetic  34.8 us (6%)
  between operations  17.5 us (3%)
    ppermute x54, waiting for transfers between devices, along_x(): lax.ppermute(value, 'x', [(i, (i + hop) % ring) for i in range(ring)])  129 us
    pallas_call x51, Pallas kernels, call(): pl.pallas_call(body, grid=grid, in_specs=in_specs or [whole(a) for a in a...  80.1 us
    ppermute x14, starting transfers between devices, swap_core_z(): return lax.ppermute(value, ('c', 'zh', 'x'), pairs)  59.3 us
    ppermute x54, starting transfers between devices, along_x(): lax.ppermute(value, 'x', [(i, (i + hop) % ring) for i in range(ring)])  54.6 us
    ppermute x67, starting transfers between devices, other_core(): return lax.ppermute(value, 'c', [(0, 1), (1, 0)])  53.1 us
    ppermute x14, waiting for transfers between devices, swap_core_z(): return lax.ppermute(value, ('c', 'zh', 'x'), pairs)  44.4 us
    unnamed x389, local copies, waits for them, and re-layouts  25.6 us
    all_to_all x2, starting transfers between devices, sum_owners(): lax.all_to_all(terms, OWNERS, 0, 0, tiled=True).astype(F32)  19.2 us
  transfers between devices with their start and end apart: 142, of which 39 were waited for; matrix products, arithmetic and copies ran while one was open for 8% of the time, Pallas kernels for 14%

commit v1 on v0

--- a/solution.py
+++ b/solution.py
@@ -401,6 +401,8 @@
     layer_output = swap_core_z(current.astype(BF16)).astype(F32)
 
     grad_rows = swap_core_z(cotangent).astype(F32)
+    attn_cols = qkv_cols + head_cols
+
     def sum_owners(terms):
         return jnp.sum(lax.all_to_all(terms, OWNERS, 0, 0, tiled=True).astype(F32), axis=0)
 
@@ -409,8 +411,9 @@
         padded = jnp.pad(values, (0, count * cols - values.shape[0]))
         return padded.reshape(count, cols).astype(BF16)
 
-    late_grads, qkv_grads = [None] * layers, [None] * layers
-    row_sums, head_sums, waiting = [], [], []
+    ffn_grads, attn_grads = [None] * layers, [None] * layers
+    row_sums, head_sums, pending = [], [], None
+    tie = lax.optimization_barrier
     for layer in reversed(range(layers)):
         (inputs, qkv, keys, values, attended, soft, mid_unit, mid_scale, mids, slopes,
          activated, out_unit, out_scale) = saved[layer]
@@ -430,6 +433,13 @@
             up_sums.append(up_sum[0])
         grad_mid = grad_second + scatter_pairs(parts)
         up_bias_term = sum(up_sums)
+        ffn_pairs = [(mids, grad_pre), (branch, activated)]
+        if layer:
+            grad_mid, terms = tie((grad_mid, weight_grads(ffn_pairs, owners)))
+            found = sum_owners(terms)
+        if pending is not None:
+            grad_mid, pending = tie((grad_mid, pending))
+            attn_grads[layer + 1] = swap_core_z(pending.astype(BF16))
         grad_first, att_gain_term, att_shift_term = norm_back(
             grad_mid, mid_unit, mid_scale, attention_gain[layer]
         )
@@ -441,24 +451,13 @@
                        out_shift_term])
         )
         head_sums.append(up_bias_term)
-        late = [(mids, grad_pre), (branch, activated), (attn_chunks, attended)]
-        if layer:
-            terms = weight_grads(late, owners)
-            found = lax.psum_scatter(terms, OWNERS, scatter_dimension=0, tiled=False)
-            late_grads[layer] = swap_core_z(found)
-        else:
+        if not layer:
             kept = sum_group(jnp.concatenate(row_sums), core, x)
             small = jnp.concatenate(head_sums + [kept.reshape(-1)])
-            cols = sum(right[0].shape[1] for _, right in late + waiting)
-            terms = weight_grads(late + waiting, owners, extra_rows(small, cols))
+            terms = weight_grads(ffn_pairs, owners, extra_rows(small, 2 * ffn_half))
+            final = ARRIVAL[-1]
+            attn_chunks[final], terms = tie((attn_chunks[final], terms))
             joint = sum_owners(terms)
-            early_sums = joint[shard_rows:].reshape(-1)[: small.shape[0]]
-            joint = swap_core_z(joint[:shard_rows].astype(BF16))
-            late_cols = cols - (layers - 1) * qkv_cols
-            late_grads[0] = joint[:, :late_cols]
-            for index in range(1, layers):
-                start = late_cols + (layers - 1 - index) * qkv_cols
-                qkv_grads[index] = joint[:, start : start + qkv_cols]
         grad_q = {}
         grad_k, grad_v = jnp.zeros(keys.shape, F32), jnp.zeros(keys.shape, F32)
         for hop in ARRIVAL:
@@ -474,27 +473,21 @@
         grad_rows = grad_first + scatter_pairs(parts)
         bias_terms = sum(sums)
         pair_sums = jnp.concatenate([bias_terms[:head_cols], bias_terms[2 * head_cols :]])
+        attn_pairs = [(inputs, grad_qkv), (attn_chunks, attended)]
         if layer:
-            waiting.append((inputs, grad_qkv))
             head_sums.append(pair_sums)
+            terms = weight_grads(attn_pairs, owners)
+            grad_rows, terms, found = tie((grad_rows, terms, found))
+            ffn_grads[layer] = swap_core_z(found.astype(BF16))
+            pending = sum_owners(terms)
         else:
-            terms = weight_grads([(inputs, grad_qkv)], owners, extra_rows(pair_sums, qkv_cols))
-            got = sum_owners(terms)
-            qkv_grads[0] = swap_core_z(got[:shard_rows].astype(BF16))
-            last_sums = got[shard_rows:].reshape(-1)[: 2 * head_cols]
+            terms = weight_grads(attn_pairs, owners, extra_rows(pair_sums, attn_cols))
+            terms, joint = tie((terms, joint))
+            last = lax.all_to_all(terms, OWNERS, 0, 0, tiled=True)
+    ffn_grads[0] = swap_core_z(joint[:shard_rows].astype(BF16))
+    early_sums = joint[shard_rows:].reshape(-1)[: small.shape[0]]
 
     head_len = sum(item.shape[0] for item in head_sums)
-    ups, pairs, place = [None] * layers, [last_sums] + [None] * (layers - 1), 0
-    for layer in reversed(range(layers)):
-        ups[layer] = early_sums[place : place + ffn_half]
-        place += ffn_half
-        if layer:
-            pairs[layer] = early_sums[place : place + 2 * head_cols]
-            place += 2 * head_cols
-    up_all = swap_core_z(jnp.stack(ups))
-    pair_all = swap_core_z(jnp.stack(pairs))
-    input_grad = swap_core_z(grad_rows.astype(BF16)).astype(F32)
-
     piece = early_sums[head_len:].reshape(layers * 6, -1)
     table = jnp.zeros((2, ring) + piece.shape, F32)
     for hop in HOPS:
@@ -509,24 +502,41 @@
         chosen = [piece[:, start : start + count].astype(F32) for piece in pieces]
         return jnp.stack([jnp.swapaxes(one, 0, 1) if turn else one for one in chosen])
 
+    ups, pairs, place = [None] * layers, [None] * layers, 0
+    for layer in reversed(range(layers)):
+        ups[layer] = early_sums[place : place + ffn_half]
+        place += ffn_half
+        if layer:
+            pairs[layer] = early_sums[place : place + 2 * head_cols]
+            place += 2 * head_cols
+    done = (
+        layer_output,
+        cols(ffn_grads, 0, ffn_half),
+        cols(ffn_grads, ffn_half, ffn_half, True),
+        swap_core_z(jnp.stack(ups)),
+        [rows_out[:, index] for index in range(6)],
+    )
+    last, done = tie((last, done))
+    layer_output, up_grads, down_grads, up_all, row_grads = done
+    got = jnp.sum(last.astype(F32), axis=0)
+    attn_grads[0] = swap_core_z(got[:shard_rows].astype(BF16))
+    pairs[0] = got[shard_rows:].reshape(-1)[: 2 * head_cols]
+    pair_all = swap_core_z(jnp.stack(pairs))
+    input_grad = swap_core_z(grad_rows.astype(BF16)).astype(F32)
+
     return (
         layer_output,
         input_grad,
-        cols(qkv_grads, 0, head_cols),
-        cols(qkv_grads, head_cols, head_cols),
-        cols(qkv_grads, 2 * head_cols, head_cols),
-        cols(late_grads, 2 * ffn_half, head_cols, True),
-        cols(late_grads, 0, ffn_half),
-        cols(late_grads, ffn_half, ffn_half, True),
+        cols(attn_grads, 0, head_cols),
+        cols(attn_grads, head_cols, head_cols),
+        cols(attn_grads, 2 * head_cols, head_cols),
+        cols(attn_grads, qkv_cols, head_cols, True),
+        up_grads,
+        down_grads,
         pair_all[:, :head_cols],
         pair_all[:, head_cols:],
         up_all,
-        rows_out[:, 0],
-        rows_out[:, 1],
-        rows_out[:, 2],
-        rows_out[:, 3],
-        rows_out[:, 4],
-        rows_out[:, 5],
+        *row_grads,
     )
 
 

time: 556 us -> 559 us (level)
  the two profiles are of different devices: /device:TPU:25 before, /device:TPU:37 now
where the time goes in v1:
time: 559 us; the launch traced here: 548 us
  starting transfers between devices  241 us (43%)
  waiting for transfers between devices  94.9 us (17%)
  Pallas kernels  93 us (17%)
  local copies, waits for them, and re-layouts  56.1 us (10%)
  other arithmetic  45.3 us (8%)
  between operations  17.5 us (3%)
    ppermute x54, starting transfers between devices, along_x(): lax.ppermute(value, 'x', [(i, (i + hop) % ring) for i in range(ring)])  99.2 us
    pallas_call x52, Pallas kernels, call(): pl.pallas_call(body, grid=grid, in_specs=in_specs or [whole(a) for a in a...  93 us
    ppermute x54, waiting for transfers between devices, along_x(): lax.ppermute(value, 'x', [(i, (i + hop) % ring) for i in range(ring)])  67.2 us
    ppermute x67, starting transfers between devices, other_core(): return lax.ppermute(value, 'c', [(0, 1), (1, 0)])  59.8 us
    ppermute x15, starting transfers between devices, swap_core_z(): return lax.ppermute(value, ('c', 'zh', 'x'), pairs)  54.3 us
    unnamed x426, local copies, waits for them, and re-layouts  36.1 us
    all_to_all x3, starting transfers between devices, sum_owners(): lax.all_to_all(terms, OWNERS, 0, 0, tiled=True).astype(F32)  16.8 us
    ppermute x15, waiting for transfers between devices, swap_core_z(): return lax.ppermute(value, ('c', 'zh', 'x'), pairs)  13.1 us
  transfers between devices with their start and end apart: 144, of which 30 were waited for; matrix products, arithmetic and copies ran while one was open for 10% of the time, Pallas kernels for 17%

profile of v1, /device:TPU:37, one launch (start us, length us, event | category | flops | bytes accessed | tf_op | source)
XLA Modules:
  0.0 548.4 jit_solution(2881434267433221792)
XLA Ops:
  13.5 5.2 collective-permute-start
  21.4 5.1 collective-permute-start.9
  29.6 5.4 all-to-all-start
  49.9 5.7 %all-to-all-done = bf16[16,64,512]{2,1,0:T(8,128)(2,1)} async-done(((bf16[16,64,512]{2,1,0:T(8,128)(2,1)}), bf16[16,64,512]{2,1,0:T(8,128)(2,1)}, u32[]{:S(2)}, u32[]{:S(2)}) %all-to-all-start) | async-done | bytes 1048608 | tf_op jit(solution)/shard_map/all_to_all | solution.py:331
  75.0 3.1 collective-permute-start.20
  92.3 3.6 collective-permute-start.27
  99.3 3.4 collective-permute-done.27.mine.refs_4_
  104.6 5.2 collective-permute-done.18.mine.refs_6_
  125.0 3.5 collective-permute-start.22
  132.3 4.3 collective-permute-done.22
  138.8 3.8 collective-permute-start.37
  146.8 4.3 collective-permute-start.38
  181.9 3.4 collective-permute-done.46
  185.9 5.9 %collective-permute-done.42 = bf16[128,1024]{1,0:T(8,128)(2,1)S(1)} collective-permute-done((bf16[128,1024]{1,0:T(8,128)(2,1)S(1)}, bf16[128,1024]{1,0:T(8,128)(2,1)S(1)}, u32[]{:S(2)}, u32[]{:S(2)}) %collective-permute-start.42) | collective-permute-done | bytes 262176 | tf_op jit(solution)/shard_map/ppermute | solution.py:31
  203.4 3.3 collective-permute-done.48.mine.refs_6_
  218.4 3.7 collective-permute-start.52
  222.1 4.1 collective-permute-start.63
  226.3 4.7 collective-permute-done.52
  237.8 3.2 collective-permute-done.72.mine.refs_16_
  241.0 4.2 collective-permute-start.73
  261.0 3.7 collective-permute-start.67
  264.7 6.6 %shard_map.342 = bf16[16,64,1024]{2,1,0:T(8,128)(2,1)} custom-call(bf16[128,1024]{1,0:T(8,128)(2,1)} %copy-done.4, bf16[128,1024]{1,0:T(8,128)(2,1)} %copy-done.26, bf16[128,1024]{1,0:T(8,128)(2,1)} %copy-done.25, bf16[128,1024]{1,0:T(8,128)(2,1)} %copy-done.29, bf16[128,1024]{1,0:T(8,128)(2,1)} %copy-done.24, bf16[128,1024]{1,0:T(8,128)(2,1)} %copy-done.28, ...), custom_call_target="tpu_custom_call" | custom-call | flops 4294967296 | bytes 8388608 | tf_op jit(solution)/shard_map/pallas_call | solution.py:87
  275.9 3.7 collective-permute-start.82
  283.9 4.3 collective-permute-start.83
  290.8 4.3 all-to-all-start.1
  312.5 4.1 collective-permute-start.117
  320.9 4.6 collective-permute-start.90
  331.0 5.7 %shard_map.351 = bf16[16,64,512]{2,1,0:T(8,128)(2,1)} custom-call(bf16[128,1024]{1,0:T(8,128)(2,1)} %copy-done.5, bf16[128,1024]{1,0:T(8,128)(2,1)} %collective-permute-done.36.other.refs_1_, bf16[128,1024]{1,0:T(8,128)(2,1)} %collective-permute-done.37.mine.refs_2_, bf16[128,1024]{1,0:T(8,128)(2,1)} %collective-permute-done.38.other.refs_3_, ...), custom_call_target="tpu_custom_call" | custom-call | flops 2147483648 | bytes 6291456 | tf_op jit(solution)/shard_map/pallas_call | solution.py:87
  343.0 3.7 collective-permute-start.100
  350.0 4.1 collective-permute-done.100.mine.refs_16_
  356.5 5.0 collective-permute-done.92.mine.refs_18_
  367.0 6.1 %all-to-all-start.2 = ((bf16[16,64,512]{2,1,0:T(8,128)(2,1)}), bf16[16,64,512]{2,1,0:T(8,128)(2,1)}, u32[]{:S(2)}, u32[]{:S(2)}) async-start(bf16[16,64,512]{2,1,0:T(8,128)(2,1)} %shard_map.351), calls=%async_computation.2 | async-start | bytes 2097152 | tf_op jit(solution)/shard_map/all_to_all | solution.py:407
  389.4 4.1 collective-permute-start.95
  397.5 4.1 collective-permute-done.95
  405.5 3.7 collective-permute-start.119
  409.2 3.6 collective-permute-start.107
  412.9 4.5 collective-permute-start.111
  424.8 6.6 %shard_map.357 = bf16[16,80,1024]{2,1,0:T(8,128)(2,1)} custom-call(bf16[128,1024]{1,0:T(8,128)(2,1)} %copy-done.3, bf16[128,1024]{1,0:T(8,128)(2,1)} %copy-done.20, bf16[128,1024]{1,0:T(8,128)(2,1)} %copy-done.18, bf16[128,1024]{1,0:T(8,128)(2,1)} %copy-done.22, bf16[128,1024]{1,0:T(8,128)(2,1)} %copy-done.17, bf16[128,1024]{1,0:T(8,128)(2,1)} %copy-done.21, ...), custom_call_target="tpu_custom_call" | custom-call | flops 4294967296 | bytes 8945664 | tf_op jit(solution)/shard_map/pallas_call | solution.py:87
  432.8 6.3 %all-to-all-start.3 = ((bf16[16,80,1024]{2,1,0:T(8,128)(2,1)}), bf16[16,80,1024]{2,1,0:T(8,128)(2,1)}, u32[]{:S(2)}, u32[]{:S(2)}) async-start(bf16[16,80,1024]{2,1,0:T(8,128)(2,1)} %shard_map.357), calls=%async_computation.3 | async-start | bytes 5242880 | tf_op jit(solution)/shard_map/all_to_all | solution.py:407
  440.7 4.4 collective-permute-start.134
  466.9 5.8 %shard_map.365 = bf16[16,80,512]{2,1,0:T(8,128)(2,1)} custom-call(bf16[128,1024]{1,0:T(8,128)(2,1)} %copy-done.6, bf16[128,1024]{1,0:T(8,128)(2,1)} %copy-done.37, bf16[128,1024]{1,0:T(8,128)(2,1)} %copy-done.35, bf16[128,1024]{1,0:T(8,128)(2,1)} %copy-done.39, bf16[128,1024]{1,0:T(8,128)(2,1)} %copy-done.36, bf16[128,1024]{1,0:T(8,128)(2,1)} %copy-done.40, ...), custom_call_target="tpu_custom_call" | custom-call | flops 2147483648 | bytes 6569984 | tf_op jit(solution)/shard_map/pallas_call | solution.py:87
  478.9 8.8 %all-to-all-done.3 = bf16[16,80,1024]{2,1,0:T(8,128)(2,1)} async-done(((bf16[16,80,1024]{2,1,0:T(8,128)(2,1)}), bf16[16,80,1024]{2,1,0:T(8,128)(2,1)}, u32[]{:S(2)}, u32[]{:S(2)}) %all-to-all-start.3) | async-done | bytes 2621472 | tf_op jit(solution)/shard_map/all_to_all | solution.py:407
  490.0 3.5 collective-permute-start.121
  495.9 5.9 %all-to-all-start.4 = ((bf16[16,80,512]{2,1,0:T(8,128)(2,1)}), bf16[16,80,512]{2,1,0:T(8,128)(2,1)S(1)}, u32[]{:S(2)}, u32[]{:S(2)}) async-start(bf16[16,80,512]{2,1,0:T(8,128)(2,1)} %shard_map.365), calls=%async_computation.4 | async-start | bytes 2621440 | tf_op jit(solution)/shard_map/all_to_all | solution.py:486
  501.9 6.5 %collective-permute-start.118 = (bf16[64,1024]{1,0:T(8,128)(2,1)S(1)}, bf16[64,1024]{1,0:T(8,128)(2,1)S(1)}, u32[]{:S(2)}, u32[]{:S(2)}) collective-permute-start(bf16[64,1024]{1,0:T(8,128)(2,1)S(1)} %slice.452), channel_id=1, source_target_pairs={{0,0},{1,1},{2,2},{3,3},{4,8},{5,9},{6,10},{7,11},{8,4},{9,5},{10,... | collective-permute-start | bytes 393224 | tf_op jit(solution)/shard_map/ppermute | solution.py:45
  514.4 9.3 %collective-permute-done.118 = bf16[64,1024]{1,0:T(8,128)(2,1)S(1)} collective-permute-done((bf16[64,1024]{1,0:T(8,128)(2,1)S(1)}, bf16[64,1024]{1,0:T(8,128)(2,1)S(1)}, u32[]{:S(2)}, u32[]{:S(2)}) %collective-permute-start.118) | collective-permute-done | bytes 131104 | tf_op jit(solution)/shard_map/ppermute | solution.py:45
  525.4 4.1 collective-permute-start.135
  534.7 3.5 collective-permute-done.133
  (893 shorter events, 305.5 us)
Async XLA Ops:
  7.2 67.8 %all-gather.4.cloned.1.call-start = ((), (), s32[]{:S(2)}) async-start(), calls=%async_computation.5 | async-start | bytes 2228224 | tf_op jit(solution)/shard_map/all_gather | solution.py:334
  9.7 120.1 %all-gather.6.cloned.1.call-start = ((), (), s32[]{:S(2)}) async-start(), calls=%async_computation.6 | async-start | bytes 1114112 | tf_op jit(solution)/shard_map/all_gather | solution.py:334
  13.5 139.5 %all-gather.8.cloned.1.call-start = ((), (), s32[]{:S(2)}) async-start(), calls=%async_computation.7 | async-start | bytes 2228224 | tf_op jit(solution)/shard_map/all_gather | solution.py:334
  13.5 21.5 %collective-permute-start = (bf16[128,1024]{1,0:T(8,128)(2,1)}, bf16[128,1024]{1,0:T(8,128)(2,1)S(1)}, u32[]{:S(2)}, u32[]{:S(2)}) collective-permute-start(bf16[128,1024]{1,0:T(8,128)(2,1)} %param.19), channel_id=1, source_target_pairs={{0,0},{1,1},{2,2},{3,3},{4,8},{5,9},{6,10},{7,11},{8,4},{9,5},{10,... | collective-permute-start | bytes 786440 | tf_op jit(solution)/shard_map/ppermute | solution.py:45
  21.4 22.5 %collective-permute-start.9 = (f32[2,768]{1,0:T(2,128)S(1)}, f32[2,768]{1,0:T(2,128)S(1)}, u32[]{:S(2)}, u32[]{:S(2)}) collective-permute-start(f32[2,768]{1,0:T(2,128)S(1)} %pad_maximum_fusion.4), channel_id=1, source_target_pairs={{0,0},{1,1},{2,2},{3,3},{4,8},{5,9},{6,10},{7,11},{8,4},{9,5},{10,... | collective-permute-start | bytes 18440 | tf_op jit(solution)/shard_map/ppermute | solution.py:45
  29.6 26.0 %all-to-all-start = ((bf16[16,64,512]{2,1,0:T(8,128)(2,1)}), bf16[16,64,512]{2,1,0:T(8,128)(2,1)}, u32[]{:S(2)}, u32[]{:S(2)}) async-start(bf16[16,64,512]{2,1,0:T(8,128)(2,1)} %broadcast_in_dim.18), calls=%async_computation | async-start | bytes 2097152 | tf_op jit(solution)/shard_map/all_to_all | solution.py:331
  38.0 19.8 %collective-permute-start.1 = (bf16[128,1024]{1,0:T(8,128)(2,1)S(1)}, bf16[128,1024]{1,0:T(8,128)(2,1)S(1)}, u32[]{:S(2)}, u32[]{:S(2)}) collective-permute-start(bf16[128,1024]{1,0:T(8,128)(2,1)S(1)} %collective-permute-done.mine.refs_0_), channel_id=1, source_target_pairs={{0,8},{8,0},{1,9},{9,1},{2,10},{10,2},{3,11},{11,3},{4,12},{12,4},... | collective-permute-start | bytes 786440 | tf_op jit(solution)/shard_map/ppermute | solution.py:35
  42.0 16.3 %collective-permute-start.3 = (bf16[128,1024]{1,0:T(8,128)(2,1)S(1)}, bf16[128,1024]{1,0:T(8,128)(2,1)S(1)}, u32[]{:S(2)}, u32[]{:S(2)}) collective-permute-start(bf16[128,1024]{1,0:T(8,128)(2,1)S(1)} %collective-permute-done.2.mine.refs_2_), channel_id=1, source_target_pairs={{0,8},{8,0},{1,9},{9,1},{2,10},{10,2},{3,11},{11,3},{4,12},{12,4},... | collective-permute-start | bytes 786440 | tf_op jit(solution)/shard_map/ppermute | solution.py:35
  44.5 14.3 %collective-permute-start.5 = (bf16[128,1024]{1,0:T(8,128)(2,1)S(1)}, bf16[128,1024]{1,0:T(8,128)(2,1)S(1)}, u32[]{:S(2)}, u32[]{:S(2)}) collective-permute-start(bf16[128,1024]{1,0:T(8,128)(2,1)S(1)} %collective-permute-done.4.mine.refs_4_), channel_id=1, source_target_pairs={{0,8},{8,0},{1,9},{9,1},{2,10},{10,2},{3,11},{11,3},{4,12},{12,4},... | collective-permute-start | bytes 786440 | tf_op jit(solution)/shard_map/ppermute | solution.py:35
  66.9 18.3 %collective-permute-start.17 = (bf16[128,1024]{1,0:T(8,128)(2,1)S(1)}, bf16[128,1024]{1,0:T(8,128)(2,1)}, u32[]{:S(2)}, u32[]{:S(2)}) collective-permute-start(bf16[128,1024]{1,0:T(8,128)(2,1)S(1)} %get-tuple-element.235), channel_id=1, source_target_pairs={{0,8},{8,0},{1,9},{9,1},{2,10},{10,2},{3,11},{11,3},{4,12},{12,4},... | collective-permute-start | bytes 786440 | tf_op jit(solution)/shard_map/ppermute | solution.py:35
  75.0 36.1 %collective-permute-start.20 = (bf16[1024,1024]{1,0:T(8,128)(2,1)}, bf16[1024,1024]{1,0:T(8,128)(2,1)S(1)}, u32[]{:S(2)}, u32[]{:S(2)}) collective-permute-start(bf16[1024,1024]{1,0:T(8,128)(2,1)} %all-gather.4.cloned.1.call-done), channel_id=1, source_target_pairs={{0,0},{1,1},{2,2},{3,3},{4,8},{5,9},{6,10},{7,11},{8,4},{9,5},{10,... | collective-permute-start | bytes 6291464 | tf_op jit(solution)/shard_map/ppermute | solution.py:45
  96.5 13.3 %collective-permute-start.18 = (bf16[128,1024]{1,0:T(8,128)(2,1)S(1)}, bf16[128,1024]{1,0:T(8,128)(2,1)S(1)}, u32[]{:S(2)}, u32[]{:S(2)}) collective-permute-start(bf16[128,1024]{1,0:T(8,128)(2,1)S(1)} %fusion.7.mine.refs_0_), channel_id=1, source_target_pairs={{0,2},{1,3},{2,0},{3,1},{4,6},{5,7},{6,4},{7,5},{8,10},{9,11},{10,... | collective-permute-start | bytes 786440 | tf_op jit(solution)/shard_map/ppermute | solution.py:31
  98.3 14.7 %collective-permute-start.31 = (bf16[128,1024]{1,0:T(8,128)(2,1)S(1)}, bf16[128,1024]{1,0:T(8,128)(2,1)S(1)}, u32[]{:S(2)}, u32[]{:S(2)}) collective-permute-start(bf16[128,1024]{1,0:T(8,128)(2,1)S(1)} %fusion.7.mine.refs_0_), channel_id=1, source_target_pairs={{0,8},{8,0},{1,9},{9,1},{2,10},{10,2},{3,11},{11,3},{4,12},{12,4},... | collective-permute-start | bytes 786440 | tf_op jit(solution)/shard_map/ppermute | solution.py:35
  116.9 15.3 %collective-permute-start.32 = (bf16[128,1024]{1,0:T(8,128)(2,1)}, bf16[128,1024]{1,0:T(8,128)(2,1)}, u32[]{:S(2)}, u32[]{:S(2)}) collective-permute-start(bf16[128,1024]{1,0:T(8,128)(2,1)} %get-tuple-element.243), channel_id=1, source_target_pairs={{0,8},{8,0},{1,9},{9,1},{2,10},{10,2},{3,11},{11,3},{4,12},{12,4},... | collective-permute-start | bytes 786440 | tf_op jit(solution)/shard_map/ppermute | solution.py:35
  129.8 22.1 %collective-permute-start.35 = (bf16[1024,512]{1,0:T(8,128)(2,1)}, bf16[1024,512]{1,0:T(8,128)(2,1)S(1)}, u32[]{:S(2)}, u32[]{:S(2)}) collective-permute-start(bf16[1024,512]{1,0:T(8,128)(2,1)} %all-gather.6.cloned.1.call-done), channel_id=1, source_target_pairs={{0,0},{1,1},{2,2},{3,3},{4,8},{5,9},{6,10},{7,11},{8,4},{9,5},{10,... | collective-permute-start | bytes 3145736 | tf_op jit(solution)/shard_map/ppermute | solution.py:45
  152.9 50.3 %collective-permute-start.50 = (bf16[1024,1024]{1,0:T(8,128)(2,1)}, bf16[1024,1024]{1,0:T(8,128)(2,1)S(1)}, u32[]{:S(2)}, u32[]{:S(2)}) collective-permute-start(bf16[1024,1024]{1,0:T(8,128)(2,1)} %all-gather.8.cloned.1.call-done), channel_id=1, source_target_pairs={{0,0},{1,1},{2,2},{3,3},{4,8},{5,9},{6,10},{7,11},{8,4},{9,5},{10,... | collective-permute-start | bytes 6291464 | tf_op jit(solution)/shard_map/ppermute | solution.py:45
  194.8 15.7 %collective-permute-start.61 = (bf16[128,1024]{1,0:T(8,128)(2,1)S(1)}, bf16[128,1024]{1,0:T(8,128)(2,1)S(1)}, u32[]{:S(2)}, u32[]{:S(2)}) collective-permute-start(bf16[128,1024]{1,0:T(8,128)(2,1)S(1)} %fusion.9.mine.refs_0_), channel_id=1, source_target_pairs={{0,8},{8,0},{1,9},{9,1},{2,10},{10,2},{3,11},{11,3},{4,12},{12,4},... | collective-permute-start | bytes 786440 | tf_op jit(solution)/shard_map/ppermute | solution.py:35
  212.2 14.0 %collective-permute-start.62 = (bf16[128,1024]{1,0:T(8,128)(2,1)S(1)}, bf16[128,1024]{1,0:T(8,128)(2,1)S(1)}, u32[]{:S(2)}, u32[]{:S(2)}) collective-permute-start(bf16[128,1024]{1,0:T(8,128)(2,1)S(1)} %get-tuple-element.271), channel_id=1, source_target_pairs={{0,8},{8,0},{1,9},{9,1},{2,10},{10,2},{3,11},{11,3},{4,12},{12,4},... | collective-permute-start | bytes 786440 | tf_op jit(solution)/shard_map/ppermute | solution.py:35
  254.7 16.6 %collective-permute-start.77 = (bf16[128,1024]{1,0:T(8,128)(2,1)}, bf16[128,1024]{1,0:T(8,128)(2,1)}, u32[]{:S(2)}, u32[]{:S(2)}) collective-permute-start(bf16[128,1024]{1,0:T(8,128)(2,1)} %get-tuple-element.283), channel_id=1, source_target_pairs={{0,8},{8,0},{1,9},{9,1},{2,10},{10,2},{3,11},{11,3},{4,12},{12,4},... | collective-permute-start | bytes 786440 | tf_op jit(solution)/shard_map/ppermute | solution.py:35
  279.6 15.5 %collective-permute-start.78 = (bf16[128,1024]{1,0:T(8,128)(2,1)S(1)}, bf16[128,1024]{1,0:T(8,128)(2,1)}, u32[]{:S(2)}, u32[]{:S(2)}) collective-permute-start(bf16[128,1024]{1,0:T(8,128)(2,1)S(1)} %get-tuple-element.440.mine.refs_12_), channel_id=1, source_target_pairs={{0,2},{1,3},{2,0},{3,1},{4,6},{5,7},{6,4},{7,5},{8,10},{9,11},{10,... | collective-permute-start | bytes 786440 | tf_op jit(solution)/shard_map/ppermute | solution.py:31
  281.5 14.6 %collective-permute-start.84 = (bf16[128,1024]{1,0:T(8,128)(2,1)S(1)}, bf16[128,1024]{1,0:T(8,128)(2,1)}, u32[]{:S(2)}, u32[]{:S(2)}) collective-permute-start(bf16[128,1024]{1,0:T(8,128)(2,1)S(1)} %get-tuple-element.440.mine.refs_12_), channel_id=1, source_target_pairs={{0,8},{8,0},{1,9},{9,1},{2,10},{10,2},{3,11},{11,3},{4,12},{12,4},... | collective-permute-start | bytes 786440 | tf_op jit(solution)/shard_map/ppermute | solution.py:35
  283.9 19.1 %collective-permute-start.83 = (bf16[128,1024]{1,0:T(8,128)(2,1)}, bf16[128,1024]{1,0:T(8,128)(2,1)}, u32[]{:S(2)}, u32[]{:S(2)}) collective-permute-start(bf16[128,1024]{1,0:T(8,128)(2,1)} %collective-permute-done.82.mine.refs_14_), channel_id=1, source_target_pairs={{0,8},{8,0},{1,9},{9,1},{2,10},{10,2},{3,11},{11,3},{4,12},{12,4},... | collective-permute-start | bytes 786440 | tf_op jit(solution)/shard_map/ppermute | solution.py:35
  288.2 17.8 %collective-permute-start.81 = (bf16[128,1024]{1,0:T(8,128)(2,1)}, bf16[128,1024]{1,0:T(8,128)(2,1)}, u32[]{:S(2)}, u32[]{:S(2)}) collective-permute-start(bf16[128,1024]{1,0:T(8,128)(2,1)} %collective-permute-done.80.mine.refs_16_), channel_id=1, source_target_pairs={{0,8},{8,0},{1,9},{9,1},{2,10},{10,2},{3,11},{11,3},{4,12},{12,4},... | collective-permute-start | bytes 786440 | tf_op jit(solution)/shard_map/ppermute | solution.py:35
  290.8 48.2 %all-to-all-start.1 = ((bf16[16,64,1024]{2,1,0:T(8,128)(2,1)}), bf16[16,64,1024]{2,1,0:T(8,128)(2,1)}, u32[]{:S(2)}, u32[]{:S(2)}) async-start(bf16[16,64,1024]{2,1,0:T(8,128)(2,1)} %shard_map.342), calls=%async_computation.1 | async-start | bytes 4194304 | tf_op jit(solution)/shard_map/all_to_all | solution.py:407
  295.1 13.9 %collective-permute-start.79 = (bf16[128,1024]{1,0:T(8,128)(2,1)}, bf16[128,1024]{1,0:T(8,128)(2,1)S(1)}, u32[]{:S(2)}, u32[]{:S(2)}) collective-permute-start(bf16[128,1024]{1,0:T(8,128)(2,1)} %collective-permute-done.78.mine.refs_18_), channel_id=1, source_target_pairs={{0,8},{8,0},{1,9},{9,1},{2,10},{10,2},{3,11},{11,3},{4,12},{12,4},... | collective-permute-start | bytes 786440 | tf_op jit(solution)/shard_map/ppermute | solution.py:35
  312.5 16.7 %collective-permute-start.117 = (bf16[128,1024]{1,0:T(8,128)(2,1)}, bf16[128,1024]{1,0:T(8,128)(2,1)}, u32[]{:S(2)}, u32[]{:S(2)}) collective-permute-start(bf16[128,1024]{1,0:T(8,128)(2,1)} %get-tuple-element.454), channel_id=1, source_target_pairs={{0,0},{1,1},{2,2},{3,3},{4,8},{5,9},{6,10},{7,11},{8,4},{9,5},{10,... | collective-permute-start | bytes 786440 | tf_op jit(solution)/shard_map/ppermute | solution.py:45
  318.5 18.2 %collective-permute-start.91 = (bf16[128,1024]{1,0:T(8,128)(2,1)}, bf16[128,1024]{1,0:T(8,128)(2,1)}, u32[]{:S(2)}, u32[]{:S(2)}) collective-permute-start(bf16[128,1024]{1,0:T(8,128)(2,1)} %get-tuple-element.316), channel_id=1, source_target_pairs={{0,8},{8,0},{1,9},{9,1},{2,10},{10,2},{3,11},{11,3},{4,12},{12,4},... | collective-permute-start | bytes 786440 | tf_op jit(solution)/shard_map/ppermute | solution.py:35
  320.9 15.8 %collective-permute-start.90 = (bf16[128,1024]{1,0:T(8,128)(2,1)}, bf16[128,1024]{1,0:T(8,128)(2,1)}, u32[]{:S(2)}, u32[]{:S(2)}) collective-permute-start(bf16[128,1024]{1,0:T(8,128)(2,1)} %add_convert_fusion.8), channel_id=1, source_target_pairs={{0,1},{1,2},{2,3},{3,0},{4,5},{5,6},{6,7},{7,4},{8,9},{9,10},{10,1... | collective-permute-start | bytes 786440 | tf_op jit(solution)/shard_map/ppermute | solution.py:31
  348.2 13.3 %collective-permute-start.92 = (bf16[128,1024]{1,0:T(8,128)(2,1)S(1)}, bf16[128,1024]{1,0:T(8,128)(2,1)}, u32[]{:S(2)}, u32[]{:S(2)}) collective-permute-start(bf16[128,1024]{1,0:T(8,128)(2,1)S(1)} %get-tuple-element.432.mine.refs_12_), channel_id=1, source_target_pairs={{0,2},{1,3},{2,0},{3,1},{4,6},{5,7},{6,4},{7,5},{8,10},{9,11},{10,... | collective-permute-start | bytes 786440 | tf_op jit(solution)/shard_map/ppermute | solution.py:31
  355.9 17.3 %collective-permute-start.104 = (bf16[128,1024]{1,0:T(8,128)(2,1)S(1)}, bf16[128,1024]{1,0:T(8,128)(2,1)}, u32[]{:S(2)}, u32[]{:S(2)}) collective-permute-start(bf16[128,1024]{1,0:T(8,128)(2,1)S(1)} %get-tuple-element.432.mine.refs_12_), channel_id=1, source_target_pairs={{0,8},{8,0},{1,9},{9,1},{2,10},{10,2},{3,11},{11,3},{4,12},{12,4},... | collective-permute-start | bytes 786440 | tf_op jit(solution)/shard_map/ppermute | solution.py:35
  356.0 23.1 %collective-permute-start.97 = (bf16[128,1024]{1,0:T(8,128)(2,1)}, bf16[128,1024]{1,0:T(8,128)(2,1)}, u32[]{:S(2)}, u32[]{:S(2)}) collective-permute-start(bf16[128,1024]{1,0:T(8,128)(2,1)} %collective-permute-done.96.mine.refs_14_), channel_id=1, source_target_pairs={{0,8},{8,0},{1,9},{9,1},{2,10},{10,2},{3,11},{11,3},{4,12},{12,4},... | collective-permute-start | bytes 786440 | tf_op jit(solution)/shard_map/ppermute | solution.py:35
  361.5 20.2 %collective-permute-start.93 = (bf16[128,1024]{1,0:T(8,128)(2,1)}, bf16[128,1024]{1,0:T(8,128)(2,1)}, u32[]{:S(2)}, u32[]{:S(2)}) collective-permute-start(bf16[128,1024]{1,0:T(8,128)(2,1)} %collective-permute-done.92.mine.refs_18_), channel_id=1, source_target_pairs={{0,8},{8,0},{1,9},{9,1},{2,10},{10,2},{3,11},{11,3},{4,12},{12,4},... | collective-permute-start | bytes 786440 | tf_op jit(solution)/shard_map/ppermute | solution.py:35
  367.0 17.1 %collective-permute-start.102 = (bf16[128,1024]{1,0:T(8,128)(2,1)}, bf16[128,1024]{1,0:T(8,128)(2,1)}, u32[]{:S(2)}, u32[]{:S(2)}) collective-permute-start(bf16[128,1024]{1,0:T(8,128)(2,1)} %get-tuple-element.335), channel_id=1, source_target_pairs={{0,8},{8,0},{1,9},{9,1},{2,10},{10,2},{3,11},{11,3},{4,12},{12,4},... | collective-permute-start | bytes 786440 | tf_op jit(solution)/shard_map/ppermute | solution.py:35
  367.0 26.5 %all-to-all-start.2 = ((bf16[16,64,512]{2,1,0:T(8,128)(2,1)}), bf16[16,64,512]{2,1,0:T(8,128)(2,1)}, u32[]{:S(2)}, u32[]{:S(2)}) async-start(bf16[16,64,512]{2,1,0:T(8,128)(2,1)} %shard_map.351), calls=%async_computation.2 | async-start | bytes 2097152 | tf_op jit(solution)/shard_map/all_to_all | solution.py:407
  378.1 17.4 %collective-permute-start.105 = (bf16[128,1024]{1,0:T(8,128)(2,1)}, bf16[128,1024]{1,0:T(8,128)(2,1)}, u32[]{:S(2)}, u32[]{:S(2)}) collective-permute-start(bf16[128,1024]{1,0:T(8,128)(2,1)} %get-tuple-element.338), channel_id=1, source_target_pairs={{0,8},{8,0},{1,9},{9,1},{2,10},{10,2},{3,11},{11,3},{4,12},{12,4},... | collective-permute-start | bytes 786440 | tf_op jit(solution)/shard_map/ppermute | solution.py:35
  405.5 33.6 %collective-permute-start.119 = (bf16[64,1024]{1,0:T(8,128)(2,1)}, bf16[64,1024]{1,0:T(8,128)(2,1)}, u32[]{:S(2)}, u32[]{:S(2)}) collective-permute-start(bf16[64,1024]{1,0:T(8,128)(2,1)} %convert_reduce_fusion.1), channel_id=1, source_target_pairs={{0,0},{1,1},{2,2},{3,3},{4,8},{5,9},{6,10},{7,11},{8,4},{9,5},{10,... | collective-permute-start | bytes 393224 | tf_op jit(solution)/shard_map/ppermute | solution.py:45
  409.2 14.8 %collective-permute-start.107 = (bf16[128,1024]{1,0:T(8,128)(2,1)S(1)}, bf16[128,1024]{1,0:T(8,128)(2,1)S(1)}, u32[]{:S(2)}, u32[]{:S(2)}) collective-permute-start(bf16[128,1024]{1,0:T(8,128)(2,1)S(1)} %get-tuple-element.435.mine.refs_12_), channel_id=1, source_target_pairs={{0,2},{1,3},{2,0},{3,1},{4,6},{5,7},{6,4},{7,5},{8,10},{9,11},{10,... | collective-permute-start | bytes 786440 | tf_op jit(solution)/shard_map/ppermute | solution.py:31
  418.3 26.7 %collective-permute-start.106 = (bf16[128,1024]{1,0:T(8,128)(2,1)S(1)}, bf16[128,1024]{1,0:T(8,128)(2,1)S(1)}, u32[]{:S(2)}, u32[]{:S(2)}) collective-permute-start(bf16[128,1024]{1,0:T(8,128)(2,1)S(1)} %get-tuple-element.435.mine.refs_12_), channel_id=1, source_target_pairs={{0,8},{8,0},{1,9},{9,1},{2,10},{10,2},{3,11},{11,3},{4,12},{12,4},... | collective-permute-start | bytes 786440 | tf_op jit(solution)/shard_map/ppermute | solution.py:35
  431.5 19.7 %collective-permute-start.114 = (bf16[128,1024]{1,0:T(8,128)(2,1)S(1)}, bf16[128,1024]{1,0:T(8,128)(2,1)}, u32[]{:S(2)}, u32[]{:S(2)}) collective-permute-start(bf16[128,1024]{1,0:T(8,128)(2,1)S(1)} %collective-permute-done.113.mine.refs_16_), channel_id=1, source_target_pairs={{0,8},{8,0},{1,9},{9,1},{2,10},{10,2},{3,11},{11,3},{4,12},{12,4},... | collective-permute-start | bytes 786440 | tf_op jit(solution)/shard_map/ppermute | solution.py:35
  431.7 16.6 %collective-permute-start.116 = (bf16[128,1024]{1,0:T(8,128)(2,1)S(1)}, bf16[128,1024]{1,0:T(8,128)(2,1)}, u32[]{:S(2)}, u32[]{:S(2)}) collective-permute-start(bf16[128,1024]{1,0:T(8,128)(2,1)S(1)} %collective-permute-done.115.mine.refs_14_), channel_id=1, source_target_pairs={{0,8},{8,0},{1,9},{9,1},{2,10},{10,2},{3,11},{11,3},{4,12},{12,4},... | collective-permute-start | bytes 786440 | tf_op jit(solution)/shard_map/ppermute | solution.py:35
  432.8 54.8 %all-to-all-start.3 = ((bf16[16,80,1024]{2,1,0:T(8,128)(2,1)}), bf16[16,80,1024]{2,1,0:T(8,128)(2,1)}, u32[]{:S(2)}, u32[]{:S(2)}) async-start(bf16[16,80,1024]{2,1,0:T(8,128)(2,1)} %shard_map.357), calls=%async_computation.3 | async-start | bytes 5242880 | tf_op jit(solution)/shard_map/all_to_all | solution.py:407
  440.7 88.8 %collective-permute-start.134 = (bf16[64,512]{1,0:T(8,128)(2,1)}, bf16[64,512]{1,0:T(8,128)(2,1)}, u32[]{:S(2)}, u32[]{:S(2)}) collective-permute-start(bf16[64,512]{1,0:T(8,128)(2,1)} %convert_reduce_fusion.3), channel_id=1, source_target_pairs={{0,0},{1,1},{2,2},{3,3},{4,8},{5,9},{6,10},{7,11},{8,4},{9,5},{10,... | collective-permute-start | bytes 196616 | tf_op jit(solution)/shard_map/ppermute | solution.py:45
  475.8 54.5 %collective-permute-start.132 = (bf16[128,1024]{1,0:T(8,128)(2,1)S(1)}, bf16[128,1024]{1,0:T(8,128)(2,1)S(1)}, u32[]{:S(2)}, u32[]{:S(2)}) collective-permute-start(bf16[128,1024]{1,0:T(8,128)(2,1)S(1)} %add_convert_fusion), channel_id=1, source_target_pairs={{0,0},{1,1},{2,2},{3,3},{4,8},{5,9},{6,10},{7,11},{8,4},{9,5},{10,... | collective-permute-start | bytes 786440 | tf_op jit(solution)/shard_map/ppermute | solution.py:45
  493.5 14.9 %collective-permute-start.122 = (f32[12,128]{1,0:T(8,128)S(1)}, f32[12,128]{1,0:T(8,128)S(1)}, u32[]{:S(2)}, u32[]{:S(2)}) collective-permute-start(f32[12,128]{1,0:T(8,128)S(1)} %slice.395), channel_id=1, source_target_pairs={{0,3},{1,0},{2,1},{3,2},{4,7},{5,4},{6,5},{7,6},{8,11},{9,8},{10,9... | collective-permute-start | bytes 18440 | tf_op jit(solution)/shard_map/ppermute | solution.py:31
  493.5 15.0 %collective-permute-start.123 = (f32[12,128]{1,0:T(8,128)S(1)}, f32[12,128]{1,0:T(8,128)S(1)}, u32[]{:S(2)}, u32[]{:S(2)}) collective-permute-start(f32[12,128]{1,0:T(8,128)S(1)} %slice.395), channel_id=1, source_target_pairs={{0,2},{1,3},{2,0},{3,1},{4,6},{5,7},{6,4},{7,5},{8,10},{9,11},{10,... | collective-permute-start | bytes 18440 | tf_op jit(solution)/shard_map/ppermute | solution.py:31
  495.9 29.3 %all-to-all-start.4 = ((bf16[16,80,512]{2,1,0:T(8,128)(2,1)}), bf16[16,80,512]{2,1,0:T(8,128)(2,1)S(1)}, u32[]{:S(2)}, u32[]{:S(2)}) async-start(bf16[16,80,512]{2,1,0:T(8,128)(2,1)} %shard_map.365), calls=%async_computation.4 | async-start | bytes 2621440 | tf_op jit(solution)/shard_map/all_to_all | solution.py:486
  501.9 21.8 %collective-permute-start.118 = (bf16[64,1024]{1,0:T(8,128)(2,1)S(1)}, bf16[64,1024]{1,0:T(8,128)(2,1)S(1)}, u32[]{:S(2)}, u32[]{:S(2)}) collective-permute-start(bf16[64,1024]{1,0:T(8,128)(2,1)S(1)} %slice.452), channel_id=1, source_target_pairs={{0,0},{1,1},{2,2},{3,3},{4,8},{5,9},{6,10},{7,11},{8,4},{9,5},{10,... | collective-permute-start | bytes 393224 | tf_op jit(solution)/shard_map/ppermute | solution.py:45
  508.7 16.5 %collective-permute-start.120 = (f32[2,512]{1,0:T(2,128)S(1)}, f32[2,512]{1,0:T(2,128)S(1)}, u32[]{:S(2)}, u32[]{:S(2)}) collective-permute-start(f32[2,512]{1,0:T(2,128)S(1)} %pad_maximum_fusion.6), channel_id=1, source_target_pairs={{0,0},{1,1},{2,2},{3,3},{4,8},{5,9},{6,10},{7,11},{8,4},{9,5},{10,... | collective-permute-start | bytes 12296 | tf_op jit(solution)/shard_map/ppermute | solution.py:45
  (288 other events, 2514.6 us)
Sparse Core Ops, SparseCore 0:
  10.3 42.3 all-gather.3
  55.0 36.9 all-gather.5
  93.7 34.4 all-gather.7

commit v2 on v1

--- a/solution.py
+++ b/solution.py
@@ -183,7 +183,9 @@
     outs = [shaped(query.shape, BF16), shaped(key.shape, F32), shaped(key.shape, F32)]
     args = (*pair, out_mat, query, key, value, soft, key_sum, value_sum)
     flops = 8 * soft.shape[0] * query.shape[0] * key.size
-    return call(attend_back_body, args, outs, 2 * flops)
+    half = pl.BlockSpec((query.shape[0] // 2, pair[0].shape[1]), lambda *_: (0, 0))
+    specs = [half, half] + [whole(a) for a in args[2:]]
+    return call(attend_back_body, args, outs, 2 * flops, (1,), specs)
 
 
 def inputs_back_body(grad_query, grad_key, grad_value, mat, joined, sums, keep, send):
@@ -239,7 +241,7 @@
     args, specs, cols = [], [], 0
     for left, right in pairs:
         flat = [half for hop in HOPS for half in left[hop]]
-        rows, width = flat[0].shape
+        rows, width = right[0].shape[0] // 2, flat[0].shape[1]
         args += flat + [right[hop] for hop in HOPS]
         specs += [pl.BlockSpec((rows, tile), lambda i: (0, i))] * len(flat)
         specs += [whole(right[hop]) for hop in HOPS]
@@ -277,19 +279,17 @@
     return jnp.concatenate([chunks[hop] for hop in HOPS], axis=0)
 
 
-def sum_group(vectors, core, x):
+def sum_rows(chunks, start, count, core, x):
     ring = lax.axis_size("x")
-    slices = vectors.reshape(vectors.shape[0], 2, ring, -1)
-    slices = jnp.transpose(slices, (1, 2, 0, 3))
-    mine = lax.dynamic_index_in_dim(slices, core, 0, False)
-    send = lax.dynamic_index_in_dim(slices, 1 - core, 0, False)
-    both = mine + other_core(send)
-    kept = None
-    for hop in HOPS:
-        part = lax.dynamic_index_in_dim(both, lax.rem(x + ring - hop, ring), 0, False)
-        part = along_x(part, -hop) if hop else part
-        kept = part if kept is None else kept + part
-    return kept
+    table = [[chunks[hop][side][start : start + 2 * count] for hop in range(ring)] for side in (0, 1)]
+    table = jnp.stack([jnp.stack(side) for side in table]).astype(F32)
+    table = jnp.where(core == 0, table, table[::-1])
+    ordered = [
+        lax.dynamic_index_in_dim(table, lax.rem(x + ring - where, ring), 1, False)
+        for where in range(ring)
+    ]
+    total = jnp.sum(jnp.stack(ordered), axis=(0, 1))
+    return total[:count] + total[count:]
 
 
 def on_device(
@@ -445,15 +445,19 @@
         )
         attn_low = grad_first.astype(BF16)
         out_bias_term = jnp.sum(attn_low.astype(F32), axis=0)
-        attn_chunks = gather_pairs(attn_low)
-        row_sums.append(
-            jnp.stack([out_bias_term, down_bias_term, att_gain_term, att_shift_term, out_gain_term,
-                       out_shift_term])
+        own_sums = jnp.stack(
+            [out_bias_term, down_bias_term, att_gain_term, att_shift_term, out_gain_term,
+             out_shift_term]
         )
+        upper = own_sums.astype(BF16)
+        lower = (own_sums - upper.astype(F32)).astype(BF16)
+        blank = jnp.zeros((16 - 2 * upper.shape[0], upper.shape[1]), BF16)
+        block = tie(jnp.concatenate([attn_low, upper, lower, blank], axis=0))
+        attn_chunks = gather_pairs(block)
+        row_sums.append(sum_rows(attn_chunks, attn_low.shape[0], upper.shape[0], core, x))
         head_sums.append(up_bias_term)
         if not layer:
-            kept = sum_group(jnp.concatenate(row_sums), core, x)
-            small = jnp.concatenate(head_sums + [kept.reshape(-1)])
+            small = jnp.concatenate(head_sums + [item.reshape(-1) for item in row_sums])
             terms = weight_grads(ffn_pairs, owners, extra_rows(small, 2 * ffn_half))
             final = ARRIVAL[-1]
             attn_chunks[final], terms = tie((attn_chunks[final], terms))
@@ -488,15 +492,7 @@
     early_sums = joint[shard_rows:].reshape(-1)[: small.shape[0]]
 
     head_len = sum(item.shape[0] for item in head_sums)
-    piece = early_sums[head_len:].reshape(layers * 6, -1)
-    table = jnp.zeros((2, ring) + piece.shape, F32)
-    for hop in HOPS:
-        one = along_x(piece, hop) if hop else piece
-        where = lax.rem(x + ring - hop, ring)
-        table = lax.dynamic_update_slice(table, one[None, None], (core, where, 0, 0))
-    pair = lax.dynamic_slice_in_dim(table, core, 1, 0)
-    table = lax.dynamic_update_slice(table, other_core(pair), (1 - core, 0, 0, 0))
-    rows_out = jnp.transpose(table, (2, 0, 1, 3)).reshape(layers, 6, -1)[::-1]
+    rows_out = early_sums[head_len:].reshape(layers, 6, -1)[::-1]
 
     def cols(pieces, start, count, turn=False):
         chosen = [piece[:, start : start + count].astype(F32) for piece in pieces]

time: 559 us -> 559 us (level)
  the two profiles are of different devices: /device:TPU:37 before, /device:TPU:1 now
where the time goes in v2:
time: 559 us; the launch traced here: 548 us
  starting transfers between devices  240 us (43%)
  waiting for transfers between devices  94.6 us (17%)
  Pallas kernels  90.2 us (16%)
  local copies, waits for them, and re-layouts  60.1 us (11%)
  other arithmetic  44.5 us (8%)
  between operations  18.2 us (3%)
    ppermute x65, starting transfers between devices, other_core(): return lax.ppermute(value, 'c', [(0, 1), (1, 0)])  90.7 us
    pallas_call x52, Pallas kernels, call(): pl.pallas_call(body, grid=grid, in_specs=in_specs or [whole(a) for a in a...  90.2 us
    ppermute x48, waiting for transfers between devices, along_x(): lax.ppermute(value, 'x', [(i, (i + hop) % ring) for i in range(ring)])  73.2 us
    ppermute x48, starting transfers between devices, along_x(): lax.ppermute(value, 'x', [(i, (i + hop) % ring) for i in range(ring)])  62 us
    ppermute x15, starting transfers between devices, swap_core_z(): return lax.ppermute(value, ('c', 'zh', 'x'), pairs)  56.8 us
    unnamed x490, local copies, waits for them, and re-layouts  40.3 us
    all_to_all x3, starting transfers between devices, sum_owners(): lax.all_to_all(terms, OWNERS, 0, 0, tiled=True).astype(F32)  19.5 us
  transfers between devices with their start and end apart: 136, of which 29 were waited for; matrix products, arithmetic and copies ran while one was open for 11% of the time, Pallas kernels for 16%

profile of v2, /device:TPU:1, one launch (start us, length us, event | category | flops | bytes accessed | tf_op | source)
XLA Modules:
  0.0 547.7 jit_solution(10271170987511764916)
XLA Ops:
  13.5 6.9 %collective-permute-start = (bf16[128,1024]{1,0:T(8,128)(2,1)}, bf16[128,1024]{1,0:T(8,128)(2,1)S(1)}, u32[]{:S(2)}, u32[]{:S(2)}) collective-permute-start(bf16[128,1024]{1,0:T(8,128)(2,1)} %param.19), channel_id=1, source_target_pairs={{0,0},{1,1},{2,2},{3,3},{4,8},{5,9},{6,10},{7,11},{8,4},{9,5},{10,... | collective-permute-start | bytes 786440 | tf_op jit(solution)/shard_map/ppermute | solution.py:45
  23.1 5.2 collective-permute-start.9
  31.4 4.8 all-to-all-start
  46.6 4.7 collective-permute-start.5
  52.8 3.3 all-to-all-done
  84.1 3.7 collective-permute-done.14
  92.3 5.2 collective-permute-start.27
  102.9 6.8 %collective-permute-start.28 = (bf16[128,1024]{1,0:T(8,128)(2,1)S(1)}, bf16[128,1024]{1,0:T(8,128)(2,1)S(1)}, u32[]{:S(2)}, u32[]{:S(2)}) collective-permute-start(bf16[128,1024]{1,0:T(8,128)(2,1)S(1)} %collective-permute-done.27.mine.refs_4_), channel_id=1, source_target_pairs={{0,8},{8,0},{1,9},{9,1},{2,10},{10,2},{3,11},{11,3},{4,12},{12,4},... | collective-permute-start | bytes 786440 | tf_op jit(solution)/shard_map/ppermute | solution.py:35
  109.7 3.4 collective-permute-start.24
  132.3 4.3 collective-permute-done.22
  148.0 3.1 collective-permute-start.38
  179.2 6.4 %collective-permute-done.46 = bf16[128,1024]{1,0:T(8,128)(2,1)S(1)} collective-permute-done((bf16[128,1024]{1,0:T(8,128)(2,1)S(1)}, bf16[128,1024]{1,0:T(8,128)(2,1)S(1)}, u32[]{:S(2)}, u32[]{:S(2)}) %collective-permute-start.46) | collective-permute-done | bytes 262176 | tf_op jit(solution)/shard_map/ppermute | solution.py:31
  185.7 4.8 collective-permute-done.42
  197.9 8.0 %collective-permute-start.58 = (bf16[128,1024]{1,0:T(8,128)(2,1)S(1)}, bf16[128,1024]{1,0:T(8,128)(2,1)S(1)}, u32[]{:S(2)}, u32[]{:S(2)}) collective-permute-start(bf16[128,1024]{1,0:T(8,128)(2,1)S(1)} %collective-permute-done.57.mine.refs_4_), channel_id=1, source_target_pairs={{0,8},{8,0},{1,9},{9,1},{2,10},{10,2},{3,11},{11,3},{4,12},{12,4},... | collective-permute-start | bytes 786440 | tf_op jit(solution)/shard_map/ppermute | solution.py:35
  205.9 3.4 collective-permute-start.54
  219.4 3.0 collective-permute-start.63
  222.4 3.1 collective-permute-done.60
  225.6 4.6 collective-permute-done.52
  233.3 3.0 collective-permute-start.72
  240.2 8.2 %collective-permute-start.73 = (bf16[128,1024]{1,0:T(8,128)(2,1)S(1)}, bf16[128,1024]{1,0:T(8,128)(2,1)S(1)}, u32[]{:S(2)}, u32[]{:S(2)}) collective-permute-start(bf16[128,1024]{1,0:T(8,128)(2,1)S(1)} %collective-permute-done.72.mine.refs_16_), channel_id=1, source_target_pairs={{0,8},{8,0},{1,9},{9,1},{2,10},{10,2},{3,11},{11,3},{4,12},{12,4},... | collective-permute-start | bytes 786440 | tf_op jit(solution)/shard_map/ppermute | solution.py:35
  269.8 3.5 collective-permute-start.71
  275.2 6.7 %shard_map.342 = bf16[16,64,1024]{2,1,0:T(8,128)(2,1)} custom-call(bf16[128,1024]{1,0:T(8,128)(2,1)} %copy-done.7, bf16[128,1024]{1,0:T(8,128)(2,1)} %copy-done.27, bf16[128,1024]{1,0:T(8,128)(2,1)} %copy-done.26, bf16[128,1024]{1,0:T(8,128)(2,1)} %copy-done.30, bf16[128,1024]{1,0:T(8,128)(2,1)} %copy-done.25, bf16[128,1024]{1,0:T(8,128)(2,1)} %copy-done.29, ...), custom_call_target="tpu_custom_call" | custom-call | flops 4294967296 | bytes 8388608 | tf_op jit(solution)/shard_map/pallas_call | solution.py:87
  293.7 6.3 %all-to-all-start.1 = ((bf16[16,64,1024]{2,1,0:T(8,128)(2,1)}), bf16[16,64,1024]{2,1,0:T(8,128)(2,1)}, u32[]{:S(2)}, u32[]{:S(2)}) async-start(bf16[16,64,1024]{2,1,0:T(8,128)(2,1)} %shard_map.342), calls=%async_computation.1 | async-start | bytes 4194304 | tf_op jit(solution)/shard_map/all_to_all | solution.py:407
  300.0 3.2 collective-permute-start.81
  304.8 4.7 collective-permute-done.82.mine.refs_14_
  317.8 2.9 shard_map.344
  335.8 5.7 %shard_map.351 = bf16[16,64,512]{2,1,0:T(8,128)(2,1)} custom-call(bf16[128,1024]{1,0:T(8,128)(2,1)} %copy-done.8, bf16[128,1024]{1,0:T(8,128)(2,1)} %collective-permute-done.36.other.refs_1_, bf16[128,1024]{1,0:T(8,128)(2,1)} %collective-permute-done.37.mine.refs_2_, bf16[128,1024]{1,0:T(8,128)(2,1)} %collective-permute-done.38.other.refs_3_, ...), custom_call_target="tpu_custom_call" | custom-call | flops 2147483648 | bytes 6553600 | tf_op jit(solution)/shard_map/pallas_call | solution.py:87
  341.6 4.5 collective-permute-done.90
  353.4 3.3 collective-permute-start.100
  358.2 3.2 collective-permute-done.100.mine.refs_16_
  361.3 7.6 %collective-permute-start.101 = (bf16[128,1024]{1,0:T(8,128)(2,1)S(1)}, bf16[128,1024]{1,0:T(8,128)(2,1)S(1)}, u32[]{:S(2)}, u32[]{:S(2)}) collective-permute-start(bf16[128,1024]{1,0:T(8,128)(2,1)S(1)} %collective-permute-done.100.mine.refs_16_), channel_id=1, source_target_pairs={{0,8},{8,0},{1,9},{9,1},{2,10},{10,2},{3,11},{11,3},{4,12},{12,4},... | collective-permute-start | bytes 786440 | tf_op jit(solution)/shard_map/ppermute | solution.py:35
  369.0 3.6 collective-permute-start.97
  376.2 6.1 %all-to-all-start.2 = ((bf16[16,64,512]{2,1,0:T(8,128)(2,1)}), bf16[16,64,512]{2,1,0:T(8,128)(2,1)}, u32[]{:S(2)}, u32[]{:S(2)}) async-start(bf16[16,64,512]{2,1,0:T(8,128)(2,1)} %shard_map.351), calls=%async_computation.2 | async-start | bytes 2097152 | tf_op jit(solution)/shard_map/all_to_all | solution.py:407
  397.2 5.6 %collective-permute-start.115 = (bf16[64,1024]{1,0:T(8,128)(2,1)}, bf16[64,1024]{1,0:T(8,128)(2,1)}, u32[]{:S(2)}, u32[]{:S(2)}) collective-permute-start(bf16[64,1024]{1,0:T(8,128)(2,1)} %convert_reduce_fusion.1), channel_id=1, source_target_pairs={{0,0},{1,1},{2,2},{3,3},{4,8},{5,9},{6,10},{7,11},{8,4},{9,5},{10,... | collective-permute-start | bytes 393224 | tf_op jit(solution)/shard_map/ppermute | solution.py:45
  410.2 3.5 collective-permute-start.110
  416.6 3.4 collective-permute-done.110.mine.refs_16_
  420.0 7.2 %collective-permute-start.112 = (bf16[144,1024]{1,0:T(8,128)(2,1)S(1)}, bf16[144,1024]{1,0:T(8,128)(2,1)S(1)}, u32[]{:S(2)}, u32[]{:S(2)}) collective-permute-start(bf16[144,1024]{1,0:T(8,128)(2,1)S(1)} %collective-permute-done.110.mine.refs_16_), channel_id=1, source_target_pairs={{0,8},{8,0},{1,9},{9,1},{2,10},{10,2},{3,11},{11,3},{4,12},{12,4},... | collective-permute-start | bytes 884744 | tf_op jit(solution)/shard_map/ppermute | solution.py:35
  427.7 4.9 collective-permute-done.109.mine.refs_14_
  436.5 6.6 %shard_map.357 = bf16[16,80,1024]{2,1,0:T(8,128)(2,1)} custom-call(bf16[128,1024]{1,0:T(8,128)(2,1)} %copy-done.6, bf16[128,1024]{1,0:T(8,128)(2,1)} %copy-done.21, bf16[128,1024]{1,0:T(8,128)(2,1)} %copy-done.19, bf16[128,1024]{1,0:T(8,128)(2,1)} %copy-done.23, bf16[128,1024]{1,0:T(8,128)(2,1)} %copy-done.18, bf16[128,1024]{1,0:T(8,128)(2,1)} %copy-done.22, ...), custom_call_target="tpu_custom_call" | custom-call | flops 4294967296 | bytes 8945664 | tf_op jit(solution)/shard_map/pallas_call | solution.py:87
  443.2 7.1 %all-to-all-start.3 = ((bf16[16,80,1024]{2,1,0:T(8,128)(2,1)}), bf16[16,80,1024]{2,1,0:T(8,128)(2,1)}, u32[]{:S(2)}, u32[]{:S(2)}) async-start(bf16[16,80,1024]{2,1,0:T(8,128)(2,1)} %shard_map.357), calls=%async_computation.3 | async-start | bytes 5242880 | tf_op jit(solution)/shard_map/all_to_all | solution.py:407
  451.9 5.5 %collective-permute-start.126 = (bf16[64,512]{1,0:T(8,128)(2,1)}, bf16[64,512]{1,0:T(8,128)(2,1)}, u32[]{:S(2)}, u32[]{:S(2)}) collective-permute-start(bf16[64,512]{1,0:T(8,128)(2,1)} %convert_reduce_fusion.3), channel_id=1, source_target_pairs={{0,0},{1,1},{2,2},{3,3},{4,8},{5,9},{6,10},{7,11},{8,4},{9,5},{10,... | collective-permute-start | bytes 196616 | tf_op jit(solution)/shard_map/ppermute | solution.py:45
  474.1 5.8 %shard_map.365 = bf16[16,80,512]{2,1,0:T(8,128)(2,1)} custom-call(bf16[128,1024]{1,0:T(8,128)(2,1)} %copy-done.9, bf16[128,1024]{1,0:T(8,128)(2,1)} %copy-done.38, bf16[128,1024]{1,0:T(8,128)(2,1)} %copy-done.36, bf16[128,1024]{1,0:T(8,128)(2,1)} %copy-done.40, bf16[128,1024]{1,0:T(8,128)(2,1)} %copy-done.37, bf16[128,1024]{1,0:T(8,128)(2,1)} %copy-done.41, ...), custom_call_target="tpu_custom_call" | custom-call | flops 2147483648 | bytes 6832128 | tf_op jit(solution)/shard_map/pallas_call | solution.py:87
  479.9 5.4 collective-permute-done.122
  487.7 5.9 %all-to-all-done.3 = bf16[16,80,1024]{2,1,0:T(8,128)(2,1)} async-done(((bf16[16,80,1024]{2,1,0:T(8,128)(2,1)}), bf16[16,80,1024]{2,1,0:T(8,128)(2,1)}, u32[]{:S(2)}, u32[]{:S(2)}) %all-to-all-start.3) | async-done | bytes 2621472 | tf_op jit(solution)/shard_map/all_to_all | solution.py:407
  495.9 6.2 %all-to-all-start.4 = ((bf16[16,80,512]{2,1,0:T(8,128)(2,1)}), bf16[16,80,512]{2,1,0:T(8,128)(2,1)S(1)}, u32[]{:S(2)}, u32[]{:S(2)}) async-start(bf16[16,80,512]{2,1,0:T(8,128)(2,1)} %shard_map.365), calls=%async_computation.4 | async-start | bytes 2621440 | tf_op jit(solution)/shard_map/all_to_all | solution.py:490
  502.2 8.1 %collective-permute-start.114 = (bf16[64,1024]{1,0:T(8,128)(2,1)S(1)}, bf16[64,1024]{1,0:T(8,128)(2,1)S(1)}, u32[]{:S(2)}, u32[]{:S(2)}) collective-permute-start(bf16[64,1024]{1,0:T(8,128)(2,1)S(1)} %slice.568), channel_id=1, source_target_pairs={{0,0},{1,1},{2,2},{3,3},{4,8},{5,9},{6,10},{7,11},{8,4},{9,5},{10,... | collective-permute-start | bytes 393224 | tf_op jit(solution)/shard_map/ppermute | solution.py:45
  516.0 8.6 %collective-permute-done.114 = bf16[64,1024]{1,0:T(8,128)(2,1)S(1)} collective-permute-done((bf16[64,1024]{1,0:T(8,128)(2,1)S(1)}, bf16[64,1024]{1,0:T(8,128)(2,1)S(1)}, u32[]{:S(2)}, u32[]{:S(2)}) %collective-permute-start.114) | collective-permute-done | bytes 131104 | tf_op jit(solution)/shard_map/ppermute | solution.py:45
  530.5 4.5 collective-permute-start.125
  (962 shorter events, 284.0 us)
Async XLA Ops:
  7.2 68.9 %all-gather.4.cloned.1.call-start = ((), (), s32[]{:S(2)}) async-start(), calls=%async_computation.5 | async-start | bytes 2228224 | tf_op jit(solution)/shard_map/all_gather | solution.py:334
  9.7 118.7 %all-gather.6.cloned.1.call-start = ((), (), s32[]{:S(2)}) async-start(), calls=%async_computation.6 | async-start | bytes 1114112 | tf_op jit(solution)/shard_map/all_gather | solution.py:334
  13.5 138.5 %all-gather.8.cloned.1.call-start = ((), (), s32[]{:S(2)}) async-start(), calls=%async_computation.7 | async-start | bytes 2228224 | tf_op jit(solution)/shard_map/all_gather | solution.py:334
  13.5 22.7 %collective-permute-start = (bf16[128,1024]{1,0:T(8,128)(2,1)}, bf16[128,1024]{1,0:T(8,128)(2,1)S(1)}, u32[]{:S(2)}, u32[]{:S(2)}) collective-permute-start(bf16[128,1024]{1,0:T(8,128)(2,1)} %param.19), channel_id=1, source_target_pairs={{0,0},{1,1},{2,2},{3,3},{4,8},{5,9},{6,10},{7,11},{8,4},{9,5},{10,... | collective-permute-start | bytes 786440 | tf_op jit(solution)/shard_map/ppermute | solution.py:45
  23.1 23.4 %collective-permute-start.9 = (f32[2,768]{1,0:T(2,128)S(1)}, f32[2,768]{1,0:T(2,128)S(1)}, u32[]{:S(2)}, u32[]{:S(2)}) collective-permute-start(f32[2,768]{1,0:T(2,128)S(1)} %pad_maximum_fusion.4), channel_id=1, source_target_pairs={{0,0},{1,1},{2,2},{3,3},{4,8},{5,9},{6,10},{7,11},{8,4},{9,5},{10,... | collective-permute-start | bytes 18440 | tf_op jit(solution)/shard_map/ppermute | solution.py:45
  31.4 24.8 %all-to-all-start = ((bf16[16,64,512]{2,1,0:T(8,128)(2,1)}), bf16[16,64,512]{2,1,0:T(8,128)(2,1)}, u32[]{:S(2)}, u32[]{:S(2)}) async-start(bf16[16,64,512]{2,1,0:T(8,128)(2,1)} %broadcast_in_dim.10), calls=%async_computation | async-start | bytes 2097152 | tf_op jit(solution)/shard_map/all_to_all | solution.py:331
  39.7 18.9 %collective-permute-start.1 = (bf16[128,1024]{1,0:T(8,128)(2,1)S(1)}, bf16[128,1024]{1,0:T(8,128)(2,1)S(1)}, u32[]{:S(2)}, u32[]{:S(2)}) collective-permute-start(bf16[128,1024]{1,0:T(8,128)(2,1)S(1)} %collective-permute-done.mine.refs_0_), channel_id=1, source_target_pairs={{0,8},{8,0},{1,9},{9,1},{2,10},{10,2},{3,11},{11,3},{4,12},{12,4},... | collective-permute-start | bytes 786440 | tf_op jit(solution)/shard_map/ppermute | solution.py:35
  44.7 14.4 %collective-permute-start.3 = (bf16[128,1024]{1,0:T(8,128)(2,1)S(1)}, bf16[128,1024]{1,0:T(8,128)(2,1)S(1)}, u32[]{:S(2)}, u32[]{:S(2)}) collective-permute-start(bf16[128,1024]{1,0:T(8,128)(2,1)S(1)} %collective-permute-done.2.mine.refs_2_), channel_id=1, source_target_pairs={{0,8},{8,0},{1,9},{9,1},{2,10},{10,2},{3,11},{11,3},{4,12},{12,4},... | collective-permute-start | bytes 786440 | tf_op jit(solution)/shard_map/ppermute | solution.py:35
  68.0 16.0 %collective-permute-start.17 = (bf16[128,1024]{1,0:T(8,128)(2,1)S(1)}, bf16[128,1024]{1,0:T(8,128)(2,1)}, u32[]{:S(2)}, u32[]{:S(2)}) collective-permute-start(bf16[128,1024]{1,0:T(8,128)(2,1)S(1)} %get-tuple-element.235), channel_id=1, source_target_pairs={{0,8},{8,0},{1,9},{9,1},{2,10},{10,2},{3,11},{11,3},{4,12},{12,4},... | collective-permute-start | bytes 786440 | tf_op jit(solution)/shard_map/ppermute | solution.py:35
  76.1 37.2 %collective-permute-start.20 = (bf16[1024,1024]{1,0:T(8,128)(2,1)}, bf16[1024,1024]{1,0:T(8,128)(2,1)S(1)}, u32[]{:S(2)}, u32[]{:S(2)}) collective-permute-start(bf16[1024,1024]{1,0:T(8,128)(2,1)} %all-gather.4.cloned.1.call-done), channel_id=1, source_target_pairs={{0,0},{1,1},{2,2},{3,3},{4,8},{5,9},{6,10},{7,11},{8,4},{9,5},{10,... | collective-permute-start | bytes 6291464 | tf_op jit(solution)/shard_map/ppermute | solution.py:45
  97.6 15.5 %collective-permute-start.18 = (bf16[128,1024]{1,0:T(8,128)(2,1)S(1)}, bf16[128,1024]{1,0:T(8,128)(2,1)S(1)}, u32[]{:S(2)}, u32[]{:S(2)}) collective-permute-start(bf16[128,1024]{1,0:T(8,128)(2,1)S(1)} %fusion.7.mine.refs_0_), channel_id=1, source_target_pairs={{0,2},{1,3},{2,0},{3,1},{4,6},{5,7},{6,4},{7,5},{8,10},{9,11},{10,... | collective-permute-start | bytes 786440 | tf_op jit(solution)/shard_map/ppermute | solution.py:31
  98.8 17.3 %collective-permute-start.31 = (bf16[128,1024]{1,0:T(8,128)(2,1)S(1)}, bf16[128,1024]{1,0:T(8,128)(2,1)S(1)}, u32[]{:S(2)}, u32[]{:S(2)}) collective-permute-start(bf16[128,1024]{1,0:T(8,128)(2,1)S(1)} %fusion.7.mine.refs_0_), channel_id=1, source_target_pairs={{0,8},{8,0},{1,9},{9,1},{2,10},{10,2},{3,11},{11,3},{4,12},{12,4},... | collective-permute-start | bytes 786440 | tf_op jit(solution)/shard_map/ppermute | solution.py:35
  128.4 23.4 %collective-permute-start.35 = (bf16[1024,512]{1,0:T(8,128)(2,1)}, bf16[1024,512]{1,0:T(8,128)(2,1)S(1)}, u32[]{:S(2)}, u32[]{:S(2)}) collective-permute-start(bf16[1024,512]{1,0:T(8,128)(2,1)} %all-gather.6.cloned.1.call-done), channel_id=1, source_target_pairs={{0,0},{1,1},{2,2},{3,3},{4,8},{5,9},{6,10},{7,11},{8,4},{9,5},{10,... | collective-permute-start | bytes 3145736 | tf_op jit(solution)/shard_map/ppermute | solution.py:45
  152.0 57.3 %collective-permute-start.50 = (bf16[1024,1024]{1,0:T(8,128)(2,1)}, bf16[1024,1024]{1,0:T(8,128)(2,1)S(1)}, u32[]{:S(2)}, u32[]{:S(2)}) collective-permute-start(bf16[1024,1024]{1,0:T(8,128)(2,1)} %all-gather.8.cloned.1.call-done), channel_id=1, source_target_pairs={{0,0},{1,1},{2,2},{3,3},{4,8},{5,9},{6,10},{7,11},{8,4},{9,5},{10,... | collective-permute-start | bytes 6291464 | tf_op jit(solution)/shard_map/ppermute | solution.py:45
  193.7 17.4 %collective-permute-start.61 = (bf16[128,1024]{1,0:T(8,128)(2,1)S(1)}, bf16[128,1024]{1,0:T(8,128)(2,1)S(1)}, u32[]{:S(2)}, u32[]{:S(2)}) collective-permute-start(bf16[128,1024]{1,0:T(8,128)(2,1)S(1)} %fusion.9.mine.refs_0_), channel_id=1, source_target_pairs={{0,8},{8,0},{1,9},{9,1},{2,10},{10,2},{3,11},{11,3},{4,12},{12,4},... | collective-permute-start | bytes 786440 | tf_op jit(solution)/shard_map/ppermute | solution.py:35
  195.7 13.7 %collective-permute-start.48 = (bf16[128,1024]{1,0:T(8,128)(2,1)S(1)}, bf16[128,1024]{1,0:T(8,128)(2,1)S(1)}, u32[]{:S(2)}, u32[]{:S(2)}) collective-permute-start(bf16[128,1024]{1,0:T(8,128)(2,1)S(1)} %fusion.9.mine.refs_0_), channel_id=1, source_target_pairs={{0,2},{1,3},{2,0},{3,1},{4,6},{5,7},{6,4},{7,5},{8,10},{9,11},{10,... | collective-permute-start | bytes 786440 | tf_op jit(solution)/shard_map/ppermute | solution.py:31
  236.3 14.6 %collective-permute-start.68 = (bf16[128,1024]{1,0:T(8,128)(2,1)S(1)}, bf16[128,1024]{1,0:T(8,128)(2,1)}, u32[]{:S(2)}, u32[]{:S(2)}) collective-permute-start(bf16[128,1024]{1,0:T(8,128)(2,1)S(1)} %get-tuple-element.450.mine.refs_12_), channel_id=1, source_target_pairs={{0,1},{1,2},{2,3},{3,0},{4,5},{5,6},{6,7},{7,4},{8,9},{9,10},{10,1... | collective-permute-start | bytes 786440 | tf_op jit(solution)/shard_map/ppermute | solution.py:31
  236.3 16.4 %collective-permute-start.64 = (bf16[128,1024]{1,0:T(8,128)(2,1)S(1)}, bf16[128,1024]{1,0:T(8,128)(2,1)}, u32[]{:S(2)}, u32[]{:S(2)}) collective-permute-start(bf16[128,1024]{1,0:T(8,128)(2,1)S(1)} %get-tuple-element.450.mine.refs_12_), channel_id=1, source_target_pairs={{0,2},{1,3},{2,0},{3,1},{4,6},{5,7},{6,4},{7,5},{8,10},{9,11},{10,... | collective-permute-start | bytes 786440 | tf_op jit(solution)/shard_map/ppermute | solution.py:31
  252.7 13.8 %collective-permute-start.65 = (bf16[128,1024]{1,0:T(8,128)(2,1)}, bf16[128,1024]{1,0:T(8,128)(2,1)}, u32[]{:S(2)}, u32[]{:S(2)}) collective-permute-start(bf16[128,1024]{1,0:T(8,128)(2,1)} %collective-permute-done.64.mine.refs_18_), channel_id=1, source_target_pairs={{0,8},{8,0},{1,9},{9,1},{2,10},{10,2},{3,11},{11,3},{4,12},{12,4},... | collective-permute-start | bytes 786440 | tf_op jit(solution)/shard_map/ppermute | solution.py:35
  261.6 20.3 %collective-permute-start.77 = (bf16[128,1024]{1,0:T(8,128)(2,1)S(1)}, bf16[128,1024]{1,0:T(8,128)(2,1)S(1)}, u32[]{:S(2)}, u32[]{:S(2)}) collective-permute-start(bf16[128,1024]{1,0:T(8,128)(2,1)S(1)} %get-tuple-element.283), channel_id=1, source_target_pairs={{0,8},{8,0},{1,9},{9,1},{2,10},{10,2},{3,11},{11,3},{4,12},{12,4},... | collective-permute-start | bytes 786440 | tf_op jit(solution)/shard_map/ppermute | solution.py:35
  269.8 14.3 %collective-permute-start.71 = (bf16[128,1024]{1,0:T(8,128)(2,1)S(1)}, bf16[128,1024]{1,0:T(8,128)(2,1)S(1)}, u32[]{:S(2)}, u32[]{:S(2)}) collective-permute-start(bf16[128,1024]{1,0:T(8,128)(2,1)S(1)} %add_convert_fusion.12), channel_id=1, source_target_pairs={{0,3},{1,0},{2,1},{3,2},{4,7},{5,4},{6,5},{7,6},{8,11},{9,8},{10,9... | collective-permute-start | bytes 786440 | tf_op jit(solution)/shard_map/ppermute | solution.py:31
  291.1 20.0 %collective-permute-start.84 = (bf16[144,1024]{1,0:T(8,128)(2,1)S(1)}, bf16[144,1024]{1,0:T(8,128)(2,1)S(1)}, u32[]{:S(2)}, u32[]{:S(2)}) collective-permute-start(bf16[144,1024]{1,0:T(8,128)(2,1)S(1)} %maximum_maximum_fusion.mine.refs_12_), channel_id=1, source_target_pairs={{0,8},{8,0},{1,9},{9,1},{2,10},{10,2},{3,11},{11,3},{4,12},{12,4},... | collective-permute-start | bytes 884744 | tf_op jit(solution)/shard_map/ppermute | solution.py:35
  293.7 15.8 %collective-permute-start.82 = (bf16[144,1024]{1,0:T(8,128)(2,1)S(1)}, bf16[144,1024]{1,0:T(8,128)(2,1)}, u32[]{:S(2)}, u32[]{:S(2)}) collective-permute-start(bf16[144,1024]{1,0:T(8,128)(2,1)S(1)} %maximum_maximum_fusion.mine.refs_12_), channel_id=1, source_target_pairs={{0,1},{1,2},{2,3},{3,0},{4,5},{5,6},{6,7},{7,4},{8,9},{9,10},{10,1... | collective-permute-start | bytes 884744 | tf_op jit(solution)/shard_map/ppermute | solution.py:31
  293.7 54.5 %all-to-all-start.1 = ((bf16[16,64,1024]{2,1,0:T(8,128)(2,1)}), bf16[16,64,1024]{2,1,0:T(8,128)(2,1)}, u32[]{:S(2)}, u32[]{:S(2)}) async-start(bf16[16,64,1024]{2,1,0:T(8,128)(2,1)} %shard_map.342), calls=%async_computation.1 | async-start | bytes 4194304 | tf_op jit(solution)/shard_map/all_to_all | solution.py:407
  300.0 20.8 %collective-permute-start.81 = (bf16[144,1024]{1,0:T(8,128)(2,1)}, bf16[144,1024]{1,0:T(8,128)(2,1)S(1)}, u32[]{:S(2)}, u32[]{:S(2)}) collective-permute-start(bf16[144,1024]{1,0:T(8,128)(2,1)} %collective-permute-done.80.mine.refs_16_), channel_id=1, source_target_pairs={{0,8},{8,0},{1,9},{9,1},{2,10},{10,2},{3,11},{11,3},{4,12},{12,4},... | collective-permute-start | bytes 884744 | tf_op jit(solution)/shard_map/ppermute | solution.py:35
  304.0 19.8 %collective-permute-start.79 = (bf16[144,1024]{1,0:T(8,128)(2,1)}, bf16[144,1024]{1,0:T(8,128)(2,1)S(1)}, u32[]{:S(2)}, u32[]{:S(2)}) collective-permute-start(bf16[144,1024]{1,0:T(8,128)(2,1)} %collective-permute-done.78.mine.refs_18_), channel_id=1, source_target_pairs={{0,8},{8,0},{1,9},{9,1},{2,10},{10,2},{3,11},{11,3},{4,12},{12,4},... | collective-permute-start | bytes 884744 | tf_op jit(solution)/shard_map/ppermute | solution.py:35
  327.9 13.6 %collective-permute-start.91 = (bf16[128,1024]{1,0:T(8,128)(2,1)S(1)}, bf16[128,1024]{1,0:T(8,128)(2,1)S(1)}, u32[]{:S(2)}, u32[]{:S(2)}) collective-permute-start(bf16[128,1024]{1,0:T(8,128)(2,1)S(1)} %get-tuple-element.316), channel_id=1, source_target_pairs={{0,8},{8,0},{1,9},{9,1},{2,10},{10,2},{3,11},{11,3},{4,12},{12,4},... | collective-permute-start | bytes 786440 | tf_op jit(solution)/shard_map/ppermute | solution.py:35
  331.3 14.8 %collective-permute-start.90 = (bf16[128,1024]{1,0:T(8,128)(2,1)S(1)}, bf16[128,1024]{1,0:T(8,128)(2,1)S(1)}, u32[]{:S(2)}, u32[]{:S(2)}) collective-permute-start(bf16[128,1024]{1,0:T(8,128)(2,1)S(1)} %add_convert_fusion.8), channel_id=1, source_target_pairs={{0,1},{1,2},{2,3},{3,0},{4,5},{5,6},{6,7},{7,4},{8,9},{9,10},{10,1... | collective-permute-start | bytes 786440 | tf_op jit(solution)/shard_map/ppermute | solution.py:31
  332.4 13.7 %collective-permute-start.88 = (bf16[128,1024]{1,0:T(8,128)(2,1)}, bf16[128,1024]{1,0:T(8,128)(2,1)S(1)}, u32[]{:S(2)}, u32[]{:S(2)}) collective-permute-start(bf16[128,1024]{1,0:T(8,128)(2,1)} %add_convert_fusion.9), channel_id=1, source_target_pairs={{0,3},{1,0},{2,1},{3,2},{4,7},{5,4},{6,5},{7,6},{8,11},{9,8},{10,9... | collective-permute-start | bytes 786440 | tf_op jit(solution)/shard_map/ppermute | solution.py:31
  357.0 15.6 %collective-permute-start.92 = (bf16[128,1024]{1,0:T(8,128)(2,1)S(1)}, bf16[128,1024]{1,0:T(8,128)(2,1)}, u32[]{:S(2)}, u32[]{:S(2)}) collective-permute-start(bf16[128,1024]{1,0:T(8,128)(2,1)S(1)} %get-tuple-element.442.mine.refs_12_), channel_id=1, source_target_pairs={{0,2},{1,3},{2,0},{3,1},{4,6},{5,7},{6,4},{7,5},{8,10},{9,11},{10,... | collective-permute-start | bytes 786440 | tf_op jit(solution)/shard_map/ppermute | solution.py:31
  368.9 13.4 %collective-permute-start.104 = (bf16[128,1024]{1,0:T(8,128)(2,1)S(1)}, bf16[128,1024]{1,0:T(8,128)(2,1)}, u32[]{:S(2)}, u32[]{:S(2)}) collective-permute-start(bf16[128,1024]{1,0:T(8,128)(2,1)S(1)} %get-tuple-element.442.mine.refs_12_), channel_id=1, source_target_pairs={{0,8},{8,0},{1,9},{9,1},{2,10},{10,2},{3,11},{11,3},{4,12},{12,4},... | collective-permute-start | bytes 786440 | tf_op jit(solution)/shard_map/ppermute | solution.py:35
  369.0 17.1 %collective-permute-start.97 = (bf16[128,1024]{1,0:T(8,128)(2,1)}, bf16[128,1024]{1,0:T(8,128)(2,1)}, u32[]{:S(2)}, u32[]{:S(2)}) collective-permute-start(bf16[128,1024]{1,0:T(8,128)(2,1)} %collective-permute-done.96.mine.refs_14_), channel_id=1, source_target_pairs={{0,8},{8,0},{1,9},{9,1},{2,10},{10,2},{3,11},{11,3},{4,12},{12,4},... | collective-permute-start | bytes 786440 | tf_op jit(solution)/shard_map/ppermute | solution.py:35
  372.6 16.3 %collective-permute-start.93 = (bf16[128,1024]{1,0:T(8,128)(2,1)}, bf16[128,1024]{1,0:T(8,128)(2,1)}, u32[]{:S(2)}, u32[]{:S(2)}) collective-permute-start(bf16[128,1024]{1,0:T(8,128)(2,1)} %collective-permute-done.92.mine.refs_18_), channel_id=1, source_target_pairs={{0,8},{8,0},{1,9},{9,1},{2,10},{10,2},{3,11},{11,3},{4,12},{12,4},... | collective-permute-start | bytes 786440 | tf_op jit(solution)/shard_map/ppermute | solution.py:35
  375.7 15.5 %collective-permute-start.102 = (bf16[128,1024]{1,0:T(8,128)(2,1)}, bf16[128,1024]{1,0:T(8,128)(2,1)}, u32[]{:S(2)}, u32[]{:S(2)}) collective-permute-start(bf16[128,1024]{1,0:T(8,128)(2,1)} %get-tuple-element.335), channel_id=1, source_target_pairs={{0,8},{8,0},{1,9},{9,1},{2,10},{10,2},{3,11},{11,3},{4,12},{12,4},... | collective-permute-start | bytes 786440 | tf_op jit(solution)/shard_map/ppermute | solution.py:35
  376.2 26.6 %all-to-all-start.2 = ((bf16[16,64,512]{2,1,0:T(8,128)(2,1)}), bf16[16,64,512]{2,1,0:T(8,128)(2,1)}, u32[]{:S(2)}, u32[]{:S(2)}) async-start(bf16[16,64,512]{2,1,0:T(8,128)(2,1)} %shard_map.351), calls=%async_computation.2 | async-start | bytes 2097152 | tf_op jit(solution)/shard_map/all_to_all | solution.py:407
  385.8 19.0 %collective-permute-start.105 = (bf16[128,1024]{1,0:T(8,128)(2,1)}, bf16[128,1024]{1,0:T(8,128)(2,1)S(1)}, u32[]{:S(2)}, u32[]{:S(2)}) collective-permute-start(bf16[128,1024]{1,0:T(8,128)(2,1)} %get-tuple-element.338), channel_id=1, source_target_pairs={{0,8},{8,0},{1,9},{9,1},{2,10},{10,2},{3,11},{11,3},{4,12},{12,4},... | collective-permute-start | bytes 786440 | tf_op jit(solution)/shard_map/ppermute | solution.py:35
  393.1 13.6 %collective-permute-start.99 = (bf16[128,1024]{1,0:T(8,128)(2,1)}, bf16[128,1024]{1,0:T(8,128)(2,1)S(1)}, u32[]{:S(2)}, u32[]{:S(2)}) collective-permute-start(bf16[128,1024]{1,0:T(8,128)(2,1)} %add_convert_fusion.6), channel_id=1, source_target_pairs={{0,3},{1,0},{2,1},{3,2},{4,7},{5,4},{6,5},{7,6},{8,11},{9,8},{10,9... | collective-permute-start | bytes 786440 | tf_op jit(solution)/shard_map/ppermute | solution.py:31
  397.2 53.1 %collective-permute-start.115 = (bf16[64,1024]{1,0:T(8,128)(2,1)}, bf16[64,1024]{1,0:T(8,128)(2,1)}, u32[]{:S(2)}, u32[]{:S(2)}) collective-permute-start(bf16[64,1024]{1,0:T(8,128)(2,1)} %convert_reduce_fusion.1), channel_id=1, source_target_pairs={{0,0},{1,1},{2,2},{3,3},{4,8},{5,9},{6,10},{7,11},{8,4},{9,5},{10,... | collective-permute-start | bytes 393224 | tf_op jit(solution)/shard_map/ppermute | solution.py:45
  414.3 19.0 %collective-permute-start.106 = (bf16[144,1024]{1,0:T(8,128)(2,1)S(1)}, bf16[144,1024]{1,0:T(8,128)(2,1)S(1)}, u32[]{:S(2)}, u32[]{:S(2)}) collective-permute-start(bf16[144,1024]{1,0:T(8,128)(2,1)S(1)} %maximum_maximum_fusion.1.mine.refs_12_), channel_id=1, source_target_pairs={{0,8},{8,0},{1,9},{9,1},{2,10},{10,2},{3,11},{11,3},{4,12},{12,4},... | collective-permute-start | bytes 884744 | tf_op jit(solution)/shard_map/ppermute | solution.py:35
  416.2 16.3 %collective-permute-start.109 = (bf16[144,1024]{1,0:T(8,128)(2,1)S(1)}, bf16[144,1024]{1,0:T(8,128)(2,1)S(1)}, u32[]{:S(2)}, u32[]{:S(2)}) collective-permute-start(bf16[144,1024]{1,0:T(8,128)(2,1)S(1)} %maximum_maximum_fusion.1.mine.refs_12_), channel_id=1, source_target_pairs={{0,1},{1,2},{2,3},{3,0},{4,5},{5,6},{6,7},{7,4},{8,9},{9,10},{10,1... | collective-permute-start | bytes 884744 | tf_op jit(solution)/shard_map/ppermute | solution.py:31
  443.2 50.5 %all-to-all-start.3 = ((bf16[16,80,1024]{2,1,0:T(8,128)(2,1)}), bf16[16,80,1024]{2,1,0:T(8,128)(2,1)}, u32[]{:S(2)}, u32[]{:S(2)}) async-start(bf16[16,80,1024]{2,1,0:T(8,128)(2,1)} %shard_map.357), calls=%async_computation.3 | async-start | bytes 5242880 | tf_op jit(solution)/shard_map/all_to_all | solution.py:407
  451.9 77.0 %collective-permute-start.126 = (bf16[64,512]{1,0:T(8,128)(2,1)}, bf16[64,512]{1,0:T(8,128)(2,1)}, u32[]{:S(2)}, u32[]{:S(2)}) collective-permute-start(bf16[64,512]{1,0:T(8,128)(2,1)} %convert_reduce_fusion.3), channel_id=1, source_target_pairs={{0,0},{1,1},{2,2},{3,3},{4,8},{5,9},{6,10},{7,11},{8,4},{9,5},{10,... | collective-permute-start | bytes 196616 | tf_op jit(solution)/shard_map/ppermute | solution.py:45
  470.4 14.9 %collective-permute-start.122 = (bf16[128,1024]{1,0:T(8,128)(2,1)S(1)}, bf16[128,1024]{1,0:T(8,128)(2,1)S(1)}, u32[]{:S(2)}, u32[]{:S(2)}) collective-permute-start(bf16[128,1024]{1,0:T(8,128)(2,1)S(1)} %add_convert_fusion.1), channel_id=1, source_target_pairs={{0,1},{1,2},{2,3},{3,0},{4,5},{5,6},{6,7},{7,4},{8,9},{9,10},{10,1... | collective-permute-start | bytes 786440 | tf_op jit(solution)/shard_map/ppermute | solution.py:31
  470.5 14.7 %collective-permute-start.120 = (bf16[128,1024]{1,0:T(8,128)(2,1)S(1)}, bf16[128,1024]{1,0:T(8,128)(2,1)S(1)}, u32[]{:S(2)}, u32[]{:S(2)}) collective-permute-start(bf16[128,1024]{1,0:T(8,128)(2,1)S(1)} %add_convert_fusion.2), channel_id=1, source_target_pairs={{0,3},{1,0},{2,1},{3,2},{4,7},{5,4},{6,5},{7,6},{8,11},{9,8},{10,9... | collective-permute-start | bytes 786440 | tf_op jit(solution)/shard_map/ppermute | solution.py:31
  485.5 44.2 %collective-permute-start.124 = (bf16[128,1024]{1,0:T(8,128)(2,1)S(1)}, bf16[128,1024]{1,0:T(8,128)(2,1)S(1)}, u32[]{:S(2)}, u32[]{:S(2)}) collective-permute-start(bf16[128,1024]{1,0:T(8,128)(2,1)S(1)} %add_convert_fusion), channel_id=1, source_target_pairs={{0,0},{1,1},{2,2},{3,3},{4,8},{5,9},{6,10},{7,11},{8,4},{9,5},{10,... | collective-permute-start | bytes 786440 | tf_op jit(solution)/shard_map/ppermute | solution.py:45
  495.9 30.1 %all-to-all-start.4 = ((bf16[16,80,512]{2,1,0:T(8,128)(2,1)}), bf16[16,80,512]{2,1,0:T(8,128)(2,1)S(1)}, u32[]{:S(2)}, u32[]{:S(2)}) async-start(bf16[16,80,512]{2,1,0:T(8,128)(2,1)} %shard_map.365), calls=%async_computation.4 | async-start | bytes 2621440 | tf_op jit(solution)/shard_map/all_to_all | solution.py:490
  502.2 22.3 %collective-permute-start.114 = (bf16[64,1024]{1,0:T(8,128)(2,1)S(1)}, bf16[64,1024]{1,0:T(8,128)(2,1)S(1)}, u32[]{:S(2)}, u32[]{:S(2)}) collective-permute-start(bf16[64,1024]{1,0:T(8,128)(2,1)S(1)} %slice.568), channel_id=1, source_target_pairs={{0,0},{1,1},{2,2},{3,3},{4,8},{5,9},{6,10},{7,11},{8,4},{9,5},{10,... | collective-permute-start | bytes 393224 | tf_op jit(solution)/shard_map/ppermute | solution.py:45
  510.3 15.7 %collective-permute-start.116 = (f32[2,512]{1,0:T(2,128)S(1)}, f32[2,512]{1,0:T(2,128)S(1)}, u32[]{:S(2)}, u32[]{:S(2)}) collective-permute-start(f32[2,512]{1,0:T(2,128)S(1)} %pad_maximum_fusion.6), channel_id=1, source_target_pairs={{0,0},{1,1},{2,2},{3,3},{4,8},{5,9},{6,10},{7,11},{8,4},{9,5},{10,... | collective-permute-start | bytes 12296 | tf_op jit(solution)/shard_map/ppermute | solution.py:45
  (318 other events, 3047.0 us)
Sparse Core Ops, SparseCore 0:
  10.3 43.4 all-gather.3
  56.0 37.5 all-gather.5
  95.3 34.2 all-gather.7

commit v3 on v2

--- a/solution.py
+++ b/solution.py
@@ -434,12 +434,6 @@
         grad_mid = grad_second + scatter_pairs(parts)
         up_bias_term = sum(up_sums)
         ffn_pairs = [(mids, grad_pre), (branch, activated)]
-        if layer:
-            grad_mid, terms = tie((grad_mid, weight_grads(ffn_pairs, owners)))
-            found = sum_owners(terms)
-        if pending is not None:
-            grad_mid, pending = tie((grad_mid, pending))
-            attn_grads[layer + 1] = swap_core_z(pending.astype(BF16))
         grad_first, att_gain_term, att_shift_term = norm_back(
             grad_mid, mid_unit, mid_scale, attention_gain[layer]
         )
@@ -460,7 +454,10 @@
             small = jnp.concatenate(head_sums + [item.reshape(-1) for item in row_sums])
             terms = weight_grads(ffn_pairs, owners, extra_rows(small, 2 * ffn_half))
             final = ARRIVAL[-1]
-            attn_chunks[final], terms = tie((attn_chunks[final], terms))
+            attn_chunks[final], terms, pending = tie((attn_chunks[final], terms, pending))
+            pending = swap_core_z(pending.astype(BF16))
+            ffn_grads[1] = pending[:, : 2 * ffn_half]
+            attn_grads[1] = pending[:, 2 * ffn_half :]
             joint = sum_owners(terms)
         grad_q = {}
         grad_k, grad_v = jnp.zeros(keys.shape, F32), jnp.zeros(keys.shape, F32)
@@ -480,9 +477,8 @@
         attn_pairs = [(inputs, grad_qkv), (attn_chunks, attended)]
         if layer:
             head_sums.append(pair_sums)
-            terms = weight_grads(attn_pairs, owners)
-            grad_rows, terms, found = tie((grad_rows, terms, found))
-            ffn_grads[layer] = swap_core_z(found.astype(BF16))
+            terms = weight_grads(ffn_pairs + attn_pairs, owners)
+            grad_rows, terms = tie((grad_rows, terms))
             pending = sum_owners(terms)
         else:
             terms = weight_grads(attn_pairs, owners, extra_rows(pair_sums, attn_cols))

time: 559 us -> 548 us (0.980)
  the two profiles are of different devices: /device:TPU:1 before, /device:TPU:3 now
where the time goes in v3:
time: 548 us; the launch traced here: 537 us
  starting transfers between devices  203 us (37%)
  waiting for transfers between devices  129 us (24%)
  Pallas kernels  80.2 us (15%)
  local copies, waits for them, and re-layouts  60.9 us (11%)
  other arithmetic  46 us (8%)
  between operations  17.9 us (3%)
    ppermute x48, waiting for transfers between devices, along_x(): lax.ppermute(value, 'x', [(i, (i + hop) % ring) for i in range(ring)])  99 us
    pallas_call x51, Pallas kernels, call(): pl.pallas_call(body, grid=grid, in_specs=in_specs or [whole(a) for a in a...  80.2 us
    ppermute x48, starting transfers between devices, along_x(): lax.ppermute(value, 'x', [(i, (i + hop) % ring) for i in range(ring)])  65.2 us
    ppermute x14, starting transfers between devices, swap_core_z(): return lax.ppermute(value, ('c', 'zh', 'x'), pairs)  55.7 us
    ppermute x65, starting transfers between devices, other_core(): return lax.ppermute(value, 'c', [(0, 1), (1, 0)])  54.3 us
    unnamed x448, local copies, waits for them, and re-layouts  38.1 us
    ppermute x14, waiting for transfers between devices, swap_core_z(): return lax.ppermute(value, ('c', 'zh', 'x'), pairs)  18.1 us
    all_to_all x2, starting transfers between devices, sum_owners(): lax.all_to_all(terms, OWNERS, 0, 0, tiled=True).astype(F32)  15.7 us
  transfers between devices with their start and end apart: 134, of which 36 were waited for; matrix products, arithmetic and copies ran while one was open for 11% of the time, Pallas kernels for 14%

profile of v3, /device:TPU:3, one launch (start us, length us, event | category | flops | bytes accessed | tf_op | source)
XLA Modules:
  0.0 537.1 jit_solution(1814288215453826562)
XLA Ops:
  15.6 5.4 %collective-permute-start.9 = (f32[2,768]{1,0:T(2,128)S(1)}, f32[2,768]{1,0:T(2,128)S(1)}, u32[]{:S(2)}, u32[]{:S(2)}) collective-permute-start(f32[2,768]{1,0:T(2,128)S(1)} %pad_maximum_fusion.4), channel_id=1, source_target_pairs={{0,0},{1,1},{2,2},{3,3},{4,8},{5,9},{6,10},{7,11},{8,4},{9,5},{10,... | collective-permute-start | bytes 18440 | tf_op jit(solution)/shard_map/ppermute | solution.py:45
  23.0 5.1 collective-permute-start
  31.3 4.7 all-to-all-start
  47.4 3.4 collective-permute-done.6.mine.refs_6_
  52.4 2.8 all-to-all-done
  79.1 2.8 collective-permute-start.20
  88.4 4.3 collective-permute-done.14
  99.8 4.1 collective-permute-done.18.mine.refs_6_
  126.0 4.4 collective-permute-start.35
  130.5 5.6 %collective-permute-done.26 = bf16[128,1024]{1,0:T(8,128)(2,1)} collective-permute-done((bf16[128,1024]{1,0:T(8,128)(2,1)}, bf16[128,1024]{1,0:T(8,128)(2,1)}, u32[]{:S(2)}, u32[]{:S(2)}) %collective-permute-start.26) | collective-permute-done | bytes 262176 | tf_op jit(solution)/shard_map/ppermute | solution.py:31
  142.4 3.6 collective-permute-done.37.mine.refs_26_
  174.4 3.5 collective-permute-start.42
  181.3 3.3 collective-permute-done.42
  184.6 5.8 %collective-permute-done.44 = bf16[128,1024]{1,0:T(8,128)(2,1)S(1)} collective-permute-done((bf16[128,1024]{1,0:T(8,128)(2,1)S(1)}, bf16[128,1024]{1,0:T(8,128)(2,1)S(1)}, u32[]{:S(2)}, u32[]{:S(2)}) %collective-permute-start.44) | collective-permute-done | bytes 262176 | tf_op jit(solution)/shard_map/ppermute | solution.py:31
  198.2 3.2 collective-permute-done.48.mine.refs_6_
  201.4 2.8 collective-permute-start.49
  204.3 3.3 collective-permute-done.53.mine.refs_2_
  219.6 5.9 %collective-permute-start.63 = (bf16[128,1024]{1,0:T(8,128)(2,1)S(1)}, bf16[128,1024]{1,0:T(8,128)(2,1)S(1)}, u32[]{:S(2)}, u32[]{:S(2)}) collective-permute-start(bf16[128,1024]{1,0:T(8,128)(2,1)S(1)} %copy-done.208), channel_id=1, source_target_pairs={{0,0},{1,1},{2,2},{3,3},{4,8},{5,9},{6,10},{7,11},{8,4},{9,5},{10,... | collective-permute-start | bytes 786440 | tf_op jit(solution)/shard_map/ppermute | solution.py:45
  225.6 5.1 collective-permute-done.56
  236.6 5.0 collective-permute-done.64.mine.refs_18_
  243.9 3.3 collective-permute-done.68.mine.refs_14_
  250.2 4.8 collective-permute-start.113
  269.2 6.4 %collective-permute-done.71 = bf16[128,1024]{1,0:T(8,128)(2,1)} collective-permute-done((bf16[128,1024]{1,0:T(8,128)(2,1)}, bf16[128,1024]{1,0:T(8,128)(2,1)}, u32[]{:S(2)}, u32[]{:S(2)}) %collective-permute-start.71) | collective-permute-done | bytes 262176 | tf_op jit(solution)/shard_map/ppermute | solution.py:31
  292.4 3.9 collective-permute-done.78.mine.refs_42_
  306.5 2.9 shard_map.344
  316.4 9.0 %shard_map.350 = bf16[16,64,1536]{2,1,0:T(8,128)(2,1)} custom-call(bf16[128,1024]{1,0:T(8,128)(2,1)} %copy-done.4, bf16[128,1024]{1,0:T(8,128)(2,1)} %copy-done.28, bf16[128,1024]{1,0:T(8,128)(2,1)} %copy-done.26, bf16[128,1024]{1,0:T(8,128)(2,1)} %copy-done.30, bf16[128,1024]{1,0:T(8,128)(2,1)} %copy-done.27, bf16[128,1024]{1,0:T(8,128)(2,1)} %copy-done.31, ...), custom_call_target="tpu_custom_call" | custom-call | flops 6442450944 | bytes 14942208 | tf_op jit(solution)/shard_map/pallas_call | solution.py:87
  326.5 4.0 collective-permute-start.86
  331.5 3.1 collective-permute-start.88
  337.4 5.5 %collective-permute-done.88 = bf16[128,1024]{1,0:T(8,128)(2,1)S(1)} collective-permute-done((bf16[128,1024]{1,0:T(8,128)(2,1)S(1)}, bf16[128,1024]{1,0:T(8,128)(2,1)S(1)}, u32[]{:S(2)}, u32[]{:S(2)}) %collective-permute-start.88) | collective-permute-done | bytes 262176 | tf_op jit(solution)/shard_map/ppermute | solution.py:31
  352.4 3.2 collective-permute-done.92.mine.refs_18_
  355.6 4.1 collective-permute-start.93
  359.9 3.0 collective-permute-done.96.mine.refs_14_
  374.4 6.2 %all-to-all-start.1 = ((bf16[16,64,1536]{2,1,0:T(8,128)(2,1)}), bf16[16,64,1536]{2,1,0:T(8,128)(2,1)}, u32[]{:S(2)}, u32[]{:S(2)}) async-start(bf16[16,64,1536]{2,1,0:T(8,128)(2,1)} %shard_map.350), calls=%async_computation.1 | async-start | bytes 6291456 | tf_op jit(solution)/shard_map/all_to_all | solution.py:407
  380.7 5.1 collective-permute-done.99
  398.6 5.7 %collective-permute-done.107.mine.refs_18_ = bf16[144,1024]{1,0:T(8,128)(2,1)S(1)} collective-permute-done((bf16[144,1024]{1,0:T(8,128)(2,1)S(1)}, bf16[144,1024]{1,0:T(8,128)(2,1)S(1)}, u32[]{:S(2)}, u32[]{:S(2)}) %collective-permute-start.107) | collective-permute-done | bytes 294944 | tf_op jit(solution)/shard_map/ppermute | solution.py:31
  410.0 6.6 %shard_map.356 = bf16[16,80,1024]{2,1,0:T(8,128)(2,1)} custom-call(bf16[128,1024]{1,0:T(8,128)(2,1)} %copy-done.3, bf16[128,1024]{1,0:T(8,128)(2,1)} %copy-done.21, bf16[128,1024]{1,0:T(8,128)(2,1)} %copy-done.19, bf16[128,1024]{1,0:T(8,128)(2,1)} %copy-done.23, bf16[128,1024]{1,0:T(8,128)(2,1)} %copy-done.20, bf16[128,1024]{1,0:T(8,128)(2,1)} %copy-done.24, ...), custom_call_target="tpu_custom_call" | custom-call | flops 4294967296 | bytes 8945664 | tf_op jit(solution)/shard_map/pallas_call | solution.py:87
  416.6 9.1 %all-to-all-done.1 = bf16[16,64,1536]{2,1,0:T(8,128)(2,1)} async-done(((bf16[16,64,1536]{2,1,0:T(8,128)(2,1)}), bf16[16,64,1536]{2,1,0:T(8,128)(2,1)}, u32[]{:S(2)}, u32[]{:S(2)}) %all-to-all-start.1) | async-done | bytes 3145760 | tf_op jit(solution)/shard_map/all_to_all | solution.py:407
  425.7 3.1 convert_reduce_fusion
  428.8 9.5 %all-to-all-start.2 = ((bf16[16,80,1024]{2,1,0:T(8,128)(2,1)}), bf16[16,80,1024]{2,1,0:T(8,128)(2,1)}, u32[]{:S(2)}, u32[]{:S(2)}) async-start(bf16[16,80,1024]{2,1,0:T(8,128)(2,1)} %shard_map.356), calls=%async_computation.2 | async-start | bytes 5242880 | tf_op jit(solution)/shard_map/all_to_all | solution.py:407
  447.7 3.5 collective-permute-start.117
  456.7 5.4 %collective-permute-start.115 = (bf16[64,1536]{1,0:T(8,128)(2,1)}, bf16[64,1536]{1,0:T(8,128)(2,1)S(1)}, u32[]{:S(2)}, u32[]{:S(2)}) collective-permute-start(bf16[64,1536]{1,0:T(8,128)(2,1)} %convert_reduce_fusion), channel_id=1, source_target_pairs={{0,0},{1,1},{2,2},{3,3},{4,8},{5,9},{6,10},{7,11},{8,4},{9,5},{10,... | collective-permute-start | bytes 589832 | tf_op jit(solution)/shard_map/ppermute | solution.py:45
  467.8 5.8 %shard_map.364 = bf16[16,80,512]{2,1,0:T(8,128)(2,1)} custom-call(bf16[128,1024]{1,0:T(8,128)(2,1)} %copy-done.6, bf16[128,1024]{1,0:T(8,128)(2,1)} %copy-done.38, bf16[128,1024]{1,0:T(8,128)(2,1)} %copy-done.36, bf16[128,1024]{1,0:T(8,128)(2,1)} %copy-done.40, bf16[128,1024]{1,0:T(8,128)(2,1)} %copy-done.37, bf16[128,1024]{1,0:T(8,128)(2,1)} %copy-done.41, ...), custom_call_target="tpu_custom_call" | custom-call | flops 2147483648 | bytes 6832128 | tf_op jit(solution)/shard_map/pallas_call | solution.py:87
  473.6 4.0 collective-permute-done.115
  484.0 7.0 %all-to-all-start.3 = ((bf16[16,80,512]{2,1,0:T(8,128)(2,1)}), bf16[16,80,512]{2,1,0:T(8,128)(2,1)S(1)}, u32[]{:S(2)}, u32[]{:S(2)}) async-start(bf16[16,80,512]{2,1,0:T(8,128)(2,1)} %shard_map.364), calls=%async_computation.3 | async-start | bytes 2621440 | tf_op jit(solution)/shard_map/all_to_all | solution.py:486
  491.1 6.5 %collective-permute-start.116 = (f32[2,512]{1,0:T(2,128)S(1)}, f32[2,512]{1,0:T(2,128)S(1)}, u32[]{:S(2)}, u32[]{:S(2)}) collective-permute-start(f32[2,512]{1,0:T(2,128)S(1)} %pad_maximum_fusion.6), channel_id=1, source_target_pairs={{0,0},{1,1},{2,2},{3,3},{4,8},{5,9},{6,10},{7,11},{8,4},{9,5},{10,... | collective-permute-start | bytes 12296 | tf_op jit(solution)/shard_map/ppermute | solution.py:45
  503.2 10.6 %collective-permute-done.114 = bf16[64,1024]{1,0:T(8,128)(2,1)S(1)} collective-permute-done((bf16[64,1024]{1,0:T(8,128)(2,1)S(1)}, bf16[64,1024]{1,0:T(8,128)(2,1)S(1)}, u32[]{:S(2)}, u32[]{:S(2)}) %collective-permute-start.114) | collective-permute-done | bytes 131104 | tf_op jit(solution)/shard_map/ppermute | solution.py:45
  515.5 2.7 collective-permute-start.126
  519.8 4.4 collective-permute-start.125
  (912 shorter events, 286.4 us)
Async XLA Ops:
  7.2 71.9 %all-gather.4.cloned.1.call-start = ((), (), s32[]{:S(2)}) async-start(), calls=%async_computation.4 | async-start | bytes 2228224 | tf_op jit(solution)/shard_map/all_gather | solution.py:334
  9.7 116.3 %all-gather.6.cloned.1.call-start = ((), (), s32[]{:S(2)}) async-start(), calls=%async_computation.5 | async-start | bytes 1114112 | tf_op jit(solution)/shard_map/all_gather | solution.py:334
  13.5 136.5 %all-gather.8.cloned.1.call-start = ((), (), s32[]{:S(2)}) async-start(), calls=%async_computation.6 | async-start | bytes 2228224 | tf_op jit(solution)/shard_map/all_gather | solution.py:334
  14.2 15.9 %collective-permute-start.10 = (f32[1024]{0:T(1024)S(1)}, f32[1024]{0:T(1024)S(1)}, u32[]{:S(2)}, u32[]{:S(2)}) collective-permute-start(f32[1024]{0:T(1024)S(1)} %add_convert_fusion.26), channel_id=1, source_target_pairs={{0,8},{8,0},{1,9},{9,1},{2,10},{10,2},{3,11},{11,3},{4,12},{12,4},... | collective-permute-start | bytes 12296 | tf_op jit(solution)/shard_map/ppermute | solution.py:35
  15.6 29.3 %collective-permute-start.9 = (f32[2,768]{1,0:T(2,128)S(1)}, f32[2,768]{1,0:T(2,128)S(1)}, u32[]{:S(2)}, u32[]{:S(2)}) collective-permute-start(f32[2,768]{1,0:T(2,128)S(1)} %pad_maximum_fusion.4), channel_id=1, source_target_pairs={{0,0},{1,1},{2,2},{3,3},{4,8},{5,9},{6,10},{7,11},{8,4},{9,5},{10,... | collective-permute-start | bytes 18440 | tf_op jit(solution)/shard_map/ppermute | solution.py:45
  23.0 13.1 %collective-permute-start = (bf16[128,1024]{1,0:T(8,128)(2,1)}, bf16[128,1024]{1,0:T(8,128)(2,1)S(1)}, u32[]{:S(2)}, u32[]{:S(2)}) collective-permute-start(bf16[128,1024]{1,0:T(8,128)(2,1)} %param.19), channel_id=1, source_target_pairs={{0,0},{1,1},{2,2},{3,3},{4,8},{5,9},{6,10},{7,11},{8,4},{9,5},{10,... | collective-permute-start | bytes 786440 | tf_op jit(solution)/shard_map/ppermute | solution.py:45
  31.3 23.9 %all-to-all-start = ((bf16[16,64,512]{2,1,0:T(8,128)(2,1)}), bf16[16,64,512]{2,1,0:T(8,128)(2,1)S(1)}, u32[]{:S(2)}, u32[]{:S(2)}) async-start(bf16[16,64,512]{2,1,0:T(8,128)(2,1)} %broadcast_in_dim.10), calls=%async_computation | async-start | bytes 2097152 | tf_op jit(solution)/shard_map/all_to_all | solution.py:331
  39.0 19.4 %collective-permute-start.1 = (bf16[128,1024]{1,0:T(8,128)(2,1)S(1)}, bf16[128,1024]{1,0:T(8,128)(2,1)S(1)}, u32[]{:S(2)}, u32[]{:S(2)}) collective-permute-start(bf16[128,1024]{1,0:T(8,128)(2,1)S(1)} %collective-permute-done.mine.refs_0_), channel_id=1, source_target_pairs={{0,8},{8,0},{1,9},{9,1},{2,10},{10,2},{3,11},{11,3},{4,12},{12,4},... | collective-permute-start | bytes 786440 | tf_op jit(solution)/shard_map/ppermute | solution.py:35
  43.7 15.2 %collective-permute-start.3 = (bf16[128,1024]{1,0:T(8,128)(2,1)S(1)}, bf16[128,1024]{1,0:T(8,128)(2,1)S(1)}, u32[]{:S(2)}, u32[]{:S(2)}) collective-permute-start(bf16[128,1024]{1,0:T(8,128)(2,1)S(1)} %collective-permute-done.2.mine.refs_2_), channel_id=1, source_target_pairs={{0,8},{8,0},{1,9},{9,1},{2,10},{10,2},{3,11},{11,3},{4,12},{12,4},... | collective-permute-start | bytes 786440 | tf_op jit(solution)/shard_map/ppermute | solution.py:35
  45.0 14.4 %collective-permute-start.5 = (bf16[128,1024]{1,0:T(8,128)(2,1)S(1)}, bf16[128,1024]{1,0:T(8,128)(2,1)S(1)}, u32[]{:S(2)}, u32[]{:S(2)}) collective-permute-start(bf16[128,1024]{1,0:T(8,128)(2,1)S(1)} %collective-permute-done.4.mine.refs_4_), channel_id=1, source_target_pairs={{0,8},{8,0},{1,9},{9,1},{2,10},{10,2},{3,11},{11,3},{4,12},{12,4},... | collective-permute-start | bytes 786440 | tf_op jit(solution)/shard_map/ppermute | solution.py:35
  69.2 12.7 %collective-permute-start.13 = (bf16[128,1024]{1,0:T(8,128)(2,1)}, bf16[128,1024]{1,0:T(8,128)(2,1)}, u32[]{:S(2)}, u32[]{:S(2)}) collective-permute-start(bf16[128,1024]{1,0:T(8,128)(2,1)} %get-tuple-element.225), channel_id=1, source_target_pairs={{0,8},{8,0},{1,9},{9,1},{2,10},{10,2},{3,11},{11,3},{4,12},{12,4},... | collective-permute-start | bytes 786440 | tf_op jit(solution)/shard_map/ppermute | solution.py:35
  79.1 33.3 %collective-permute-start.20 = (bf16[1024,1024]{1,0:T(8,128)(2,1)}, bf16[1024,1024]{1,0:T(8,128)(2,1)S(1)}, u32[]{:S(2)}, u32[]{:S(2)}) collective-permute-start(bf16[1024,1024]{1,0:T(8,128)(2,1)} %all-gather.4.cloned.1.call-done), channel_id=1, source_target_pairs={{0,0},{1,1},{2,2},{3,3},{4,8},{5,9},{6,10},{7,11},{8,4},{9,5},{10,... | collective-permute-start | bytes 6291464 | tf_op jit(solution)/shard_map/ppermute | solution.py:45
  98.3 20.5 %collective-permute-start.31 = (bf16[128,1024]{1,0:T(8,128)(2,1)S(1)}, bf16[128,1024]{1,0:T(8,128)(2,1)S(1)}, u32[]{:S(2)}, u32[]{:S(2)}) collective-permute-start(bf16[128,1024]{1,0:T(8,128)(2,1)S(1)} %fusion.7.mine.refs_0_), channel_id=1, source_target_pairs={{0,8},{8,0},{1,9},{9,1},{2,10},{10,2},{3,11},{11,3},{4,12},{12,4},... | collective-permute-start | bytes 786440 | tf_op jit(solution)/shard_map/ppermute | solution.py:35
  122.5 13.6 %collective-permute-start.26 = (bf16[128,1024]{1,0:T(8,128)(2,1)}, bf16[128,1024]{1,0:T(8,128)(2,1)}, u32[]{:S(2)}, u32[]{:S(2)}) collective-permute-start(bf16[128,1024]{1,0:T(8,128)(2,1)} %add_convert_fusion.21), channel_id=1, source_target_pairs={{0,3},{1,0},{2,1},{3,2},{4,7},{5,4},{6,5},{7,6},{8,11},{9,8},{10,9... | collective-permute-start | bytes 786440 | tf_op jit(solution)/shard_map/ppermute | solution.py:31
  123.3 12.8 %collective-permute-start.30 = (bf16[128,1024]{1,0:T(8,128)(2,1)}, bf16[128,1024]{1,0:T(8,128)(2,1)}, u32[]{:S(2)}, u32[]{:S(2)}) collective-permute-start(bf16[128,1024]{1,0:T(8,128)(2,1)} %add_convert_fusion.20), channel_id=1, source_target_pairs={{0,1},{1,2},{2,3},{3,0},{4,5},{5,6},{6,7},{7,4},{8,9},{9,10},{10,1... | collective-permute-start | bytes 786440 | tf_op jit(solution)/shard_map/ppermute | solution.py:31
  126.0 22.9 %collective-permute-start.35 = (bf16[1024,512]{1,0:T(8,128)(2,1)}, bf16[1024,512]{1,0:T(8,128)(2,1)S(1)}, u32[]{:S(2)}, u32[]{:S(2)}) collective-permute-start(bf16[1024,512]{1,0:T(8,128)(2,1)} %all-gather.6.cloned.1.call-done), channel_id=1, source_target_pairs={{0,0},{1,1},{2,2},{3,3},{4,8},{5,9},{6,10},{7,11},{8,4},{9,5},{10,... | collective-permute-start | bytes 3145736 | tf_op jit(solution)/shard_map/ppermute | solution.py:45
  138.5 13.9 %collective-permute-start.39 = (bf16[128,1024]{1,0:T(8,128)(2,1)S(1)}, bf16[128,1024]{1,0:T(8,128)(2,1)}, u32[]{:S(2)}, u32[]{:S(2)}) collective-permute-start(bf16[128,1024]{1,0:T(8,128)(2,1)S(1)} %fusion.8.mine.refs_24_), channel_id=1, source_target_pairs={{0,3},{1,0},{2,1},{3,2},{4,7},{5,4},{6,5},{7,6},{8,11},{9,8},{10,9... | collective-permute-start | bytes 786440 | tf_op jit(solution)/shard_map/ppermute | solution.py:31
  140.0 13.0 %collective-permute-start.33 = (bf16[128,1024]{1,0:T(8,128)(2,1)S(1)}, bf16[128,1024]{1,0:T(8,128)(2,1)}, u32[]{:S(2)}, u32[]{:S(2)}) collective-permute-start(bf16[128,1024]{1,0:T(8,128)(2,1)S(1)} %fusion.8.mine.refs_24_), channel_id=1, source_target_pairs={{0,2},{1,3},{2,0},{3,1},{4,6},{5,7},{6,4},{7,5},{8,10},{9,11},{10,... | collective-permute-start | bytes 786440 | tf_op jit(solution)/shard_map/ppermute | solution.py:31
  141.3 13.0 %collective-permute-start.36 = (bf16[128,1024]{1,0:T(8,128)(2,1)S(1)}, bf16[128,1024]{1,0:T(8,128)(2,1)}, u32[]{:S(2)}, u32[]{:S(2)}) collective-permute-start(bf16[128,1024]{1,0:T(8,128)(2,1)S(1)} %fusion.8.mine.refs_24_), channel_id=1, source_target_pairs={{0,8},{8,0},{1,9},{9,1},{2,10},{10,2},{3,11},{11,3},{4,12},{12,4},... | collective-permute-start | bytes 786440 | tf_op jit(solution)/shard_map/ppermute | solution.py:35
  150.0 58.9 %collective-permute-start.50 = (bf16[1024,1024]{1,0:T(8,128)(2,1)}, bf16[1024,1024]{1,0:T(8,128)(2,1)S(1)}, u32[]{:S(2)}, u32[]{:S(2)}) collective-permute-start(bf16[1024,1024]{1,0:T(8,128)(2,1)} %all-gather.8.cloned.1.call-done), channel_id=1, source_target_pairs={{0,0},{1,1},{2,2},{3,3},{4,8},{5,9},{6,10},{7,11},{8,4},{9,5},{10,... | collective-permute-start | bytes 6291464 | tf_op jit(solution)/shard_map/ppermute | solution.py:45
  194.8 12.7 %collective-permute-start.53 = (bf16[128,1024]{1,0:T(8,128)(2,1)S(1)}, bf16[128,1024]{1,0:T(8,128)(2,1)S(1)}, u32[]{:S(2)}, u32[]{:S(2)}) collective-permute-start(bf16[128,1024]{1,0:T(8,128)(2,1)S(1)} %fusion.9.mine.refs_0_), channel_id=1, source_target_pairs={{0,1},{1,2},{2,3},{3,0},{4,5},{5,6},{6,7},{7,4},{8,9},{9,10},{10,1... | collective-permute-start | bytes 786440 | tf_op jit(solution)/shard_map/ppermute | solution.py:31
  197.2 13.6 %collective-permute-start.61 = (bf16[128,1024]{1,0:T(8,128)(2,1)S(1)}, bf16[128,1024]{1,0:T(8,128)(2,1)S(1)}, u32[]{:S(2)}, u32[]{:S(2)}) collective-permute-start(bf16[128,1024]{1,0:T(8,128)(2,1)S(1)} %fusion.9.mine.refs_0_), channel_id=1, source_target_pairs={{0,8},{8,0},{1,9},{9,1},{2,10},{10,2},{3,11},{11,3},{4,12},{12,4},... | collective-permute-start | bytes 786440 | tf_op jit(solution)/shard_map/ppermute | solution.py:35
  212.5 13.1 %collective-permute-start.62 = (bf16[128,1024]{1,0:T(8,128)(2,1)S(1)}, bf16[128,1024]{1,0:T(8,128)(2,1)S(1)}, u32[]{:S(2)}, u32[]{:S(2)}) collective-permute-start(bf16[128,1024]{1,0:T(8,128)(2,1)S(1)} %get-tuple-element.267), channel_id=1, source_target_pairs={{0,8},{8,0},{1,9},{9,1},{2,10},{10,2},{3,11},{11,3},{4,12},{12,4},... | collective-permute-start | bytes 786440 | tf_op jit(solution)/shard_map/ppermute | solution.py:35
  217.8 12.9 %collective-permute-start.56 = (bf16[128,1024]{1,0:T(8,128)(2,1)S(1)}, bf16[128,1024]{1,0:T(8,128)(2,1)S(1)}, u32[]{:S(2)}, u32[]{:S(2)}) collective-permute-start(bf16[128,1024]{1,0:T(8,128)(2,1)S(1)} %add_convert_fusion.15), channel_id=1, source_target_pairs={{0,3},{1,0},{2,1},{3,2},{4,7},{5,4},{6,5},{7,6},{8,11},{9,8},{10,9... | collective-permute-start | bytes 786440 | tf_op jit(solution)/shard_map/ppermute | solution.py:31
  250.2 15.8 %collective-permute-start.113 = (bf16[128,1024]{1,0:T(8,128)(2,1)}, bf16[128,1024]{1,0:T(8,128)(2,1)}, u32[]{:S(2)}, u32[]{:S(2)}) collective-permute-start(bf16[128,1024]{1,0:T(8,128)(2,1)} %get-tuple-element.460), channel_id=1, source_target_pairs={{0,0},{1,1},{2,2},{3,3},{4,8},{5,9},{6,10},{7,11},{8,4},{9,5},{10,... | collective-permute-start | bytes 786440 | tf_op jit(solution)/shard_map/ppermute | solution.py:45
  284.9 13.1 %collective-permute-start.84 = (bf16[144,1024]{1,0:T(8,128)(2,1)S(1)}, bf16[144,1024]{1,0:T(8,128)(2,1)S(1)}, u32[]{:S(2)}, u32[]{:S(2)}) collective-permute-start(bf16[144,1024]{1,0:T(8,128)(2,1)S(1)} %maximum_maximum_fusion.mine.refs_36_), channel_id=1, source_target_pairs={{0,8},{8,0},{1,9},{9,1},{2,10},{10,2},{3,11},{11,3},{4,12},{12,4},... | collective-permute-start | bytes 884744 | tf_op jit(solution)/shard_map/ppermute | solution.py:35
  289.4 17.1 %collective-permute-start.81 = (bf16[144,1024]{1,0:T(8,128)(2,1)}, bf16[144,1024]{1,0:T(8,128)(2,1)S(1)}, u32[]{:S(2)}, u32[]{:S(2)}) collective-permute-start(bf16[144,1024]{1,0:T(8,128)(2,1)} %collective-permute-done.80.mine.refs_40_), channel_id=1, source_target_pairs={{0,8},{8,0},{1,9},{9,1},{2,10},{10,2},{3,11},{11,3},{4,12},{12,4},... | collective-permute-start | bytes 884744 | tf_op jit(solution)/shard_map/ppermute | solution.py:35
  296.3 13.8 %collective-permute-start.79 = (bf16[144,1024]{1,0:T(8,128)(2,1)S(1)}, bf16[144,1024]{1,0:T(8,128)(2,1)S(1)}, u32[]{:S(2)}, u32[]{:S(2)}) collective-permute-start(bf16[144,1024]{1,0:T(8,128)(2,1)S(1)} %collective-permute-done.78.mine.refs_42_), channel_id=1, source_target_pairs={{0,8},{8,0},{1,9},{9,1},{2,10},{10,2},{3,11},{11,3},{4,12},{12,4},... | collective-permute-start | bytes 884744 | tf_op jit(solution)/shard_map/ppermute | solution.py:35
  315.8 14.7 %collective-permute-start.87 = (bf16[128,1024]{1,0:T(8,128)(2,1)S(1)}, bf16[128,1024]{1,0:T(8,128)(2,1)}, u32[]{:S(2)}, u32[]{:S(2)}) collective-permute-start(bf16[128,1024]{1,0:T(8,128)(2,1)S(1)} %get-tuple-element.297), channel_id=1, source_target_pairs={{0,8},{8,0},{1,9},{9,1},{2,10},{10,2},{3,11},{11,3},{4,12},{12,4},... | collective-permute-start | bytes 786440 | tf_op jit(solution)/shard_map/ppermute | solution.py:35
  315.8 18.7 %collective-permute-start.89 = (bf16[128,1024]{1,0:T(8,128)(2,1)S(1)}, bf16[128,1024]{1,0:T(8,128)(2,1)}, u32[]{:S(2)}, u32[]{:S(2)}) collective-permute-start(bf16[128,1024]{1,0:T(8,128)(2,1)S(1)} %get-tuple-element.300), channel_id=1, source_target_pairs={{0,8},{8,0},{1,9},{9,1},{2,10},{10,2},{3,11},{11,3},{4,12},{12,4},... | collective-permute-start | bytes 786440 | tf_op jit(solution)/shard_map/ppermute | solution.py:35
  316.3 21.0 %collective-permute-start.91 = (bf16[128,1024]{1,0:T(8,128)(2,1)S(1)}, bf16[128,1024]{1,0:T(8,128)(2,1)}, u32[]{:S(2)}, u32[]{:S(2)}) collective-permute-start(bf16[128,1024]{1,0:T(8,128)(2,1)S(1)} %get-tuple-element.303), channel_id=1, source_target_pairs={{0,8},{8,0},{1,9},{9,1},{2,10},{10,2},{3,11},{11,3},{4,12},{12,4},... | collective-permute-start | bytes 786440 | tf_op jit(solution)/shard_map/ppermute | solution.py:35
  350.0 13.0 %collective-permute-start.96 = (bf16[128,1024]{1,0:T(8,128)(2,1)S(1)}, bf16[128,1024]{1,0:T(8,128)(2,1)S(1)}, u32[]{:S(2)}, u32[]{:S(2)}) collective-permute-start(bf16[128,1024]{1,0:T(8,128)(2,1)S(1)} %get-tuple-element.434.mine.refs_12_), channel_id=1, source_target_pairs={{0,1},{1,2},{2,3},{3,0},{4,5},{5,6},{6,7},{7,4},{8,9},{9,10},{10,1... | collective-permute-start | bytes 786440 | tf_op jit(solution)/shard_map/ppermute | solution.py:31
  367.9 12.7 %collective-permute-start.105 = (bf16[128,1024]{1,0:T(8,128)(2,1)}, bf16[128,1024]{1,0:T(8,128)(2,1)}, u32[]{:S(2)}, u32[]{:S(2)}) collective-permute-start(bf16[128,1024]{1,0:T(8,128)(2,1)} %get-tuple-element.332), channel_id=1, source_target_pairs={{0,8},{8,0},{1,9},{9,1},{2,10},{10,2},{3,11},{11,3},{4,12},{12,4},... | collective-permute-start | bytes 786440 | tf_op jit(solution)/shard_map/ppermute | solution.py:35
  371.6 14.2 %collective-permute-start.99 = (bf16[128,1024]{1,0:T(8,128)(2,1)S(1)}, bf16[128,1024]{1,0:T(8,128)(2,1)}, u32[]{:S(2)}, u32[]{:S(2)}) collective-permute-start(bf16[128,1024]{1,0:T(8,128)(2,1)S(1)} %add_convert_fusion.6), channel_id=1, source_target_pairs={{0,3},{1,0},{2,1},{3,2},{4,7},{5,4},{6,5},{7,6},{8,11},{9,8},{10,9... | collective-permute-start | bytes 786440 | tf_op jit(solution)/shard_map/ppermute | solution.py:31
  374.4 51.3 %all-to-all-start.1 = ((bf16[16,64,1536]{2,1,0:T(8,128)(2,1)}), bf16[16,64,1536]{2,1,0:T(8,128)(2,1)}, u32[]{:S(2)}, u32[]{:S(2)}) async-start(bf16[16,64,1536]{2,1,0:T(8,128)(2,1)} %shard_map.350), calls=%async_computation.1 | async-start | bytes 6291456 | tf_op jit(solution)/shard_map/all_to_all | solution.py:407
  391.1 15.4 %collective-permute-start.106 = (bf16[144,1024]{1,0:T(8,128)(2,1)S(1)}, bf16[144,1024]{1,0:T(8,128)(2,1)S(1)}, u32[]{:S(2)}, u32[]{:S(2)}) collective-permute-start(bf16[144,1024]{1,0:T(8,128)(2,1)S(1)} %maximum_maximum_fusion.1.mine.refs_12_), channel_id=1, source_target_pairs={{0,8},{8,0},{1,9},{9,1},{2,10},{10,2},{3,11},{11,3},{4,12},{12,4},... | collective-permute-start | bytes 884744 | tf_op jit(solution)/shard_map/ppermute | solution.py:35
  391.9 14.3 %collective-permute-start.109 = (bf16[144,1024]{1,0:T(8,128)(2,1)S(1)}, bf16[144,1024]{1,0:T(8,128)(2,1)S(1)}, u32[]{:S(2)}, u32[]{:S(2)}) collective-permute-start(bf16[144,1024]{1,0:T(8,128)(2,1)S(1)} %maximum_maximum_fusion.1.mine.refs_12_), channel_id=1, source_target_pairs={{0,1},{1,2},{2,3},{3,0},{4,5},{5,6},{6,7},{7,4},{8,9},{9,10},{10,1... | collective-permute-start | bytes 884744 | tf_op jit(solution)/shard_map/ppermute | solution.py:31
  428.8 52.9 %all-to-all-start.2 = ((bf16[16,80,1024]{2,1,0:T(8,128)(2,1)}), bf16[16,80,1024]{2,1,0:T(8,128)(2,1)}, u32[]{:S(2)}, u32[]{:S(2)}) async-start(bf16[16,80,1024]{2,1,0:T(8,128)(2,1)} %shard_map.356), calls=%async_computation.2 | async-start | bytes 5242880 | tf_op jit(solution)/shard_map/all_to_all | solution.py:407
  447.7 15.0 %collective-permute-start.117 = (bf16[128,1024]{1,0:T(8,128)(2,1)S(1)}, bf16[128,1024]{1,0:T(8,128)(2,1)}, u32[]{:S(2)}, u32[]{:S(2)}) collective-permute-start(bf16[128,1024]{1,0:T(8,128)(2,1)S(1)} %get-tuple-element.390), channel_id=1, source_target_pairs={{0,8},{8,0},{1,9},{9,1},{2,10},{10,2},{3,11},{11,3},{4,12},{12,4},... | collective-permute-start | bytes 786440 | tf_op jit(solution)/shard_map/ppermute | solution.py:35
  456.7 20.9 %collective-permute-start.115 = (bf16[64,1536]{1,0:T(8,128)(2,1)}, bf16[64,1536]{1,0:T(8,128)(2,1)S(1)}, u32[]{:S(2)}, u32[]{:S(2)}) collective-permute-start(bf16[64,1536]{1,0:T(8,128)(2,1)} %convert_reduce_fusion), channel_id=1, source_target_pairs={{0,0},{1,1},{2,2},{3,3},{4,8},{5,9},{6,10},{7,11},{8,4},{9,5},{10,... | collective-permute-start | bytes 589832 | tf_op jit(solution)/shard_map/ppermute | solution.py:45
  462.2 15.4 %collective-permute-start.123 = (bf16[128,1024]{1,0:T(8,128)(2,1)S(1)}, bf16[128,1024]{1,0:T(8,128)(2,1)S(1)}, u32[]{:S(2)}, u32[]{:S(2)}) collective-permute-start(bf16[128,1024]{1,0:T(8,128)(2,1)S(1)} %get-tuple-element.396), channel_id=1, source_target_pairs={{0,8},{8,0},{1,9},{9,1},{2,10},{10,2},{3,11},{11,3},{4,12},{12,4},... | collective-permute-start | bytes 786440 | tf_op jit(solution)/shard_map/ppermute | solution.py:35
  463.7 13.9 %collective-permute-start.118 = (bf16[128,1024]{1,0:T(8,128)(2,1)S(1)}, bf16[128,1024]{1,0:T(8,128)(2,1)S(1)}, u32[]{:S(2)}, u32[]{:S(2)}) collective-permute-start(bf16[128,1024]{1,0:T(8,128)(2,1)S(1)} %add_convert_fusion.3), channel_id=1, source_target_pairs={{0,2},{1,3},{2,0},{3,1},{4,6},{5,7},{6,4},{7,5},{8,10},{9,11},{10,... | collective-permute-start | bytes 786440 | tf_op jit(solution)/shard_map/ppermute | solution.py:31
  466.1 13.3 %collective-permute-start.120 = (bf16[128,1024]{1,0:T(8,128)(2,1)S(1)}, bf16[128,1024]{1,0:T(8,128)(2,1)S(1)}, u32[]{:S(2)}, u32[]{:S(2)}) collective-permute-start(bf16[128,1024]{1,0:T(8,128)(2,1)S(1)} %add_convert_fusion.2), channel_id=1, source_target_pairs={{0,3},{1,0},{2,1},{3,2},{4,7},{5,4},{6,5},{7,6},{8,11},{9,8},{10,9... | collective-permute-start | bytes 786440 | tf_op jit(solution)/shard_map/ppermute | solution.py:31
  466.4 13.0 %collective-permute-start.122 = (bf16[128,1024]{1,0:T(8,128)(2,1)S(1)}, bf16[128,1024]{1,0:T(8,128)(2,1)S(1)}, u32[]{:S(2)}, u32[]{:S(2)}) collective-permute-start(bf16[128,1024]{1,0:T(8,128)(2,1)S(1)} %add_convert_fusion.1), channel_id=1, source_target_pairs={{0,1},{1,2},{2,3},{3,0},{4,5},{5,6},{6,7},{7,4},{8,9},{9,10},{10,1... | collective-permute-start | bytes 786440 | tf_op jit(solution)/shard_map/ppermute | solution.py:31
  479.7 39.3 %collective-permute-start.124 = (bf16[128,1024]{1,0:T(8,128)(2,1)S(1)}, bf16[128,1024]{1,0:T(8,128)(2,1)S(1)}, u32[]{:S(2)}, u32[]{:S(2)}) collective-permute-start(bf16[128,1024]{1,0:T(8,128)(2,1)S(1)} %add_convert_fusion), channel_id=1, source_target_pairs={{0,0},{1,1},{2,2},{3,3},{4,8},{5,9},{6,10},{7,11},{8,4},{9,5},{10,... | collective-permute-start | bytes 786440 | tf_op jit(solution)/shard_map/ppermute | solution.py:45
  484.0 31.3 %all-to-all-start.3 = ((bf16[16,80,512]{2,1,0:T(8,128)(2,1)}), bf16[16,80,512]{2,1,0:T(8,128)(2,1)S(1)}, u32[]{:S(2)}, u32[]{:S(2)}) async-start(bf16[16,80,512]{2,1,0:T(8,128)(2,1)} %shard_map.364), calls=%async_computation.3 | async-start | bytes 2621440 | tf_op jit(solution)/shard_map/all_to_all | solution.py:486
  491.1 24.2 %collective-permute-start.116 = (f32[2,512]{1,0:T(2,128)S(1)}, f32[2,512]{1,0:T(2,128)S(1)}, u32[]{:S(2)}, u32[]{:S(2)}) collective-permute-start(f32[2,512]{1,0:T(2,128)S(1)} %pad_maximum_fusion.6), channel_id=1, source_target_pairs={{0,0},{1,1},{2,2},{3,3},{4,8},{5,9},{6,10},{7,11},{8,4},{9,5},{10,... | collective-permute-start | bytes 12296 | tf_op jit(solution)/shard_map/ppermute | solution.py:45
  497.6 16.2 %collective-permute-start.114 = (bf16[64,1024]{1,0:T(8,128)(2,1)S(1)}, bf16[64,1024]{1,0:T(8,128)(2,1)S(1)}, u32[]{:S(2)}, u32[]{:S(2)}) collective-permute-start(bf16[64,1024]{1,0:T(8,128)(2,1)S(1)} %slice.576), channel_id=1, source_target_pairs={{0,0},{1,1},{2,2},{3,3},{4,8},{5,9},{6,10},{7,11},{8,4},{9,5},{10,... | collective-permute-start | bytes 393224 | tf_op jit(solution)/shard_map/ppermute | solution.py:45
  (295 other events, 2723.7 us)
Sparse Core Ops, SparseCore 0:
  9.8 41.3 all-gather.3
  53.5 38.8 all-gather.5
  94.1 34.1 all-gather.7
